TPU v7x, 128 devices: a whole 4x4x4 slice. The times are simulated.
128 devices in a mesh: pts: 16 (over y_hi, x, core), coef: 8 (over z, y_lo).
Axes of the slice: x: 4, y: 4 (y_hi: 2, y_lo: 2; y = y_hi * 2 + y_lo), z: 4, core: 2. Of those that a mesh axis runs over, the one named last changes fastest.
Arguments:
- colatitude: float32 [4096], P('pts'), may hold values from 0.96 to 2.18
- longitude: float32 [1310720], P('pts'), may hold values from -3.140625 to 3.140625
- tile_of_point: int32 [1310720], P('pts'), may hold values from 0 to 4095, as said below
- order_of_slot: int32 [320], P('coef'), may hold values from 0 to 319, each once
- observations: float32 [1310720], P('pts'), may hold values from -6 to 6
- obs_weight: float32 [1310720], P('pts'), may hold values from 0.2 to 5
- prior: float32 [301], replicated, may hold values from 1 to 10
Outputs:
- coefficients: float32 [301, 2, 320], P(None, None, 'coef')
- point_residual: float32 [1310720], P('pts')
Inputs may be any that keep to these rules, and one draw needn't show every extreme that they name: `tile_of_point`: the k-th block of 81920 points lies in tiles k * 256 to (k + 1) * 256 - 1. `order_of_slot`: each number once; slots holding a number above 300 are empty and contribute nothing.
All inputs are finite; a program needn't handle non-finite values.
Results may differ from a plain program's by a relative error of at most 0.0003.
Values sent between devices are 32-bit elements; how exact they have to be, the bound alone decides.
No kernel may reach another device: no remote copies, remote signals or barrier semaphores. Data moves between devices by JAX's collectives and lax.ppermute only.
A program may use at most 64 MiB of HBM per device.

v0:
```python
import jax
import jax.numpy as jnp
from jax import lax
from jax.sharding import PartitionSpec as P

DEGREES = 301
DEG_STEP = 43
ITERS = 2


highest = lax.Precision.HIGHEST
point_parts = 8


def degree_factors(degree, orders):
    plus_sum = degree + orders
    minus_sum = degree - orders
    upward = jnp.sqrt(
        jnp.maximum((2.0 * degree - 1.0) * (2.0 * degree + 1.0), 0.0)
        / jnp.maximum(minus_sum * plus_sum, 1.0)
    )
    backward = jnp.sqrt(
        (2.0 * degree + 1.0)
        * jnp.maximum(plus_sum - 1.0, 0.0)
        * jnp.maximum(minus_sum - 1.0, 0.0)
        / jnp.maximum((2.0 * degree - 3.0) * minus_sum * plus_sum, 1.0)
    )
    return (upward, backward)


def next_row(degree, orders, cosine, sectoral, recent, earlier):
    upward, backward = degree_factors(degree, orders)
    grown = upward * cosine * recent - backward * earlier
    return jnp.where(degree < orders, 0.0, jnp.where(degree == orders, sectoral, grown))


def sectoral_values(orders, sines):
    single = (orders == 0.0).astype(jnp.float32)
    log_lead = 0.5 * (
        jnp.log(2.0 - single)
        + lax.lgamma(orders + 1.5)
        - lax.lgamma(orders * 0.0 + 1.5)
        - lax.lgamma(orders + 1.0)
    )
    return jnp.exp(log_lead + orders * jnp.log(sines))


def legendre_fold(coeff, orders, cosine, sectoral):
    empty = jnp.zeros(sectoral.shape, jnp.float32)

    def advance(block_index, carried):
        recent, earlier, running = carried
        coeff_rows = lax.dynamic_slice_in_dim(coeff, block_index * DEG_STEP, DEG_STEP, 0)
        for offset in range(DEG_STEP):
            degree = (block_index * DEG_STEP + offset).astype(jnp.float32)
            legendre = next_row(degree, orders, cosine, sectoral, recent, earlier)
            running = running + legendre[None] * coeff_rows[offset][:, :, None]
            earlier = recent
            recent = legendre
        return (recent, earlier, running)

    initial = (empty, empty, jnp.zeros((2,) + sectoral.shape, jnp.float32))
    return lax.fori_loop(0, DEGREES // DEG_STEP, advance, initial)[2]


def legendre_unfold(folded, orders, cosine, sectoral):
    empty = jnp.zeros(sectoral.shape, jnp.float32)

    def advance(block_index, carried):
        recent, earlier, gradient = carried
        collected = []
        for offset in range(DEG_STEP):
            degree = (block_index * DEG_STEP + offset).astype(jnp.float32)
            legendre = next_row(degree, orders, cosine, sectoral, recent, earlier)
            collected.append(jnp.sum(legendre[None] * folded, axis=2))
            earlier = recent
            recent = legendre
        gradient = lax.dynamic_update_slice_in_dim(
            gradient, jnp.stack(collected), block_index * DEG_STEP, 0
        )
        return (recent, earlier, gradient)

    initial = (empty, empty, jnp.zeros((DEGREES,) + folded.shape[:2], jnp.float32))
    return lax.fori_loop(0, DEGREES // DEG_STEP, advance, initial)[2]


def point_synthesis(fourier, orders_flat, longitude, local_tile):
    slot_count = fourier.shape[1]
    tile_count = fourier.shape[2]
    lookup = fourier.reshape(2 * slot_count, tile_count)
    breadth = longitude.shape[0] // point_parts

    def one_part(packed):
        angles, tile_ids = packed
        one_hot = (
            tile_ids[None, :] == lax.broadcasted_iota(jnp.int32, (tile_count, breadth), 0)
        ).astype(jnp.float32)
        picked = jnp.dot(lookup, one_hot, precision=highest, preferred_element_type=jnp.float32)
        phases = orders_flat[:, None] * angles[None, :]
        return jnp.sum(
            jnp.cos(phases) * picked[:slot_count] + jnp.sin(phases) * picked[slot_count:], axis=0
        )

    blocks = (longitude.reshape(point_parts, breadth), local_tile.reshape(point_parts, breadth))
    return lax.map(one_part, blocks).reshape(-1)


def point_analysis(point_field, orders_flat, longitude, local_tile, tile_count):
    slot_count = orders_flat.shape[0]
    breadth = longitude.shape[0] // point_parts

    def one_part(running, packed):
        angles, tile_ids, field_block = packed
        one_hot = (
            tile_ids[None, :] == lax.broadcasted_iota(jnp.int32, (tile_count, breadth), 0)
        ).astype(jnp.float32)
        phases = orders_flat[:, None] * angles[None, :]
        stacked = jnp.concatenate(
            [jnp.cos(phases) * field_block[None, :], jnp.sin(phases) * field_block[None, :]], 0
        )
        summed = lax.dot_general(
            stacked,
            one_hot,
            (((1,), (1,)), ((), ())),
            precision=highest,
            preferred_element_type=jnp.float32,
        )
        return (running + summed, None)

    initial = jnp.zeros((2 * slot_count, tile_count), jnp.float32)
    blocks = (
        longitude.reshape(point_parts, breadth),
        local_tile.reshape(point_parts, breadth),
        point_field.reshape(point_parts, breadth),
    )
    folded = lax.scan(one_part, initial, blocks)[0]
    return folded.reshape(2, slot_count, tile_count)


def shards(colatitude, longitude, tile_of_point, order_of_slot, observations, obs_weight, prior):
    tile_count = colatitude.shape[0]
    slot_count = order_of_slot.shape[0]
    orders_flat = order_of_slot.astype(jnp.float32)
    orders = orders_flat[:, None]
    cosine = jnp.cos(colatitude)[None, :]
    sectoral = sectoral_values(orders, jnp.sin(colatitude)[None, :])
    local_tile = tile_of_point - lax.axis_index("pts") * tile_count
    inverse_degree = 1.0 / DEGREES
    coeff_shape = (DEGREES, 2, slot_count)
    spread = jnp.broadcast_to(prior[:, None, None], coeff_shape)

    def synthesize(vector):
        fourier = legendre_fold(vector, orders, cosine, sectoral)
        partial_value = (
            point_synthesis(fourier, orders_flat, longitude, local_tile) * inverse_degree
        )
        return lax.psum(partial_value, "coef")

    def project(point_field):
        folded = point_analysis(
            obs_weight * point_field, orders_flat, longitude, local_tile, tile_count
        )
        return legendre_unfold(folded, orders, cosine, sectoral) * inverse_degree

    share_len = DEGREES * 2 * slot_count // lax.axis_size("pts")
    prior_part = lax.dynamic_slice_in_dim(
        spread.reshape(-1), lax.axis_index("pts") * share_len, share_len, 0
    )

    def to_full(vector):
        return lax.all_gather(vector, "pts", axis=0, tiled=True).reshape(coeff_shape)

    def reduce_terms(terms):
        return lax.psum_scatter(terms.reshape(-1), "pts", scatter_dimension=0, tiled=True)

    def global_total(sums):
        return lax.psum(sums, ("pts", "coef"))

    rhs = reduce_terms(project(observations))
    solution = jnp.zeros_like(rhs)
    residual = rhs
    direction = rhs
    norm_now = global_total(jnp.sum(residual * residual))
    for iteration in range(ITERS):
        applied = reduce_terms(project(synthesize(to_full(direction)))) + prior_part * direction
        step_size = norm_now / global_total(jnp.sum(direction * applied))
        solution = solution + step_size * direction
        residual = residual - step_size * applied
        if iteration + 1 < ITERS:
            norm_next = global_total(jnp.sum(residual * residual))
            direction = residual + norm_next / norm_now * direction
            norm_now = norm_next
    solution_full = to_full(solution)
    return (solution_full, observations - synthesize(solution_full))


def solution(mesh):
    placed = (P("pts"), P("pts"), P("pts"), P("coef"), P("pts"), P("pts"), P())
    return jax.shard_map(
        shards,
        mesh=mesh,
        in_specs=placed,
        out_specs=(P(None, None, "coef"), P("pts")),
        check_vma=False,
    )
```

profile of v0, /device:TPU:0, one launch (start us, length us, event | category | flops | bytes accessed | tf_op | source)
XLA Modules:
  0.0 2083.3 jit_solution(17269975323501718443)
XLA Ops:
  13.1 109.2 %while.192 = (s32[]{:T(128)}, f32[80,256]{1,0:T(8,128)S(1)}, f32[40]{0:T(128)S(1)}, f32[8,10240]{1,0:T(8,128)}, f32[8,10240]{1,0:T(8,128)}, /*index=5*/s32[8,10240]{1,0:T(8,128)}, s32[]{:T(128)}, s32[]{:T(128)}) while((s32[]{:T(128)}, f32[80,256]{1,0:T(8,128)S(1)}, f32[40]{0:T(128)S(1)}, f32[8,10240]{1,0:T(8,128)}, ...), condition=%wide.region_1.2_spmd.clone, body=%wide.region_0.1_spmd.clone.sunk | while | flops 2521292800 | bytes 7086343 | solution.py:136
  122.5 31.2 %while.193 = (s32[]{:T(128)}, f32[40,256]{1,0:T(8,128)S(1)}, f32[40,256]{1,0:T(8,128)S(1)}, f32[301,2,40]{2,1,0:T(2,128)S(1)}, f32[40,1]{0,1:T(1,128)S(1)}, /*in...) while((s32[]{:T(128)}, f32[40,256]{1,0:T(8,128)S(1)}, ...), condition=%wide.region_46.47_spmd.clone, body=%wide.region_2.46_spmd.clone.sunk | while | flops 4471030 | bytes 4083833 | solution.py:84
  157.1 132.1 %all-reduce.29.cloned.1.call-done = f32[24080]{0:T(1024)} async-done(((f32[24080]{0:T(1024)}), f32[24080]{0:T(1024)}) %all-reduce.29.cloned.1.call-update) | async-done | bytes 96336
  290.8 133.1 %all-reduce.23.cloned.1.call-done = f32[24080]{0:T(1024)} async-done(((f32[24080]{0:T(1024)}), f32[24080]{0:T(1024)}) %all-reduce.23.cloned.1.call-update) | async-done | bytes 96336
  425.4 28.4 %while.194 = (s32[]{:T(128)}, f32[40,256]{1,0:T(8,128)S(1)}, f32[40,256]{1,0:T(8,128)S(1)}, f32[2,40,256]{2,1,0:T(8,128)S(1)}, f32[40,1]{0,1:T(1,128)S(1)}, /*in...) while((s32[]{:T(128)}, f32[40,256]{1,0:T(8,128)S(1)}, ...), condition=%wide.region_51.52_spmd.clone, body=%wide.region_50.51_spmd.clone.sunk | while | flops 4494992 | bytes 3855018 | solution.py:63
  453.8 106.4 %while.189 = (s32[]{:T(128)}, f32[8,10240]{1,0:T(8,128)S(1)}, f32[40]{0:T(128)S(1)}, f32[8,10240]{1,0:T(8,128)}, s32[8,10240]{1,0:T(8,128)}, /*index=5*/f32[80,256]{1,0:T(8,128)S(1)}, s32[]{:T(128)}, s32[]{:T(128)}) while((s32[]{:T(128)}, f32[8,10240]{1,0:T(8,128)S(1)}, f32[40]{0:T(128)S(1)}, f32[8,10240]{1,0:T(8,128)}, ...), condition=%wide.region_54.55_spmd, body=%wide.region_52.54_spmd.sunk | while | flops 2521241600 | bytes 7004417 | solution.py:105
  561.2 74.8 %all-reduce.17.cloned.1.call-done = f32[81920]{0:T(1024)} async-done(((f32[81920]{0:T(1024)}), f32[81920]{0:T(1024)}) %all-reduce.17.cloned.1.call-update) | async-done | bytes 327696 | tf_op jit(solution)/shard_map/psum | solution.py:157
  637.8 109.4 %while.195 = (s32[]{:T(128)}, f32[80,256]{1,0:T(8,128)S(1)}, f32[40]{0:T(128)S(1)}, f32[8,10240]{1,0:T(8,128)}, f32[8,10240]{1,0:T(8,128)}, /*index=5*/s32[8,10240]{1,0:T(8,128)}, s32[]{:T(128)}, s32[]{:T(128)}) while((s32[]{:T(128)}, f32[80,256]{1,0:T(8,128)S(1)}, f32[40]{0:T(128)S(1)}, f32[8,10240]{1,0:T(8,128)}, ...), condition=%wide.region_57.58_spmd.clone, body=%wide.region_56.57_spmd.clone.sunk | while | flops 2521292800 | bytes 7086343 | solution.py:136
  747.3 30.8 %while.196 = (s32[]{:T(128)}, f32[40,256]{1,0:T(8,128)S(1)}, f32[40,256]{1,0:T(8,128)S(1)}, f32[301,2,40]{2,1,0:T(2,128)S(1)}, f32[40,1]{0,1:T(1,128)S(1)}, /*in...) while((s32[]{:T(128)}, f32[40,256]{1,0:T(8,128)S(1)}, ...), condition=%wide.region_102.103_spmd.clone, body=%wide.region_58.102_spmd.clone.sunk | while | flops 4471030 | bytes 4083833 | solution.py:84
  780.4 129.9 %all-reduce.31.cloned.1.call-done = f32[24080]{0:T(1024)} async-done(((f32[24080]{0:T(1024)}), f32[24080]{0:T(1024)}) %all-reduce.31.cloned.1.call-update) | async-done | bytes 96336
  911.8 66.5 %all-reduce.6 = (f32[]{:T(128)}, f32[]{:T(128)}) all-reduce(f32[]{:T(128)} %get-tuple-element.3005, f32[]{:T(128)} %get-tuple-element.3004), channel_id=1, replica_groups=mesh['pts'=16,'coef'=8] {'pts','coef'}, use_global_device_ids=true, to_apply=%region_49.50 | all-reduce | flops 2 | bytes 16 | tf_op jit(solution)/shard_map/psum | solution.py:177
  981.1 63.5 %psum.52 = f32[]{:T(128)} all-reduce(f32[]{:T(128)} %multiply_reduce_fusion.129), channel_id=1, replica_groups=mesh['pts'=16,'coef'=8] {'pts','coef'}, use_global_device_ids=true, to_apply=%region_107.108 | all-reduce | flops 1 | bytes 8 | tf_op jit(solution)/shard_map/psum | solution.py:177
  1047.6 128.1 %all-reduce.25.cloned.1.call-done = f32[24080]{0:T(1024)} async-done(((f32[24080]{0:T(1024)}), f32[24080]{0:T(1024)}) %all-reduce.25.cloned.1.call-update) | async-done | bytes 96336
  1177.2 28.9 %while.197 = (s32[]{:T(128)}, f32[40,256]{1,0:T(8,128)S(1)}, f32[40,256]{1,0:T(8,128)S(1)}, f32[2,40,256]{2,1,0:T(8,128)S(1)}, f32[40,1]{0,1:T(1,128)S(1)}, /*in...) while((s32[]{:T(128)}, f32[40,256]{1,0:T(8,128)S(1)}, ...), condition=%wide.region_109.110_spmd.clone, body=%wide.region_108.109_spmd.clone.sunk | while | flops 4494992 | bytes 3855018 | solution.py:63
  1206.1 106.4 %while.190 = (s32[]{:T(128)}, f32[8,10240]{1,0:T(8,128)S(1)}, f32[40]{0:T(128)S(1)}, f32[8,10240]{1,0:T(8,128)}, s32[8,10240]{1,0:T(8,128)}, /*index=5*/f32[80,256]{1,0:T(8,128)S(1)}, s32[]{:T(128)}, s32[]{:T(128)}) while((s32[]{:T(128)}, f32[8,10240]{1,0:T(8,128)S(1)}, f32[40]{0:T(128)S(1)}, f32[8,10240]{1,0:T(8,128)}, ...), condition=%wide.region_112.113_spmd, body=%wide.region_110.112_spmd.sunk | while | flops 2521241600 | bytes 7004417 | solution.py:105
  1313.5 74.8 %all-reduce.19.cloned.1.call-done = f32[81920]{0:T(1024)} async-done(((f32[81920]{0:T(1024)}), f32[81920]{0:T(1024)}) %all-reduce.19.cloned.1.call-update) | async-done | bytes 327696 | tf_op jit(solution)/shard_map/psum | solution.py:157
  1390.1 109.4 %while.198 = (s32[]{:T(128)}, f32[80,256]{1,0:T(8,128)S(1)}, f32[40]{0:T(128)S(1)}, f32[8,10240]{1,0:T(8,128)}, f32[8,10240]{1,0:T(8,128)}, /*index=5*/s32[8,10240]{1,0:T(8,128)}, s32[]{:T(128)}, s32[]{:T(128)}) while((s32[]{:T(128)}, f32[80,256]{1,0:T(8,128)S(1)}, f32[40]{0:T(128)S(1)}, f32[8,10240]{1,0:T(8,128)}, ...), condition=%wide.region_115.116_spmd.clone, body=%wide.region_114.115_spmd.clone.sunk | while | flops 2521292800 | bytes 7086343 | solution.py:136
  1499.6 30.9 %while.199 = (s32[]{:T(128)}, f32[40,256]{1,0:T(8,128)S(1)}, f32[40,256]{1,0:T(8,128)S(1)}, f32[301,2,40]{2,1,0:T(2,128)S(1)}, f32[40,1]{0,1:T(1,128)S(1)}, /*in...) while((s32[]{:T(128)}, f32[40,256]{1,0:T(8,128)S(1)}, ...), condition=%wide.region_160.161_spmd.clone, body=%wide.region_116.160_spmd.clone.sunk | while | flops 4471030 | bytes 4083833 | solution.py:84
  1531.8 130.8 %all-reduce.33.cloned.1.call-done = f32[24080]{0:T(1024)} async-done(((f32[24080]{0:T(1024)}), f32[24080]{0:T(1024)}) %all-reduce.33.cloned.1.call-update) | async-done | bytes 96336
  1664.0 66.4 %psum.54 = f32[]{:T(128)} all-reduce(f32[]{:T(128)} %fusion.3364), channel_id=1, replica_groups=mesh['pts'=16,'coef'=8] {'pts','coef'}, use_global_device_ids=true, to_apply=%region_163.164 | all-reduce | flops 1 | bytes 8 | tf_op jit(solution)/shard_map/psum | solution.py:177
  1733.4 128.8 %all-reduce.27.cloned.1.call-done = f32[24080]{0:T(1024)} async-done(((f32[24080]{0:T(1024)}), f32[24080]{0:T(1024)}) %all-reduce.27.cloned.1.call-update) | async-done | bytes 96336
  1863.6 28.8 %while.200 = (s32[]{:T(128)}, f32[40,256]{1,0:T(8,128)S(1)}, f32[40,256]{1,0:T(8,128)S(1)}, f32[2,40,256]{2,1,0:T(8,128)S(1)}, f32[40,1]{0,1:T(1,128)S(1)}, /*in...) while((s32[]{:T(128)}, f32[40,256]{1,0:T(8,128)S(1)}, ...), condition=%wide.region_165.166_spmd.clone, body=%wide.region_164.165_spmd.clone.sunk | while | flops 4494992 | bytes 3855018 | solution.py:63
  1892.5 106.4 %while.191 = (s32[]{:T(128)}, f32[8,10240]{1,0:T(8,128)S(1)}, f32[40]{0:T(128)S(1)}, f32[8,10240]{1,0:T(8,128)}, s32[8,10240]{1,0:T(8,128)}, /*index=5*/f32[80,256]{1,0:T(8,128)S(1)}, s32[]{:T(128)}, s32[]{:T(128)}) while((s32[]{:T(128)}, f32[8,10240]{1,0:T(8,128)S(1)}, f32[40]{0:T(128)S(1)}, f32[8,10240]{1,0:T(8,128)}, ...), condition=%wide.region_168.169_spmd, body=%wide.region_166.168_spmd.sunk | while | flops 2521241600 | bytes 7004417 | solution.py:105
  2000.6 74.1 %all-reduce.21.cloned.1.call-done = f32[81920]{0:T(1024)} async-done(((f32[81920]{0:T(1024)}), f32[81920]{0:T(1024)}) %all-reduce.21.cloned.1.call-update) | async-done | bytes 327696 | tf_op jit(solution)/shard_map/psum | solution.py:157
  (2024 shorter events, 829.6 us)
Async XLA Ops:
  7.2 5.1 copy-start.3
  7.2 5.1 copy-start
  7.2 282.0 %all-reduce.29.cloned.1.call-start = ((), (), s32[]{:S(2)}) async-start(), calls=%async_computation.6 | async-start | bytes 196608
  13.1 109.2 %copy-start.11 = (f32[256]{0:T(256)S(1)}, f32[256]{0:T(256)}, u32[]{:S(2)}) copy-start(f32[256]{0:T(256)} %param.31) | copy-start | bytes 3076
  122.5 32.6 %copy-start.10 = (u32[128]{0:T(128)S(1)}, u32[128]{0:T(128)}, u32[]{:S(2)}) copy-start(u32[128]{0:T(128)} %constant.4156) | copy-start | bytes 1540
  155.0 268.9 %all-reduce.23.cloned.1.call-start = ((), (), s32[]{:S(2)}) async-start(), calls=%async_computation.3 | async-start | bytes 196608
  290.1 0.6 copy-start.7
  290.8 345.2 %all-reduce.17.cloned.1.call-start = ((), (), s32[]{:S(2)}) async-start(), calls=%async_computation | async-start | bytes 655360 | tf_op jit(solution)/shard_map/psum | solution.py:157
  560.3 75.7 %copy-start.1 = (f32[81920]{0:T(1024)S(1)}, f32[81920]{0:T(1024)}, u32[]{:S(2)}) copy-start(f32[81920]{0:T(1024)} %param.36) | copy-start | bytes 983044
  561.2 349.1 %all-reduce.31.cloned.1.call-start = ((), (), s32[]{:S(2)}) async-start(), calls=%async_computation.7 | async-start | bytes 196608
  747.3 32.2 %copy-start.9 = (f32[301]{0:T(512)S(1)}, f32[301]{0:T(512)}, u32[]{:S(2)}) copy-start(f32[301]{0:T(512)} %param.37) | copy-start | bytes 3616
  779.4 396.3 %all-reduce.25.cloned.1.call-start = ((), (), s32[]{:S(2)}) async-start(), calls=%async_computation.4 | async-start | bytes 196608
  780.4 267.2 %copy-start.8 = (f32[24080]{0:T(1024)}, f32[24080]{0:T(1024)S(1)}, u32[]{:S(2)}) copy-start(f32[24080]{0:T(1024)S(1)} %reshape.17699) | copy-start | bytes 288964
  1046.9 0.6 copy-start.6
  1047.5 340.7 %all-reduce.19.cloned.1.call-start = ((), (), s32[]{:S(2)}) async-start(), calls=%async_computation.1 | async-start | bytes 655360 | tf_op jit(solution)/shard_map/psum | solution.py:157
  1312.6 75.7 %copy-start.2 = (f32[81920]{0:T(1024)S(1)}, f32[81920]{0:T(1024)}, u32[]{:S(2)}) copy-start(f32[81920]{0:T(1024)} %param.36) | copy-start | bytes 983044
  1313.4 349.1 %all-reduce.33.cloned.1.call-start = ((), (), s32[]{:S(2)}) async-start(), calls=%async_computation.8 | async-start | bytes 196608
  1531.8 330.4 %all-reduce.27.cloned.1.call-start = ((), (), s32[]{:S(2)}) async-start(), calls=%async_computation.5 | async-start | bytes 196608
  1732.7 0.6 copy-start.5
  1733.3 341.3 %all-reduce.21.cloned.1.call-start = ((), (), s32[]{:S(2)}) async-start(), calls=%async_computation.2 | async-start | bytes 655360 | tf_op jit(solution)/shard_map/psum | solution.py:157
  1998.9 75.7 %copy-start.4 = (f32[81920]{0:T(1024)S(1)}, f32[81920]{0:T(1024)}, u32[]{:S(2)}) copy-start(f32[81920]{0:T(1024)} %param.35) | copy-start | bytes 983044
Sparse Core Ops, SparseCore 0:
  155.1 134.0 all-reduce.28
  292.4 131.4 all-reduce.22
  561.3 74.6 all-reduce.16
  779.6 130.6 all-reduce.30
  1047.7 128.0 all-reduce.24
  1313.6 74.6 all-reduce.18
  1531.9 130.6 all-reduce.32
  1733.5 128.6 all-reduce.26
  1999.9 74.7 all-reduce.20
where the time goes:
time: 2100 us; the launch traced here: 2080 us
  waiting for transfers between devices  1010 us (48%)
  other arithmetic  446 us (21%)
  matrix products  233 us (11%)
  blocking collectives  196 us (9%)
  local copies, waits for them, and re-layouts  151 us (7%)
  loops' own time  30.7 us (1%)
    unnamed x15, waiting for transfers between devices  783 us
    psum x3, waiting for transfers between devices, synthesize(): return lax.psum(partial_value, 'coef')  224 us
    psum x3, blocking collectives, global_total(): return lax.psum(sums, ('pts', 'coef'))  196 us
    reduce_sum x24, other arithmetic, one_part(): jnp.sum(jnp.cos(phases) * picked[:slot_count] + jnp.sin(phases) * picked[...  156 us
    mul x24, other arithmetic, one_part(): jnp.cos(phases) * field_block[None, :]  140 us
    dot_general x24, matrix products, one_part(): lax.dot_general(stacked, one_hot, (((1,), (1,)), ((), ())), precision=hig...  136 us
    dynamic_slice x96, local copies, waits for them, and re-layouts, point_analysis(): folded = lax.scan(one_part, initial, blocks)[0]  99.9 us
    dot_general x24, matrix products, one_part(): jnp.dot(lookup, one_hot, precision=highest, preferred_element_type=jnp.fl...  97.2 us
  transfers between devices with their start and end apart: 9, of which 9 were waited for; matrix products, arithmetic and copies ran while one was open for 0% of the time, Pallas kernels for 0%

commit v1 on v0

v1 whole, which is shorter than its diff:
```python
import math
import numpy as np
import jax
import jax.numpy as jnp
from jax import lax
from jax.experimental import pallas as pl
from jax.experimental.pallas import tpu as pltpu
from jax.sharding import PartitionSpec as P

DEGREES = 301
DEG_PAD = 304
SLOTS = 40
TILES = 256
GROUPS = 8
OWN_TILES = TILES // GROUPS
ORDERS = 320
GRID = 1280
HALF = GRID // 2
LANES = 128
INV = 1.0 / DEGREES
BF = jnp.bfloat16
F32 = jnp.float32
ROUNDER = 12582912.0

NN = (((1,), (0,)), ((), ()))
NT = (((1,), (1,)), ((), ()))


def fit_even(f, terms):
    r = 0.502 * np.cos((np.arange(400) + 0.5) * np.pi / 800)
    a = np.stack([r ** (2 * k) for k in range(terms)], 1)
    return [float(v) for v in np.linalg.lstsq(a, f(r), rcond=None)[0]]


SIN_TERMS = fit_even(lambda r: np.sin(np.pi * r) / r, 5)
COS_TERMS = fit_even(lambda r: np.cos(np.pi * r), 5)


def horner(x, terms):
    total = terms[-1] * x + terms[-2]
    for term in terms[-3::-1]:
        total = total * x + term
    return total


def turn_trig(order, high, low):
    whole = order * high
    near = (whole + ROUNDER) - ROUNDER
    part = (whole - near) + order * low
    square = part * part
    s = horner(square, SIN_TERMS) * part
    c = horner(square, COS_TERMS)
    twice = s + s
    return 1.0 - twice * s, twice * c


def split(x):
    high = x.astype(BF)
    return high, (x - high.astype(F32)).astype(BF)


def dot(a, b, dims):
    return lax.dot_general(a, b, dims, preferred_element_type=F32)


def mm3(x, b_high, b_low, dims):
    rows = x.shape[0]
    high, low = split(x)
    both = dot(jnp.concatenate([high, low], 0), b_high, dims)
    return both[:rows] + both[rows:] + dot(high, b_low, dims)


def vmem(n):
    return [pl.BlockSpec(memory_space=pltpu.VMEM)] * n


SMEM = pl.BlockSpec(memory_space=pltpu.SMEM)


def params(mib):
    return pltpu.CompilerParams(vmem_limit_bytes=mib * 2**20)


def cost(flops, bytes_accessed):
    return pl.CostEstimate(flops=flops, bytes_accessed=bytes_accessed, transcendentals=0)


def tile_hits(tile_row, width):
    ids = lax.broadcasted_iota(jnp.int32, (TILES, width), 0).astype(F32).astype(BF)
    return jnp.where(ids == tile_row.astype(BF), jnp.ones((), BF), jnp.zeros((), BF))


WIDTH = 512
PER_STEP = 2


def moments_kernel(points, orders, field, w_first, w_second, total):
    total[...] = jnp.zeros_like(total)
    order = jnp.broadcast_to(orders[:, 0:1], (SLOTS, WIDTH))

    def step(i, carry):
        add = None
        for part in range(PER_STEP):
            data = points[:, pl.ds(pl.multiple_of((i * PER_STEP + part) * WIDTH, WIDTH), WIDTH)]
            high, low, weight, value = data[0:1], data[1:2], data[2:3], data[3:4]
            c_far, s_far = data[4:5], data[5:6]
            c, s = turn_trig(order, high, low)
            wc, ws = weight * c, weight * s
            rows = jnp.concatenate(
                [value * c, value * s, wc, ws, wc * c_far - ws * s_far, ws * c_far + wc * s_far], 0
            )
            rows_high, rows_low = split(rows)
            hits = tile_hits(data[6:7], WIDTH)
            got = dot(jnp.concatenate([rows_high, rows_low], 0), hits, NT)
            add = got if add is None else add + got
        total[...] += add
        return carry

    lax.fori_loop(0, points.shape[1] // (WIDTH * PER_STEP), step, 0)
    whole = total[0 : 6 * SLOTS] + total[6 * SLOTS : 12 * SLOTS]
    field[...] = whole[0 : 2 * SLOTS]
    blank = jnp.zeros((LANES - 2 * SLOTS, TILES), F32)
    w_first[...] = jnp.concatenate([whole[2 * SLOTS : 4 * SLOTS], blank], 0).T
    w_second[...] = jnp.concatenate([whole[4 * SLOTS : 6 * SLOTS], blank], 0).T


def moments(points, orders):
    n = points.shape[1]
    return pl.pallas_call(
        moments_kernel,
        out_shape=[
            jax.ShapeDtypeStruct((2 * SLOTS, TILES), F32),
            jax.ShapeDtypeStruct((TILES, LANES), F32),
            jax.ShapeDtypeStruct((TILES, LANES), F32),
        ],
        in_specs=vmem(2),
        out_specs=vmem(3),
        scratch_shapes=[pltpu.VMEM((12 * SLOTS, TILES), F32)],
        compiler_params=params(40),
        cost_estimate=cost(2 * 12 * SLOTS * TILES * n, 32 * n),
    )(points, orders)


def table_kernel(orders, cosine, sectoral, scale, p_high, p_low, left, right):
    order = jnp.broadcast_to(orders[:, 0:1], (SLOTS, TILES))
    order_sq = orders[...] * orders[...]
    cos_row = jnp.broadcast_to(cosine[...], (SLOTS, TILES))
    start = sectoral[...]

    def put(n, value):
        for b in range(SLOTS // 8):
            at = pl.ds(b * 8 * DEG_PAD + n, 8, stride=DEG_PAD)
            left[at, :] = value[8 * b : 8 * b + 8, 0:LANES]
            right[at, :] = value[8 * b : 8 * b + 8, LANES:TILES]

    def step(n, carried):
        recent, earlier, back = carried
        degree = n.astype(F32)
        ratio = jnp.maximum((degree * degree - order_sq) * scale[n], 1e-20)
        up = lax.rsqrt(ratio)
        this_back = ratio * up
        up2 = jnp.concatenate([up, up], 1)
        back2 = jnp.concatenate([back, back], 1)
        grown = up2 * (cos_row * recent - back2 * earlier)
        value = jnp.where(order > degree, 0.0, jnp.where(order == degree, start, grown))
        put(n, value)
        return value, recent, this_back

    empty = jnp.zeros((SLOTS, TILES), F32)
    unset = start * 0.0
    lax.fori_loop(0, DEGREES, step, (unset, unset, order_sq * 0.0))
    for n in range(DEGREES, DEG_PAD):
        put(n, empty)

    def pack(slot, carry):
        at = pl.ds(pl.multiple_of(slot * DEG_PAD, 8), DEG_PAD)
        high, low = split(jnp.concatenate([left[at, :], right[at, :]], 1))
        p_high[slot] = high
        p_low[slot] = low
        return carry

    lax.fori_loop(0, SLOTS, pack, 0)


def legendre_table(orders, cosine, sectoral, scale):
    shape = jax.ShapeDtypeStruct((SLOTS, DEG_PAD, TILES), BF)
    return pl.pallas_call(
        table_kernel,
        out_shape=[shape, shape],
        in_specs=vmem(3) + [SMEM],
        out_specs=vmem(2),
        scratch_shapes=[pltpu.VMEM((SLOTS * DEG_PAD, LANES), F32)] * 2,
        compiler_params=params(48),
        cost_estimate=cost(20 * SLOTS * DEG_PAD * TILES, 4 * SLOTS * DEG_PAD * TILES),
    )(orders, cosine, sectoral, scale)


def by_slot(vector, p_high, p_low, width, dims, put):
    row = lax.broadcasted_iota(jnp.int32, (16, width), 0)

    def group(g, carry):
        at = pl.multiple_of(g * 8, 8)
        rows = jnp.concatenate([vector[pl.ds(at, 8), :], vector[pl.ds(at + SLOTS, 8), :]], 0)
        high, low = split(rows)
        both = jnp.concatenate([high, low], 0)
        out = jnp.zeros((16, width), F32)
        for i in range(8):
            first = dot(both, p_high[at + i], dims)
            total = first[0:16] + first[16:32] + dot(high, p_low[at + i], dims)
            out = jnp.where((row == i) | (row == i + 8), total, out)
        put(at, out)
        return carry

    lax.fori_loop(0, SLOTS // 8, group, 0)


def fold_kernel(vector, p_high, p_low, out, rows):
    def put(at, value):
        rows[pl.ds(at, 8), :] = value[0:8]
        rows[pl.ds(at + SLOTS, 8), :] = value[8:16]

    rows[2 * SLOTS :, :] = jnp.zeros((LANES - 2 * SLOTS, TILES), F32)
    by_slot(vector, p_high, p_low, TILES, NN, put)
    out[...] = rows[...].T


def fold(vector, p_high, p_low):
    return pl.pallas_call(
        fold_kernel,
        out_shape=jax.ShapeDtypeStruct((TILES, LANES), F32),
        in_specs=vmem(3),
        out_specs=pl.BlockSpec(memory_space=pltpu.VMEM),
        scratch_shapes=[pltpu.VMEM((LANES, TILES), F32)],
        compiler_params=params(32),
        cost_estimate=cost(64 * SLOTS * DEG_PAD * TILES, 4 * SLOTS * DEG_PAD * TILES),
    )(vector, p_high, p_low)


def unfold_kernel(flip, field, p_high, p_low, out, rows):
    factor = INV * INV if flip else INV
    if flip:
        rows[...] = field[...].T
        source = rows
    else:
        source = field

    def put(at, value):
        out[pl.ds(at, 8), :] = value[0:8] * factor
        out[pl.ds(at + SLOTS, 8), :] = value[8:16] * factor

    by_slot(source, p_high, p_low, DEG_PAD, NT, put)


def unfold(field, p_high, p_low, flip):
    return pl.pallas_call(
        lambda *refs: unfold_kernel(flip, *refs),
        out_shape=jax.ShapeDtypeStruct((2 * SLOTS, DEG_PAD), F32),
        in_specs=vmem(3),
        out_specs=pl.BlockSpec(memory_space=pltpu.VMEM),
        scratch_shapes=[pltpu.VMEM((LANES, TILES), F32)],
        compiler_params=params(32),
        cost_estimate=cost(64 * SLOTS * DEG_PAD * TILES, 4 * SLOTS * DEG_PAD * TILES),
    )(field, p_high, p_low)


F_ROWS = TILES
EXTRA_FIRST = TILES + 2 * OWN_TILES


def slot_hits(order_row):
    wanted = lax.broadcasted_iota(jnp.int32, (ORDERS, LANES), 0).astype(F32)
    return jnp.where(wanted == order_row, 1.0, 0.0).astype(BF)


def two_halves(x):
    lane = lax.broadcasted_iota(jnp.int32, x.shape, 1)
    return jnp.where(lane < SLOTS, x, 0.0), jnp.where((lane >= SLOTS) & (lane < 2 * SLOTS), x, 0.0)


def to_natural(pieces, hits):
    total = None
    for per_source, hit in zip(pieces, hits):
        rows = [half for x in per_source for half in two_halves(x)]
        high, low = split(jnp.concatenate(rows, 0))
        got = dot(jnp.concatenate([high, low], 0), hit, NT)
        total = got if total is None else total + got
    n = total.shape[0] // 2
    return total[:n] + total[n:]


def grid_first_kernel(me, got, c1, c1l, c2, c2l, s1, s1l, s2, s2l, back, kept):
    mine = pl.multiple_of(me[0] * OWN_TILES, OWN_TILES)
    t = OWN_TILES
    hits = [slot_hits(got[g, EXTRA_FIRST : EXTRA_FIRST + 1, :]) for g in range(GROUPS)]
    nat = to_natural(
        [
            [got[g, pl.ds(mine, t), :], got[g, TILES : TILES + t, :], got[g, TILES + t : TILES + 2 * t, :]]
            for g in range(GROUPS)
        ],
        hits,
    )
    k = lax.broadcasted_iota(jnp.int32, (1, ORDERS), 1)
    k_first = jnp.where(k == 0, 1.0 / GRID, 2.0 / GRID)
    k_second = jnp.where(k + ORDERS <= 2 * (DEGREES - 1), 2.0 / GRID, 0.0)
    even = mm3(jnp.concatenate([nat[0:t], nat[2 * t : 3 * t] * k_first], 0), c1[...], c1l[...], NN)
    odd = mm3(jnp.concatenate([nat[t : 2 * t], nat[3 * t : 4 * t] * k_first], 0), s1[...], s1l[...], NN)
    w_even = even[t:] + mm3(nat[4 * t : 5 * t] * k_second, c2[...], c2l[...], NN)
    w_odd = odd[t:] + mm3(nat[5 * t : 6 * t] * k_second, s2[...], s2l[...], NN)
    even, odd = even[:t], odd[:t]
    h_even = 2.0 * (w_even * even + w_odd * odd)
    h_odd = 2.0 * (w_even * odd + w_odd * even)
    energy = jnp.sum(jnp.sum(h_even * even + h_odd * odd, axis=1, keepdims=True), axis=0, keepdims=True)
    kept[0] = even
    kept[1] = odd
    kept[2] = w_even
    kept[3] = w_odd
    hc = mm3(h_even, c1[...], c1l[...], NT)
    hs = mm3(h_odd, s1[...], s1l[...], NT)
    c_high, c_low = split(hc)
    s_high, s_low = split(hs)
    stack = jnp.concatenate([c_high, c_low, s_high, s_low], 0)
    lane = lax.broadcasted_iota(jnp.int32, (t, LANES), 1)
    for g in range(GROUPS):
        slots = dot(stack, hits[g], NN)
        back[g, 0:t, :] = jnp.where(
            lane < SLOTS, slots[0:t] + slots[t : 2 * t], slots[2 * t : 3 * t] + slots[3 * t :]
        )
        back[g, t : t + 8, :] = jnp.broadcast_to(energy, (8, LANES))


def grid_first(me, got, waves):
    return pl.pallas_call(
        grid_first_kernel,
        out_shape=[
            jax.ShapeDtypeStruct((GROUPS, OWN_TILES + 8, LANES), F32),
            jax.ShapeDtypeStruct((4, OWN_TILES, HALF), F32),
        ],
        in_specs=[SMEM] + vmem(9),
        out_specs=vmem(2),
        compiler_params=params(32),
        cost_estimate=cost(10**9, 5 * 10**6),
    )(me, got, *waves)


def grid_second_kernel(me, ratio, got, kept, c1, c1l, s1, s1l, out):
    mine = pl.multiple_of(me[0] * OWN_TILES, OWN_TILES)
    t = OWN_TILES
    hits = [slot_hits(got[g, TILES : TILES + 1, :]) for g in range(GROUPS)]
    nat = to_natural([[got[g, pl.ds(mine, t), :]] for g in range(GROUPS)], hits)
    even = mm3(nat[0:t], c1[...], c1l[...], NN) + ratio[0] * kept[0]
    odd = mm3(nat[t:], s1[...], s1l[...], NN) + ratio[0] * kept[1]
    w_even, w_odd = kept[2], kept[3]
    terms = 2.0 * w_even * (even * even + odd * odd) + 4.0 * w_odd * (even * odd)
    energy = jnp.sum(jnp.sum(terms, axis=1, keepdims=True), axis=0, keepdims=True)
    out[...] = jnp.broadcast_to(energy, (8, LANES))


def grid_second(me, ratio, got, kept, waves):
    return pl.pallas_call(
        grid_second_kernel,
        out_shape=jax.ShapeDtypeStruct((8, LANES), F32),
        in_specs=[SMEM, SMEM] + vmem(6),
        out_specs=pl.BlockSpec(memory_space=pltpu.VMEM),
        compiler_params=params(32),
        cost_estimate=cost(10**9, 5 * 10**6),
    )(me, ratio, got, kept, *waves)


S_WIDTH = 512


def values_kernel(extra_row, me, points, got, out, z_high, z_low, picked):
    hits = jnp.concatenate(
        [slot_hits(got[g, extra_row : extra_row + 1, :]) for g in range(GROUPS)], 1
    )
    halves = [two_halves(got[g, 0:TILES, :]) for g in range(GROUPS)]
    for c in range(2):
        high, low = split(jnp.concatenate([h[c] for h in halves], 1))
        z_high[pl.ds(c * ORDERS, ORDERS), :] = dot(hits, high, NT).astype(BF)
        z_low[pl.ds(c * ORDERS, ORDERS), :] = dot(hits, low, NT).astype(BF)
    own = out.shape[0] * S_WIDTH
    first = me[0] * own
    near_order = lax.broadcasted_iota(jnp.int32, (8, S_WIDTH), 0).astype(F32)

    def step(i, carry):
        data = points[:, pl.ds(pl.multiple_of(first + i * S_WIDTH, S_WIDTH), S_WIDTH)]
        hits_here = tile_hits(data[6:7], S_WIDTH)
        picked[...] = dot(z_high[...], hits_here, NN) + dot(z_low[...], hits_here, NN)
        high, low = data[0:1], data[1:2]
        c, s = turn_trig(near_order, high, low)
        c8, s8 = turn_trig(8.0, high, low)
        c8 = jnp.broadcast_to(c8, c.shape)
        s8 = jnp.broadcast_to(s8, c.shape)
        total = None
        for b in range(ORDERS // 8):
            add = c * picked[8 * b : 8 * b + 8, :] + s * picked[ORDERS + 8 * b : ORDERS + 8 * b + 8, :]
            total = add if total is None else total + add
            c, s = c * c8 - s * s8, s * c8 + c * s8
        out[pl.ds(i, 1), :] = jnp.sum(total, axis=0, keepdims=True)
        return carry

    lax.fori_loop(0, out.shape[0], step, 0)


def point_values(me, points, got, extra_row):
    own = points.shape[1] // GROUPS
    return pl.pallas_call(
        lambda *refs: values_kernel(extra_row, *refs),
        out_shape=jax.ShapeDtypeStruct((own // S_WIDTH, S_WIDTH), F32),
        in_specs=[SMEM] + vmem(2),
        out_specs=pl.BlockSpec(memory_space=pltpu.VMEM),
        scratch_shapes=[
            pltpu.VMEM((2 * ORDERS, TILES), BF),
            pltpu.VMEM((2 * ORDERS, TILES), BF),
            pltpu.VMEM((2 * ORDERS, S_WIDTH), F32),
        ],
        compiler_params=params(40),
        cost_estimate=cost(8 * ORDERS * TILES * own, 5 * 10**6),
    )(me, points, got)


def waves():
    k = np.arange(2 * ORDERS)[:, None]
    q = np.arange(HALF)[None, :] * 2 + 1
    phase = 2 * np.pi * ((k * q) % (2 * GRID)) / (2 * GRID)
    out = []
    for f in (np.cos(phase), np.sin(phase)):
        high = f.astype(jnp.bfloat16)
        low = (f - high.astype(np.float64)).astype(jnp.bfloat16)
        out += [high[:ORDERS], low[:ORDERS], high[ORDERS:], low[ORDERS:]]
    return out


def sectoral_values(orders, sines):
    single = (orders == 0.0).astype(F32)
    log_lead = 0.5 * (
        jnp.log(2.0 - single)
        + lax.lgamma(orders + 1.5)
        - lax.lgamma(orders * 0.0 + 1.5)
        - lax.lgamma(orders + 1.0)
    )
    return jnp.exp(log_lead + orders * jnp.log(sines))


def pts_total(x):
    for d in (1, 2, 4, 8):
        x = x + lax.ppermute(x, "pts", [(i, i ^ d) for i in range(16)])
    return x


def swap(x):
    return lax.all_to_all(x, "coef", 0, 0)


def shards(colatitude, longitude, tile_of_point, order_of_slot, observations, obs_weight, prior):
    me = lax.axis_index("coef").astype(jnp.int32).reshape(1)
    local_tile = (tile_of_point - lax.axis_index("pts") * TILES).astype(F32)
    order = order_of_slot.astype(F32)
    orders = jnp.broadcast_to(order[:, None], (SLOTS, LANES))
    cosine = jnp.cos(colatitude)[None, :]
    sectoral = sectoral_values(order[:, None], jnp.sin(colatitude)[None, :])
    degree = np.arange(DEG_PAD, dtype=np.float64)
    scale = jnp.asarray((1.0 / (4 * degree * degree - 1)).astype(np.float32))
    c1, c1l, c2, c2l, s1, s1l, s2, s2l = [jnp.asarray(x) for x in waves()]

    turn = 2.0 * math.pi
    turn_high = 6.28125
    turn_low = turn - turn_high
    high = jnp.round(longitude * (4096.0 / turn)) * (1.0 / 4096.0)
    low = ((longitude - high * turn_high) - high * turn_low) * (1.0 / turn)
    far = high * ORDERS
    far = ((far - jnp.round(far)) + low * ORDERS) * turn
    points = jnp.stack(
        [high, low, obs_weight, obs_weight * observations, jnp.cos(far), jnp.sin(far), local_tile, local_tile]
    )

    field, w_first, w_second = moments(points, orders)
    p_high, p_low = legendre_table(orders, cosine, sectoral, scale)
    prior_row = jnp.pad(prior, (0, DEG_PAD - DEGREES))[None, :]

    residual = pts_total(unfold(field, p_high, p_low, False))
    fourier = fold(residual, p_high, p_low)

    order_row = jnp.concatenate([order, order, jnp.full((LANES - 2 * SLOTS,), -1.0, F32)])[None]

    def extras(*scalars):
        rows = [order_row] + [jnp.full((1, LANES), s, F32) for s in scalars]
        return jnp.concatenate(rows + [jnp.zeros((8 - len(rows), LANES), F32)], 0)

    def everywhere(x):
        return jnp.broadcast_to(x[None], (GROUPS,) + x.shape)

    def by_tiles(x):
        return x.reshape(GROUPS, OWN_TILES, LANES)

    sent = jnp.concatenate(
        [
            everywhere(fourier),
            by_tiles(w_first),
            by_tiles(w_second),
            everywhere(extras(jnp.sum(residual * residual), jnp.sum(prior_row * residual * residual))),
        ],
        1,
    )
    got = swap(sent)
    sums = jnp.sum(got[:, EXTRA_FIRST : EXTRA_FIRST + 8, 0], 0)
    norm_0, prior_00 = sums[1], sums[2]

    back, kept = grid_first(me, got, (c1, c1l, c2, c2l, s1, s1l, s2, s2l))
    seen = swap(back)
    energy_part = jnp.sum(seen[:, OWN_TILES, 0])
    applied = unfold(seen[:, :OWN_TILES].reshape(TILES, LANES), p_high, p_low, True)
    lane = lax.broadcasted_iota(jnp.int32, applied.shape, 1)
    values_0 = point_values(me, points, got, EXTRA_FIRST)
    applied = pts_total(jnp.where(lane == DEGREES, energy_part, applied))
    step_0 = norm_0 / (applied[0, DEGREES] * (INV * INV) + prior_00)
    applied = jnp.where(lane < DEGREES, applied + prior_row * residual, 0.0)
    residual_1 = residual - step_0 * applied

    fourier_1 = fold(residual_1, p_high, p_low)
    got_1 = swap(
        everywhere(
            jnp.concatenate(
                [
                    fourier_1,
                    extras(
                        jnp.sum(residual_1 * residual_1),
                        jnp.sum(prior_row * residual * residual_1),
                        jnp.sum(prior_row * residual_1 * residual_1),
                    ),
                ],
                0,
            )
        )
    )
    sums = jnp.sum(got_1[:, TILES : TILES + 8, 0], 0)
    norm_1, prior_01, prior_11 = sums[1], sums[2], sums[3]
    ratio = norm_1 / norm_0
    energy_1 = pts_total(grid_second(me, ratio.reshape(1), got_1, kept, (c1, c1l, s1, s1l)))
    values_1 = point_values(me, points, got_1, TILES)

    own_rows = values_0.size // LANES
    last = swap(
        everywhere(
            jnp.concatenate(
                [values_0.reshape(own_rows, LANES), values_1.reshape(own_rows, LANES), energy_1], 0
            )
        )
    )
    energy_1 = jnp.sum(last[:, 2 * own_rows, 0])
    curvature = energy_1 * (INV * INV) + prior_11 + 2.0 * ratio * prior_01 + ratio * ratio * prior_00
    step_1 = norm_1 / curvature
    on_0 = step_0 + step_1 * ratio
    vector = on_0 * residual + step_1 * residual_1
    fitted = on_0 * last[:, :own_rows] + step_1 * last[:, own_rows : 2 * own_rows]
    coefficients = vector.reshape(2, SLOTS, DEG_PAD)[:, :, :DEGREES].transpose(2, 0, 1)
    return coefficients, observations - fitted.reshape(-1) * INV


def solution(mesh):
    placed = (P("pts"), P("pts"), P("pts"), P("coef"), P("pts"), P("pts"), P())
    return jax.shard_map(
        shards,
        mesh=mesh,
        in_specs=placed,
        out_specs=(P(None, None, "coef"), P("pts")),
        check_vma=False,
    )
```

time: 2100 us -> 275 us (0.13)
  waiting for transfers between devices: 1010 us -> 58.4 us
  other arithmetic: 446 us -> 11.9 us
  matrix products: 233 us -> 0 us
  blocking collectives: 196 us -> 16.1 us
  local copies, waits for them, and re-layouts: 151 us -> 38.7 us
  Pallas kernels: 0 us -> 104 us
  starting transfers between devices: 0.37 us -> 37 us
  loops' own time: 30.7 us -> 0 us
    unnamed x15 -> x0, waiting for transfers between devices: 783 us -> none
    dot_general x48 -> x0, matrix products: 233 us -> none  [the longest x24 136 us: one_part(): lax.dot_general(stacked, one_hot, (((1,), (1,)), ((), ())), precision=hig...]
    psum x3 -> x0, waiting for transfers between devices: 224 us -> none  [synthesize(): return lax.psum(partial_value, 'coef')]
    psum x3 -> x0, blocking collectives: 196 us -> none  [global_total(): return lax.psum(sums, ('pts', 'coef'))]
    reduce_sum x90 -> x6, other arithmetic: 177 us -> 2.8 us  [the longest x1 0.67 us: shards(): jnp.sum(prior_row * residual_1 * residual_1)]
    mul x30 -> x2, other arithmetic: 142 us -> 0.84 us  [the longest x1 0.79 us: shards(): obs_weight * observations]
    pallas_call x0 -> x10, Pallas kernels: none -> 104 us  [the longest x1 45.3 us: moments(): pl.pallas_call(moments_kernel, out_shape=[jax.ShapeDtypeStruct((2 * SLOTS...]
    dynamic_slice x96 -> x0, local copies, waits for them, and re-layouts: 99.9 us -> none  [point_analysis(): folded = lax.scan(one_part, initial, blocks)[0]]
  transfers between devices with their start and end apart: 9 -> 15, of which waited for: 9 -> 13; matrix products, arithmetic and copies ran while one was open for 0% -> 0% of each run, Pallas kernels for 0% -> 9%
where the time goes in v1:
time: 275 us; the launch traced here: 273 us
  Pallas kernels  104 us (38%)
  waiting for transfers between devices  58.4 us (21%)
  local copies, waits for them, and re-layouts  38.7 us (14%)
  starting transfers between devices  37 us (13%)
  blocking collectives  16.1 us (6%)
  other arithmetic  11.9 us (4%)
  between operations  7.25 us (3%)
    pallas_call x1, Pallas kernels, moments(): pl.pallas_call(moments_kernel, out_shape=[jax.ShapeDtypeStruct((2 * SLOTS...  45.3 us
    all_to_all x3, waiting for transfers between devices, swap(): return lax.all_to_all(x, 'coef', 0, 0)  32.4 us
    ppermute x12, waiting for transfers between devices, pts_total(): x = x + lax.ppermute(x, 'pts', [(i, i ^ d) for i in range(16)])  26 us
    unnamed x60, local copies, waits for them, and re-layouts  25.4 us
    pallas_call x2, Pallas kernels, point_values(): pl.pallas_call(lambda *refs: values_kernel(extra_row, *refs), out_shape=j...  23.6 us
    ppermute x12, starting transfers between devices, pts_total(): x = x + lax.ppermute(x, 'pts', [(i, i ^ d) for i in range(16)])  23.4 us
    pallas_call x1, Pallas kernels, legendre_table(): pl.pallas_call(table_kernel, out_shape=[shape, shape], in_specs=vmem(3) +...  17.1 us
    all_to_all x1, blocking collectives, swap(): return lax.all_to_all(x, 'coef', 0, 0)  16.1 us
  transfers between devices with their start and end apart: 15, of which 13 were waited for; matrix products, arithmetic and copies ran while one was open for 0% of the time, Pallas kernels for 9%

profile of v1, /device:TPU:0, one launch (start us, length us, event | category | flops | bytes accessed | tf_op | source)
XLA Modules:
  0.0 273.3 jit_solution(5259551748184358420)
XLA Ops:
  2.2 3.1 %fusion.12 = (f32[81920]{0:T(1024)}, f32[81920]{0:T(1024)}, f32[81920]{0:T(1024)}, f32[81920]{0:T(1024)}) fusion(f32[81920]{0:T(1024)} %param.17), kind=kLoop, calls=%fused_computation.29 | loop fusion | flops 1146880 | bytes 1638400 | tf_op jit(solution)/shard_map/sin | solution.py:474
  6.2 6.4 %stack.32.points.refs_1_ = f32[8,81920]{1,0:T(8,128)S(1)} concatenate(f32[1,81920]{1,0:T(1,128)} %bitcast.37, f32[1,81920]{1,0:T(1,128)} %bitcast.36, f32[1,81920]{1,0:T(1,128)S(1)} %bitcast.33, f32[1,81920]{1,0:T(1,128)} %bitcast.38, f32[1,81920]{1,0:T(1,128)} %bitcast.35, f32[1,81920]{1,0:T(1,128)} %bitcast.34, f32[1,81920]{1,0:T(1,128)S(1)} %bitcast.31, f32[1,81920]{1,0:T(1,128)S(1)} %bitcast.32), dimensions={0} | concatenate | bytes 5242880 | tf_op jit(solution)/shard_map/stack | solution.py:473
  12.8 45.3 %shard_map.167 = (f32[80,256]{1,0:T(8,128)S(1)}, f32[256,128]{1,0:T(8,128)S(1)}, f32[256,128]{1,0:T(8,128)S(1)}) custom-call(f32[8,81920]{1,0:T(8,128)S(1)} %stack.32.points.refs_1_, f32[40,128]{1,0:T(8,128)S(1)} %broadcast_in_dim.71.orders), custom_call_target="tpu_custom_call" | custom-call | flops 20132659200 | bytes 2621440 | tf_op jit(solution)/shard_map/pallas_call | solution.py:129
  58.2 17.1 %shard_map.168 = (bf16[40,304,256]{2,1,0:T(8,128)(2,1)}, bf16[40,304,256]{2,1,0:T(8,128)(2,1)}) custom-call(f32[40,128]{1,0:T(8,128)S(1)} %broadcast_in_dim.71.orders, f32[1,256]{1,0:T(1,128)S(1)} %bitcast.30, f32[40,256]{1,0:T(8,128)S(1)} %add_exponential_fusion.sectoral, f32[304]{0:T(512)S(1)} %copy-done.23), custom_call_target="tpu_custom_call" | custom-call | flops 62259200 | bytes 12451840 | tf_op jit(solution)/shard_map/pallas_call | solution.py:187
  80.8 3.9 %shard_map.169 = f32[80,304]{1,0:T(8,128)S(1)} custom-call(f32[80,256]{1,0:T(8,128)S(1)} %get-tuple-element.9.refs_0_, bf16[40,304,256]{2,1,0:T(8,128)(2,1)S(1)} %copy-done, bf16[40,304,256]{2,1,0:T(8,128)(2,1)S(1)} %copy-done.4), custom_call_target="tpu_custom_call" | custom-call | flops 199229440 | bytes 12451840 | tf_op jit(solution)/shard_map/pallas_call | solution.py:255
  87.7 3.8 %collective-permute-done.1 = f32[80,304]{1,0:T(8,128)S(1)} collective-permute-done((f32[80,304]{1,0:T(8,128)S(1)}, f32[80,304]{1,0:T(8,128)S(1)}, u32[]{:S(2)}, u32[]{:S(2)}) %collective-permute-start.1) | collective-permute-done | bytes 97312 | tf_op jit(solution)/shard_map/ppermute | solution.py:447
  91.5 3.2 %collective-permute-start.2 = (f32[80,304]{1,0:T(8,128)S(1)}, f32[80,304]{1,0:T(8,128)S(1)}, u32[]{:S(2)}, u32[]{:S(2)}) collective-permute-start(f32[80,304]{1,0:T(8,128)S(1)} %add.109), channel_id=1, source_target_pairs={{0,32},{8,40},{16,48},{24,56},{32,0},{40,8},{48,16},{56,24},{64,96... | collective-permute-start | bytes 291848 | tf_op jit(solution)/shard_map/ppermute | solution.py:447
  94.8 3.2 %collective-permute-done.2 = f32[80,304]{1,0:T(8,128)S(1)} collective-permute-done((f32[80,304]{1,0:T(8,128)S(1)}, f32[80,304]{1,0:T(8,128)S(1)}, u32[]{:S(2)}, u32[]{:S(2)}) %collective-permute-start.2) | collective-permute-done | bytes 97312 | tf_op jit(solution)/shard_map/ppermute | solution.py:447
  98.0 3.3 %collective-permute-start.3 = (f32[80,304]{1,0:T(8,128)S(1)}, f32[80,304]{1,0:T(8,128)S(1)}, u32[]{:S(2)}, u32[]{:S(2)}) collective-permute-start(f32[80,304]{1,0:T(8,128)S(1)} %add.110), channel_id=1, source_target_pairs={{0,64},{8,72},{16,80},{24,88},{32,96},{40,104},{48,112},{56,120},{... | collective-permute-start | bytes 291848 | tf_op jit(solution)/shard_map/ppermute | solution.py:447
  101.4 3.0 %collective-permute-done.3 = f32[80,304]{1,0:T(8,128)S(1)} collective-permute-done((f32[80,304]{1,0:T(8,128)S(1)}, f32[80,304]{1,0:T(8,128)S(1)}, u32[]{:S(2)}, u32[]{:S(2)}) %collective-permute-start.3) | collective-permute-done | bytes 97312 | tf_op jit(solution)/shard_map/ppermute | solution.py:447
  110.6 6.6 %all-to-all-start = ((f32[8,328,128]{2,1,0:T(8,128)}), f32[8,328,128]{2,1,0:T(8,128)S(1)}, u32[]{:S(2)}, u32[]{:S(2)}) async-start(f32[8,328,128]{2,1,0:T(8,128)} %pad_maximum_fusion), calls=%async_computation | async-start | bytes 2686976 | tf_op jit(solution)/shard_map/all_to_all | solution.py:452
  117.2 16.1 %all-to-all-done.got.refs_2_ = f32[8,328,128]{2,1,0:T(8,128)S(1)} async-done(((f32[8,328,128]{2,1,0:T(8,128)}), f32[8,328,128]{2,1,0:T(8,128)S(1)}, u32[]{:S(2)}, u32[]{:S(2)}) %all-to-all-start) | async-done | bytes 1343520 | tf_op jit(solution)/shard_map/all_to_all | solution.py:452
  137.4 3.7 %shard_map.171 = (f32[8,40,128]{2,1,0:T(8,128)}, f32[4,32,640]{2,1,0:T(8,128)S(1)}) custom-call(s32[1]{0:T(128)} %bitcast.12.me.refs_0_, f32[8,328,128]{2,1,0:T(8,128)S(1)} %all-to-all-done.got.refs_2_, bf16[320,640]{1,0:T(8,128)(2,1)S(1)} %copy-done.11, bf16[320,640]{1,0:T(8,128)(2,1)S(1)} %copy-done.12, bf16[320,640]{1,0:T(8,128)(2,1)S(1)} %copy-done.17, ...), custom_call_target="tpu_custom_call" | custom-call | flops 1000000000 | bytes 5000000 | tf_op jit(solution)/shard_map/pallas_call | solution.py:332
  141.1 3.4 %all-to-all-start.1 = ((f32[8,40,128]{2,1,0:T(8,128)}), f32[8,40,128]{2,1,0:T(8,128)S(1)}, u32[]{:S(2)}, u32[]{:S(2)}) async-start(f32[8,40,128]{2,1,0:T(8,128)} %get-tuple-element.14), calls=%async_computation.1 | async-start | bytes 327680 | tf_op jit(solution)/shard_map/all_to_all | solution.py:452
  144.5 6.7 %all-to-all-done.1 = f32[8,40,128]{2,1,0:T(8,128)S(1)} async-done(((f32[8,40,128]{2,1,0:T(8,128)}), f32[8,40,128]{2,1,0:T(8,128)S(1)}, u32[]{:S(2)}, u32[]{:S(2)}) %all-to-all-start.1) | async-done | bytes 163872 | tf_op jit(solution)/shard_map/all_to_all | solution.py:452
  156.8 4.0 %shard_map.172 = f32[80,304]{1,0:T(8,128)S(1)} custom-call(f32[256,128]{1,0:T(8,128)S(1)} %bitcast.27, bf16[40,304,256]{2,1,0:T(8,128)(2,1)S(1)} %copy-done.2, bf16[40,304,256]{2,1,0:T(8,128)(2,1)S(1)} %copy-done.6), custom_call_target="tpu_custom_call" | custom-call | flops 199229440 | bytes 12451840 | tf_op jit(solution)/shard_map/pallas_call | solution.py:255
  165.7 3.9 %collective-permute-done.5 = f32[80,304]{1,0:T(8,128)S(1)} collective-permute-done((f32[80,304]{1,0:T(8,128)S(1)}, f32[80,304]{1,0:T(8,128)S(1)}, u32[]{:S(2)}, u32[]{:S(2)}) %collective-permute-start.5) | collective-permute-done | bytes 97312 | tf_op jit(solution)/shard_map/ppermute | solution.py:447
  169.6 3.1 %collective-permute-start.6 = (f32[80,304]{1,0:T(8,128)S(1)}, f32[80,304]{1,0:T(8,128)S(1)}, u32[]{:S(2)}, u32[]{:S(2)}) collective-permute-start(f32[80,304]{1,0:T(8,128)S(1)} %add.113), channel_id=1, source_target_pairs={{0,32},{8,40},{16,48},{24,56},{32,0},{40,8},{48,16},{56,24},{64,96... | collective-permute-start | bytes 291848 | tf_op jit(solution)/shard_map/ppermute | solution.py:447
  172.8 3.2 %collective-permute-done.6 = f32[80,304]{1,0:T(8,128)S(1)} collective-permute-done((f32[80,304]{1,0:T(8,128)S(1)}, f32[80,304]{1,0:T(8,128)S(1)}, u32[]{:S(2)}, u32[]{:S(2)}) %collective-permute-start.6) | collective-permute-done | bytes 97312 | tf_op jit(solution)/shard_map/ppermute | solution.py:447
  195.8 16.1 %all_to_all.20.refs_2_.got = f32[8,264,128]{2,1,0:T(8,128)S(1)} all-to-all(f32[8,264,128]{2,1,0:T(8,128)S(1)} %broadcast_in_dim.86), channel_id=1, replica_groups=mesh['pts'=16,'coef'=8] {'coef'}, dimensions={0} | all-to-all | bytes 2162688 | tf_op jit(solution)/shard_map/all_to_all | solution.py:452
  225.7 11.8 %shard_map.174 = f32[20,512]{1,0:T(8,128)S(1)} custom-call(s32[1]{0:T(128)} %bitcast.12.me.refs_0_, f32[8,81920]{1,0:T(8,128)S(1)} %copy-done.9, f32[8,328,128]{2,1,0:T(8,128)S(1)} %all-to-all-done.got.refs_2_), custom_call_target="tpu_custom_call" | custom-call | flops 6710886400 | bytes 5000000 | tf_op jit(solution)/shard_map/pallas_call | solution.py:407
  242.2 11.8 %shard_map.175 = f32[20,512]{1,0:T(8,128)S(1)} custom-call(s32[1]{0:T(128)} %bitcast.12.me.refs_0_, f32[8,81920]{1,0:T(8,128)S(1)} %copy-done.10, f32[8,264,128]{2,1,0:T(8,128)S(1)} %all_to_all.20.refs_2_.got), custom_call_target="tpu_custom_call" | custom-call | flops 6710886400 | bytes 5000000 | tf_op jit(solution)/shard_map/pallas_call | solution.py:407
  255.0 3.7 %all-to-all-start.3 = ((f32[8,168,128]{2,1,0:T(8,128)}), f32[8,168,128]{2,1,0:T(8,128)S(1)}, u32[]{:S(2)}, u32[]{:S(2)}) async-start(f32[8,168,128]{2,1,0:T(8,128)} %broadcast_in_dim.87), calls=%async_computation.3 | async-start | bytes 1376256 | tf_op jit(solution)/shard_map/all_to_all | solution.py:452
  259.8 9.5 %all-to-all-done.3 = f32[8,168,128]{2,1,0:T(8,128)S(1)} async-done(((f32[8,168,128]{2,1,0:T(8,128)}), f32[8,168,128]{2,1,0:T(8,128)S(1)}, u32[]{:S(2)}, u32[]{:S(2)}) %all-to-all-start.3) | async-done | bytes 688160 | tf_op jit(solution)/shard_map/all_to_all | solution.py:452
  (135 shorter events, 70.1 us)
Async XLA Ops:
  12.7 45.4 %copy-start.8 = (f32[8,81920]{1,0:T(8,128)}, f32[8,81920]{1,0:T(8,128)S(1)}, u32[]{:S(2)}) copy-start(f32[8,81920]{1,0:T(8,128)S(1)} %stack.32.points.refs_1_) | copy-start | bytes 7864324
  12.8 45.4 %copy-start.23 = (f32[304]{0:T(512)S(1)}, f32[304]{0:T(512)}, u32[]{:S(2)}) copy-start(f32[304]{0:T(512)} %constant.124.clone.scale) | copy-start | bytes 3652
  80.8 24.3 %copy-start.1 = (bf16[40,304,256]{2,1,0:T(8,128)(2,1)S(1)}, bf16[40,304,256]{2,1,0:T(8,128)(2,1)}, u32[]{:S(2)}) copy-start(bf16[40,304,256]{2,1,0:T(8,128)(2,1)} %get-tuple-element.10.refs_1_.p_high) | copy-start | bytes 18677764
  80.8 24.3 %copy-start.5 = (bf16[40,304,256]{2,1,0:T(8,128)(2,1)S(1)}, bf16[40,304,256]{2,1,0:T(8,128)(2,1)}, u32[]{:S(2)}) copy-start(bf16[40,304,256]{2,1,0:T(8,128)(2,1)} %get-tuple-element.11.refs_2_.p_low) | copy-start | bytes 18677764
  84.7 1.4 collective-permute-start
  86.0 5.5 %collective-permute-start.1 = (f32[80,304]{1,0:T(8,128)S(1)}, f32[80,304]{1,0:T(8,128)S(1)}, u32[]{:S(2)}, u32[]{:S(2)}) collective-permute-start(f32[80,304]{1,0:T(8,128)S(1)} %add.108), channel_id=1, source_target_pairs={{0,16},{8,24},{16,0},{24,8},{32,48},{40,56},{48,32},{56,40},{64,80... | collective-permute-start | bytes 291848 | tf_op jit(solution)/shard_map/ppermute | solution.py:447
  91.5 6.5 %collective-permute-start.2 = (f32[80,304]{1,0:T(8,128)S(1)}, f32[80,304]{1,0:T(8,128)S(1)}, u32[]{:S(2)}, u32[]{:S(2)}) collective-permute-start(f32[80,304]{1,0:T(8,128)S(1)} %add.109), channel_id=1, source_target_pairs={{0,32},{8,40},{16,48},{24,56},{32,0},{40,8},{48,16},{56,24},{64,96... | collective-permute-start | bytes 291848 | tf_op jit(solution)/shard_map/ppermute | solution.py:447
  98.0 6.5 %collective-permute-start.3 = (f32[80,304]{1,0:T(8,128)S(1)}, f32[80,304]{1,0:T(8,128)S(1)}, u32[]{:S(2)}, u32[]{:S(2)}) collective-permute-start(f32[80,304]{1,0:T(8,128)S(1)} %add.110), channel_id=1, source_target_pairs={{0,64},{8,72},{16,80},{24,88},{32,96},{40,104},{48,112},{56,120},{... | collective-permute-start | bytes 291848 | tf_op jit(solution)/shard_map/ppermute | solution.py:447
  110.6 22.7 %copy-start.11 = (bf16[320,640]{1,0:T(8,128)(2,1)S(1)}, bf16[320,640]{1,0:T(8,128)(2,1)}, u32[]{:S(2)}) copy-start(bf16[320,640]{1,0:T(8,128)(2,1)} %constant.125.clone.c1) | copy-start | bytes 1228804
  110.6 22.7 %copy-start.12 = (bf16[320,640]{1,0:T(8,128)(2,1)S(1)}, bf16[320,640]{1,0:T(8,128)(2,1)}, u32[]{:S(2)}) copy-start(bf16[320,640]{1,0:T(8,128)(2,1)} %constant.126.clone.c1l) | copy-start | bytes 1228804
  110.6 22.7 %copy-start.13 = (bf16[320,640]{1,0:T(8,128)(2,1)S(1)}, bf16[320,640]{1,0:T(8,128)(2,1)}, u32[]{:S(2)}) copy-start(bf16[320,640]{1,0:T(8,128)(2,1)} %constant.129.clone.s1) | copy-start | bytes 1228804
  110.6 22.7 %copy-start.15 = (bf16[320,640]{1,0:T(8,128)(2,1)S(1)}, bf16[320,640]{1,0:T(8,128)(2,1)}, u32[]{:S(2)}) copy-start(bf16[320,640]{1,0:T(8,128)(2,1)} %constant.130.clone.s1l) | copy-start | bytes 1228804
  110.6 22.7 %all-to-all-start = ((f32[8,328,128]{2,1,0:T(8,128)}), f32[8,328,128]{2,1,0:T(8,128)S(1)}, u32[]{:S(2)}, u32[]{:S(2)}) async-start(f32[8,328,128]{2,1,0:T(8,128)} %pad_maximum_fusion), calls=%async_computation | async-start | bytes 2686976 | tf_op jit(solution)/shard_map/all_to_all | solution.py:452
  141.1 19.7 %copy-start.21 = (f32[4,32,640]{2,1,0:T(8,128)}, f32[4,32,640]{2,1,0:T(8,128)S(1)}, u32[]{:S(2)}) copy-start(f32[4,32,640]{2,1,0:T(8,128)S(1)} %get-tuple-element.15.kept) | copy-start | bytes 983044
  141.1 10.1 %all-to-all-start.1 = ((f32[8,40,128]{2,1,0:T(8,128)}), f32[8,40,128]{2,1,0:T(8,128)S(1)}, u32[]{:S(2)}, u32[]{:S(2)}) async-start(f32[8,40,128]{2,1,0:T(8,128)} %get-tuple-element.14), calls=%async_computation.1 | async-start | bytes 327680 | tf_op jit(solution)/shard_map/all_to_all | solution.py:452
  162.0 1.4 collective-permute-start.4
  164.1 5.5 %collective-permute-start.5 = (f32[80,304]{1,0:T(8,128)S(1)}, f32[80,304]{1,0:T(8,128)S(1)}, u32[]{:S(2)}, u32[]{:S(2)}) collective-permute-start(f32[80,304]{1,0:T(8,128)S(1)} %fusion.30), channel_id=1, source_target_pairs={{0,16},{8,24},{16,0},{24,8},{32,48},{40,56},{48,32},{56,40},{64,80... | collective-permute-start | bytes 291848 | tf_op jit(solution)/shard_map/ppermute | solution.py:447
  169.6 6.5 %collective-permute-start.6 = (f32[80,304]{1,0:T(8,128)S(1)}, f32[80,304]{1,0:T(8,128)S(1)}, u32[]{:S(2)}, u32[]{:S(2)}) collective-permute-start(f32[80,304]{1,0:T(8,128)S(1)} %add.113), channel_id=1, source_target_pairs={{0,32},{8,40},{16,48},{24,56},{32,0},{40,8},{48,16},{56,24},{64,96... | collective-permute-start | bytes 291848 | tf_op jit(solution)/shard_map/ppermute | solution.py:447
  176.0 6.5 %collective-permute-start.7 = (f32[80,304]{1,0:T(8,128)S(1)}, f32[80,304]{1,0:T(8,128)S(1)}, u32[]{:S(2)}, u32[]{:S(2)}) collective-permute-start(f32[80,304]{1,0:T(8,128)S(1)} %add.114), channel_id=1, source_target_pairs={{0,64},{8,72},{16,80},{24,88},{32,96},{40,104},{48,112},{56,120},{... | collective-permute-start | bytes 291848 | tf_op jit(solution)/shard_map/ppermute | solution.py:447
  217.9 1.2 collective-permute-start.8
  219.0 3.6 %collective-permute-start.9 = (f32[8,128]{1,0:T(8,128)S(1)}, f32[8,128]{1,0:T(8,128)S(1)}, u32[]{:S(2)}, u32[]{:S(2)}) collective-permute-start(f32[8,128]{1,0:T(8,128)S(1)} %add.118), channel_id=1, source_target_pairs={{0,16},{8,24},{16,0},{24,8},{32,48},{40,56},{48,32},{56,40},{64,80... | collective-permute-start | bytes 12296 | tf_op jit(solution)/shard_map/ppermute | solution.py:447
  222.7 14.8 %collective-permute-start.10 = (f32[8,128]{1,0:T(8,128)S(1)}, f32[8,128]{1,0:T(8,128)S(1)}, u32[]{:S(2)}, u32[]{:S(2)}) collective-permute-start(f32[8,128]{1,0:T(8,128)S(1)} %add.119), channel_id=1, source_target_pairs={{0,32},{8,40},{16,48},{24,56},{32,0},{40,8},{48,16},{56,24},{64,96... | collective-permute-start | bytes 12296 | tf_op jit(solution)/shard_map/ppermute | solution.py:447
  237.5 16.5 %collective-permute-start.11 = (f32[8,128]{1,0:T(8,128)S(1)}, f32[8,128]{1,0:T(8,128)S(1)}, u32[]{:S(2)}, u32[]{:S(2)}) collective-permute-start(f32[8,128]{1,0:T(8,128)S(1)} %add.120), channel_id=1, source_target_pairs={{0,64},{8,72},{16,80},{24,88},{32,96},{40,104},{48,112},{56,120},{... | collective-permute-start | bytes 12296 | tf_op jit(solution)/shard_map/ppermute | solution.py:447
  255.0 14.4 %all-to-all-start.3 = ((f32[8,168,128]{2,1,0:T(8,128)}), f32[8,168,128]{2,1,0:T(8,128)S(1)}, u32[]{:S(2)}, u32[]{:S(2)}) async-start(f32[8,168,128]{2,1,0:T(8,128)} %broadcast_in_dim.87), calls=%async_computation.3 | async-start | bytes 1376256 | tf_op jit(solution)/shard_map/all_to_all | solution.py:452
  (21 other events, 83.9 us)

commit v2 on v1

--- a/solution.py
+++ b/solution.py
@@ -86,37 +86,43 @@
 
 
 def tile_hits(tile_row, width):
-    ids = lax.broadcasted_iota(jnp.int32, (TILES, width), 0).astype(F32).astype(BF)
-    return jnp.where(ids == tile_row.astype(BF), jnp.ones((), BF), jnp.zeros((), BF))
-
-
-WIDTH = 512
-PER_STEP = 2
-
-
-def moments_kernel(points, orders, field, w_first, w_second, total):
+    ids = lax.broadcasted_iota(jnp.int32, (TILES, width), 0).astype(F32)
+    return jnp.where(ids == tile_row, 1.0, 0.0).astype(BF)
+
+
+WIDTH = 1024
+UNROLL = 2
+
+
+def moments_kernel(high_r, low_r, weight_r, value_r, c_far_r, s_far_r, tile_r, orders, field, w_first, w_second, total):
     total[...] = jnp.zeros_like(total)
-    order = jnp.broadcast_to(orders[:, 0:1], (SLOTS, WIDTH))
-
-    def step(i, carry):
-        add = None
-        for part in range(PER_STEP):
-            data = points[:, pl.ds(pl.multiple_of((i * PER_STEP + part) * WIDTH, WIDTH), WIDTH)]
-            high, low, weight, value = data[0:1], data[1:2], data[2:3], data[3:4]
-            c_far, s_far = data[4:5], data[5:6]
-            c, s = turn_trig(order, high, low)
+    order = orders[...]
+
+    def make(first):
+        parts = []
+        for j in range(WIDTH // LANES):
+            at = pl.ds(pl.multiple_of(first + j * LANES, LANES), LANES)
+            c, s = turn_trig(order, high_r[:, at], low_r[:, at])
+            weight, value = weight_r[:, at], value_r[:, at]
+            c_far, s_far = c_far_r[:, at], s_far_r[:, at]
             wc, ws = weight * c, weight * s
             rows = jnp.concatenate(
                 [value * c, value * s, wc, ws, wc * c_far - ws * s_far, ws * c_far + wc * s_far], 0
             )
-            rows_high, rows_low = split(rows)
-            hits = tile_hits(data[6:7], WIDTH)
-            got = dot(jnp.concatenate([rows_high, rows_low], 0), hits, NT)
+            parts.append(split(rows) + (tile_hits(tile_r[:, at], LANES),))
+        high, low, hits = [jnp.concatenate(x, 1) for x in zip(*parts)]
+        return jnp.concatenate([high, low], 0), hits
+
+    def step(i, carry):
+        add = None
+        for part in range(UNROLL):
+            rows, hits = make((i * UNROLL + part) * WIDTH)
+            got = dot(rows, hits, NT)
             add = got if add is None else add + got
         total[...] += add
         return carry
 
-    lax.fori_loop(0, points.shape[1] // (WIDTH * PER_STEP), step, 0)
+    lax.fori_loop(0, high_r.shape[1] // (WIDTH * UNROLL), step, 0)
     whole = total[0 : 6 * SLOTS] + total[6 * SLOTS : 12 * SLOTS]
     field[...] = whole[0 : 2 * SLOTS]
     blank = jnp.zeros((LANES - 2 * SLOTS, TILES), F32)
@@ -125,7 +131,7 @@
 
 
 def moments(points, orders):
-    n = points.shape[1]
+    n = points[0].shape[1]
     return pl.pallas_call(
         moments_kernel,
         out_shape=[
@@ -133,12 +139,12 @@
             jax.ShapeDtypeStruct((TILES, LANES), F32),
             jax.ShapeDtypeStruct((TILES, LANES), F32),
         ],
-        in_specs=vmem(2),
+        in_specs=vmem(8),
         out_specs=vmem(3),
         scratch_shapes=[pltpu.VMEM((12 * SLOTS, TILES), F32)],
-        compiler_params=params(40),
+        compiler_params=params(12),
         cost_estimate=cost(2 * 12 * SLOTS * TILES * n, 32 * n),
-    )(points, orders)
+    )(*points, orders)
 
 
 def table_kernel(orders, cosine, sectoral, scale, p_high, p_low, left, right):
@@ -168,7 +174,7 @@
 
     empty = jnp.zeros((SLOTS, TILES), F32)
     unset = start * 0.0
-    lax.fori_loop(0, DEGREES, step, (unset, unset, order_sq * 0.0))
+    lax.fori_loop(0, DEG_PAD, step, (unset, unset, order_sq * 0.0), unroll=4)
     for n in range(DEGREES, DEG_PAD):
         put(n, empty)
 
@@ -190,7 +196,7 @@
         in_specs=vmem(3) + [SMEM],
         out_specs=vmem(2),
         scratch_shapes=[pltpu.VMEM((SLOTS * DEG_PAD, LANES), F32)] * 2,
-        compiler_params=params(48),
+        compiler_params=params(16),
         cost_estimate=cost(20 * SLOTS * DEG_PAD * TILES, 4 * SLOTS * DEG_PAD * TILES),
     )(orders, cosine, sectoral, scale)
 
@@ -214,57 +220,126 @@
     lax.fori_loop(0, SLOTS // 8, group, 0)
 
 
-def fold_kernel(vector, p_high, p_low, out, rows):
+EXTRA_FIRST = TILES + 2 * OWN_TILES
+
+
+def all_sum(x):
+    return jnp.sum(jnp.sum(x, axis=1, keepdims=True), axis=0, keepdims=True)
+
+
+def extra_rows(order_row, sums):
+    rows = [order_row] + [jnp.broadcast_to(x, (1, LANES)) for x in sums]
+    return jnp.concatenate(rows + [jnp.zeros((8 - len(rows), LANES), F32)], 0)
+
+
+def source_sum(got, row):
+    total = got[0, row : row + 1, 0:1]
+    for g in range(1, GROUPS):
+        total = total + got[g, row : row + 1, 0:1]
+    return total
+
+
+def fold_into(vector, p_high, p_low, rows):
     def put(at, value):
         rows[pl.ds(at, 8), :] = value[0:8]
         rows[pl.ds(at + SLOTS, 8), :] = value[8:16]
 
     rows[2 * SLOTS :, :] = jnp.zeros((LANES - 2 * SLOTS, TILES), F32)
     by_slot(vector, p_high, p_low, TILES, NN, put)
-    out[...] = rows[...].T
-
-
-def fold(vector, p_high, p_low):
-    return pl.pallas_call(
-        fold_kernel,
-        out_shape=jax.ShapeDtypeStruct((TILES, LANES), F32),
-        in_specs=vmem(3),
+    return rows[...].T
+
+
+def fold_first_kernel(vector, p_high, p_low, prior, order_row, w_first, w_second, sent, rows):
+    folded = fold_into(vector, p_high, p_low, rows)
+    v = vector[...]
+    extra = extra_rows(order_row[...], [all_sum(v * v), all_sum(prior[...] * v * v)])
+    t = OWN_TILES
+    for g in range(GROUPS):
+        sent[g, 0:TILES, :] = folded
+        sent[g, TILES : TILES + t, :] = w_first[g * t : (g + 1) * t, :]
+        sent[g, TILES + t : TILES + 2 * t, :] = w_second[g * t : (g + 1) * t, :]
+        sent[g, EXTRA_FIRST : EXTRA_FIRST + 8, :] = extra
+
+
+def fold_first(vector, p_high, p_low, prior, order_row, w_first, w_second):
+    return pl.pallas_call(
+        fold_first_kernel,
+        out_shape=jax.ShapeDtypeStruct((GROUPS, EXTRA_FIRST + 8, LANES), F32),
+        in_specs=vmem(7),
         out_specs=pl.BlockSpec(memory_space=pltpu.VMEM),
         scratch_shapes=[pltpu.VMEM((LANES, TILES), F32)],
-        compiler_params=params(32),
+        compiler_params=params(8),
         cost_estimate=cost(64 * SLOTS * DEG_PAD * TILES, 4 * SLOTS * DEG_PAD * TILES),
-    )(vector, p_high, p_low)
-
-
-def unfold_kernel(flip, field, p_high, p_low, out, rows):
-    factor = INV * INV if flip else INV
-    if flip:
-        rows[...] = field[...].T
-        source = rows
-    else:
-        source = field
-
+    )(vector, p_high, p_low, prior, order_row, w_first, w_second)
+
+
+def fold_second_kernel(vector, applied, got, p_high, p_low, prior, order_row, sent, next_vector, step, rows):
+    v = vector[...]
+    lane = lax.broadcasted_iota(jnp.int32, v.shape, 1)
+    norm = source_sum(got, EXTRA_FIRST + 1)
+    weighed = source_sum(got, EXTRA_FIRST + 2)
+    alpha = norm / (applied[0:1, DEGREES : DEGREES + 1] * (INV * INV) + weighed)
+    r = v - alpha * jnp.where(lane < DEGREES, applied[...] + prior[...] * v, 0.0)
+    next_vector[...] = r
+    step[...] = jnp.concatenate(
+        [jnp.broadcast_to(x, (1, LANES)) for x in (alpha, norm, weighed)] + [jnp.zeros((5, LANES), F32)], 0
+    )
+    folded = fold_into(next_vector, p_high, p_low, rows)
+    extra = extra_rows(
+        order_row[...], [all_sum(r * r), all_sum(prior[...] * v * r), all_sum(prior[...] * r * r)]
+    )
+    for g in range(GROUPS):
+        sent[g, 0:TILES, :] = folded
+        sent[g, TILES : TILES + 8, :] = extra
+
+
+def fold_second(vector, applied, got, p_high, p_low, prior, order_row):
+    return pl.pallas_call(
+        fold_second_kernel,
+        out_shape=[
+            jax.ShapeDtypeStruct((GROUPS, TILES + 8, LANES), F32),
+            jax.ShapeDtypeStruct((2 * SLOTS, DEG_PAD), F32),
+            jax.ShapeDtypeStruct((8, LANES), F32),
+        ],
+        in_specs=vmem(7),
+        out_specs=vmem(3),
+        scratch_shapes=[pltpu.VMEM((LANES, TILES), F32)],
+        compiler_params=params(8),
+        cost_estimate=cost(64 * SLOTS * DEG_PAD * TILES, 4 * SLOTS * DEG_PAD * TILES),
+    )(vector, applied, got, p_high, p_low, prior, order_row)
+
+
+def unfold_first_kernel(field, p_high, p_low, out):
     def put(at, value):
-        out[pl.ds(at, 8), :] = value[0:8] * factor
-        out[pl.ds(at + SLOTS, 8), :] = value[8:16] * factor
-
-    by_slot(source, p_high, p_low, DEG_PAD, NT, put)
-
-
-def unfold(field, p_high, p_low, flip):
-    return pl.pallas_call(
-        lambda *refs: unfold_kernel(flip, *refs),
+        out[pl.ds(at, 8), :] = value[0:8] * INV
+        out[pl.ds(at + SLOTS, 8), :] = value[8:16] * INV
+
+    by_slot(field, p_high, p_low, DEG_PAD, NT, put)
+
+
+def unfold_second_kernel(seen, p_high, p_low, out, rows):
+    t = OWN_TILES
+    rows[...] = jnp.concatenate([seen[g, 0:t, :] for g in range(GROUPS)], 0).T
+    energy = source_sum(seen, t)
+    lane = lax.broadcasted_iota(jnp.int32, (8, DEG_PAD), 1)
+
+    def put(at, value):
+        out[pl.ds(at, 8), :] = jnp.where(lane == DEGREES, energy, value[0:8] * (INV * INV))
+        out[pl.ds(at + SLOTS, 8), :] = value[8:16] * (INV * INV)
+
+    by_slot(rows, p_high, p_low, DEG_PAD, NT, put)
+
+
+def unfold(field, p_high, p_low, second):
+    return pl.pallas_call(
+        unfold_second_kernel if second else unfold_first_kernel,
         out_shape=jax.ShapeDtypeStruct((2 * SLOTS, DEG_PAD), F32),
         in_specs=vmem(3),
         out_specs=pl.BlockSpec(memory_space=pltpu.VMEM),
-        scratch_shapes=[pltpu.VMEM((LANES, TILES), F32)],
-        compiler_params=params(32),
+        scratch_shapes=[pltpu.VMEM((LANES, TILES), F32)] if second else [],
+        compiler_params=params(8),
         cost_estimate=cost(64 * SLOTS * DEG_PAD * TILES, 4 * SLOTS * DEG_PAD * TILES),
     )(field, p_high, p_low)
-
-
-F_ROWS = TILES
-EXTRA_FIRST = TILES + 2 * OWN_TILES
 
 
 def slot_hits(order_row):
@@ -309,7 +384,7 @@
     even, odd = even[:t], odd[:t]
     h_even = 2.0 * (w_even * even + w_odd * odd)
     h_odd = 2.0 * (w_even * odd + w_odd * even)
-    energy = jnp.sum(jnp.sum(h_even * even + h_odd * odd, axis=1, keepdims=True), axis=0, keepdims=True)
+    energy = all_sum(h_even * even + h_odd * odd)
     kept[0] = even
     kept[1] = odd
     kept[2] = w_even
@@ -337,39 +412,40 @@
         ],
         in_specs=[SMEM] + vmem(9),
         out_specs=vmem(2),
-        compiler_params=params(32),
+        compiler_params=params(8),
         cost_estimate=cost(10**9, 5 * 10**6),
     )(me, got, *waves)
 
 
-def grid_second_kernel(me, ratio, got, kept, c1, c1l, s1, s1l, out):
+def grid_second_kernel(me, step, got, kept, c1, c1l, s1, s1l, out):
     mine = pl.multiple_of(me[0] * OWN_TILES, OWN_TILES)
     t = OWN_TILES
     hits = [slot_hits(got[g, TILES : TILES + 1, :]) for g in range(GROUPS)]
     nat = to_natural([[got[g, pl.ds(mine, t), :]] for g in range(GROUPS)], hits)
-    even = mm3(nat[0:t], c1[...], c1l[...], NN) + ratio[0] * kept[0]
-    odd = mm3(nat[t:], s1[...], s1l[...], NN) + ratio[0] * kept[1]
+    ratio = source_sum(got, TILES + 1) / step[1:2, 0:1]
+    even = mm3(nat[0:t], c1[...], c1l[...], NN) + ratio * kept[0]
+    odd = mm3(nat[t:], s1[...], s1l[...], NN) + ratio * kept[1]
     w_even, w_odd = kept[2], kept[3]
     terms = 2.0 * w_even * (even * even + odd * odd) + 4.0 * w_odd * (even * odd)
-    energy = jnp.sum(jnp.sum(terms, axis=1, keepdims=True), axis=0, keepdims=True)
+    energy = all_sum(terms)
     out[...] = jnp.broadcast_to(energy, (8, LANES))
 
 
-def grid_second(me, ratio, got, kept, waves):
+def grid_second(me, step, got, kept, waves):
     return pl.pallas_call(
         grid_second_kernel,
         out_shape=jax.ShapeDtypeStruct((8, LANES), F32),
-        in_specs=[SMEM, SMEM] + vmem(6),
+        in_specs=[SMEM] + vmem(7),
         out_specs=pl.BlockSpec(memory_space=pltpu.VMEM),
-        compiler_params=params(32),
+        compiler_params=params(8),
         cost_estimate=cost(10**9, 5 * 10**6),
-    )(me, ratio, got, kept, *waves)
+    )(me, step, got, kept, *waves)
 
 
 S_WIDTH = 512
 
 
-def values_kernel(extra_row, me, points, got, out, z_high, z_low, picked):
+def lookup_kernel(extra_row, got, z_high, z_low):
     hits = jnp.concatenate(
         [slot_hits(got[g, extra_row : extra_row + 1, :]) for g in range(GROUPS)], 1
     )
@@ -378,15 +454,29 @@
         high, low = split(jnp.concatenate([h[c] for h in halves], 1))
         z_high[pl.ds(c * ORDERS, ORDERS), :] = dot(hits, high, NT).astype(BF)
         z_low[pl.ds(c * ORDERS, ORDERS), :] = dot(hits, low, NT).astype(BF)
-    own = out.shape[0] * S_WIDTH
-    first = me[0] * own
+
+
+def lookup(got, extra_row):
+    shape = jax.ShapeDtypeStruct((2 * ORDERS, TILES), BF)
+    return pl.pallas_call(
+        lambda *refs: lookup_kernel(extra_row, *refs),
+        out_shape=[shape, shape],
+        in_specs=vmem(1),
+        out_specs=vmem(2),
+        compiler_params=params(10),
+        cost_estimate=cost(10**9, 3 * 10**6),
+    )(got)
+
+
+def values_kernel(start, me, high_r, low_r, tile_r, z_high, z_low, out):
+    first = me[0] * (high_r.shape[1] // GROUPS) + start * S_WIDTH
     near_order = lax.broadcasted_iota(jnp.int32, (8, S_WIDTH), 0).astype(F32)
 
     def step(i, carry):
-        data = points[:, pl.ds(pl.multiple_of(first + i * S_WIDTH, S_WIDTH), S_WIDTH)]
-        hits_here = tile_hits(data[6:7], S_WIDTH)
-        picked[...] = dot(z_high[...], hits_here, NN) + dot(z_low[...], hits_here, NN)
-        high, low = data[0:1], data[1:2]
+        at = pl.ds(pl.multiple_of(first + i * S_WIDTH, S_WIDTH), S_WIDTH)
+        hits_here = tile_hits(tile_r[:, at], S_WIDTH)
+        picked = dot(z_high[...], hits_here, NN) + dot(z_low[...], hits_here, NN)
+        high, low = high_r[:, at], low_r[:, at]
         c, s = turn_trig(near_order, high, low)
         c8, s8 = turn_trig(8.0, high, low)
         c8 = jnp.broadcast_to(c8, c.shape)
@@ -402,21 +492,47 @@
     lax.fori_loop(0, out.shape[0], step, 0)
 
 
-def point_values(me, points, got, extra_row):
-    own = points.shape[1] // GROUPS
-    return pl.pallas_call(
-        lambda *refs: values_kernel(extra_row, *refs),
-        out_shape=jax.ShapeDtypeStruct((own // S_WIDTH, S_WIDTH), F32),
-        in_specs=[SMEM] + vmem(2),
+def point_values(me, points, tables, start, rows):
+    high, low, tile = points
+    return pl.pallas_call(
+        lambda *refs: values_kernel(start, *refs),
+        out_shape=jax.ShapeDtypeStruct((rows, S_WIDTH), F32),
+        in_specs=[SMEM] + vmem(5),
         out_specs=pl.BlockSpec(memory_space=pltpu.VMEM),
-        scratch_shapes=[
-            pltpu.VMEM((2 * ORDERS, TILES), BF),
-            pltpu.VMEM((2 * ORDERS, TILES), BF),
-            pltpu.VMEM((2 * ORDERS, S_WIDTH), F32),
+        compiler_params=params(10),
+        cost_estimate=cost(8 * ORDERS * TILES * rows * S_WIDTH, 10**6),
+    )(me, high, low, tile, *tables)
+
+
+def final_kernel(last, step, got, vector, next_vector, observed, fitted, coefficients):
+    rows = fitted.shape[1]
+    alpha, norm, prior_00 = step[0:1, 0:1], step[1:2, 0:1], step[2:3, 0:1]
+    norm_1 = source_sum(got, TILES + 1)
+    prior_01 = source_sum(got, TILES + 2)
+    prior_11 = source_sum(got, TILES + 3)
+    energy = source_sum(last, 2 * rows)
+    ratio = norm_1 / norm
+    curvature = energy * (INV * INV) + prior_11 + 2.0 * ratio * prior_01 + ratio * ratio * prior_00
+    beta = norm_1 / curvature
+    on_first = alpha + beta * ratio
+    coefficients[...] = on_first * vector[...] + beta * next_vector[...]
+    on_first, beta = on_first * INV, beta * INV
+    for g in range(GROUPS):
+        fitted[g] = observed[g] - (on_first * last[g, 0:rows, :] + beta * last[g, rows : 2 * rows, :])
+
+
+def final(last, step, got, vector, next_vector, observed):
+    return pl.pallas_call(
+        final_kernel,
+        out_shape=[
+            jax.ShapeDtypeStruct(observed.shape, F32),
+            jax.ShapeDtypeStruct(vector.shape, F32),
         ],
-        compiler_params=params(40),
-        cost_estimate=cost(8 * ORDERS * TILES * own, 5 * 10**6),
-    )(me, points, got)
+        in_specs=vmem(6),
+        out_specs=vmem(2),
+        compiler_params=params(8),
+        cost_estimate=cost(10**7, 3 * 10**6),
+    )(last, step, got, vector, next_vector, observed)
 
 
 def waves():
@@ -442,10 +558,20 @@
     return jnp.exp(log_lead + orders * jnp.log(sines))
 
 
-def pts_total(x):
-    for d in (1, 2, 4, 8):
-        x = x + lax.ppermute(x, "pts", [(i, i ^ d) for i in range(16)])
-    return x
+def pts_total(x, beside=()):
+    made = []
+    for k, d in enumerate((1, 2, 4, 8)):
+        task = beside[k] if k < len(beside) else None
+        gate = jnp.zeros((1,), jnp.int32)
+        if task is not None:
+            x, gate = lax.optimization_barrier((x, gate))
+        other = lax.ppermute(x, "pts", [(i, i ^ d) for i in range(16)])
+        if task is not None:
+            out = task(gate)
+            other, out = lax.optimization_barrier((other, out))
+            made.append(out)
+        x = x + other
+    return x, made
 
 
 def swap(x):
@@ -470,91 +596,53 @@
     low = ((longitude - high * turn_high) - high * turn_low) * (1.0 / turn)
     far = high * ORDERS
     far = ((far - jnp.round(far)) + low * ORDERS) * turn
-    points = jnp.stack(
-        [high, low, obs_weight, obs_weight * observations, jnp.cos(far), jnp.sin(far), local_tile, local_tile]
-    )
+    weighted = obs_weight * observations
+    points = [x[None] for x in (high, low, obs_weight, weighted, jnp.cos(far), jnp.sin(far), local_tile)]
+    near = points[0], points[1], points[6]
 
     field, w_first, w_second = moments(points, orders)
     p_high, p_low = legendre_table(orders, cosine, sectoral, scale)
     prior_row = jnp.pad(prior, (0, DEG_PAD - DEGREES))[None, :]
-
-    residual = pts_total(unfold(field, p_high, p_low, False))
-    fourier = fold(residual, p_high, p_low)
-
     order_row = jnp.concatenate([order, order, jnp.full((LANES - 2 * SLOTS,), -1.0, F32)])[None]
-
-    def extras(*scalars):
-        rows = [order_row] + [jnp.full((1, LANES), s, F32) for s in scalars]
-        return jnp.concatenate(rows + [jnp.zeros((8 - len(rows), LANES), F32)], 0)
-
-    def everywhere(x):
-        return jnp.broadcast_to(x[None], (GROUPS,) + x.shape)
-
-    def by_tiles(x):
-        return x.reshape(GROUPS, OWN_TILES, LANES)
-
-    sent = jnp.concatenate(
+    own_rows = high.shape[0] // (GROUPS * S_WIDTH)
+    half = own_rows // 2
+
+    residual, _ = pts_total(unfold(field, p_high, p_low, False))
+    got = swap(fold_first(residual, p_high, p_low, prior_row, order_row, w_first, w_second))
+
+    back, kept = grid_first(me, got, (c1, c1l, c2, c2l, s1, s1l, s2, s2l))
+    tables_0 = lookup(got, EXTRA_FIRST)
+    back, me_0 = lax.optimization_barrier((back, me))
+    seen = swap(back)
+    values_00 = point_values(me_0, near, tables_0, 0, half)
+    seen, values_00 = lax.optimization_barrier((seen, values_00))
+    applied, (values_01,) = pts_total(
+        unfold(seen, p_high, p_low, True),
+        [None, None, lambda gate: point_values(me + gate, near, tables_0, half, own_rows - half)],
+    )
+    sent_1, residual_1, step = fold_second(residual, applied, got, p_high, p_low, prior_row, order_row)
+    got_1 = swap(sent_1)
+    part = grid_second(me, step, got_1, kept, (c1, c1l, s1, s1l))
+    tables_1 = lookup(got_1, TILES)
+    third = own_rows // 3
+    energy_1, values_1 = pts_total(
+        part,
         [
-            everywhere(fourier),
-            by_tiles(w_first),
-            by_tiles(w_second),
-            everywhere(extras(jnp.sum(residual * residual), jnp.sum(prior_row * residual * residual))),
+            None,
+            lambda gate: point_values(me + gate, near, tables_1, 0, third),
+            lambda gate: point_values(me + gate, near, tables_1, third, third),
+            lambda gate: point_values(me + gate, near, tables_1, 2 * third, own_rows - 2 * third),
         ],
-        1,
-    )
-    got = swap(sent)
-    sums = jnp.sum(got[:, EXTRA_FIRST : EXTRA_FIRST + 8, 0], 0)
-    norm_0, prior_00 = sums[1], sums[2]
-
-    back, kept = grid_first(me, got, (c1, c1l, c2, c2l, s1, s1l, s2, s2l))
-    seen = swap(back)
-    energy_part = jnp.sum(seen[:, OWN_TILES, 0])
-    applied = unfold(seen[:, :OWN_TILES].reshape(TILES, LANES), p_high, p_low, True)
-    lane = lax.broadcasted_iota(jnp.int32, applied.shape, 1)
-    values_0 = point_values(me, points, got, EXTRA_FIRST)
-    applied = pts_total(jnp.where(lane == DEGREES, energy_part, applied))
-    step_0 = norm_0 / (applied[0, DEGREES] * (INV * INV) + prior_00)
-    applied = jnp.where(lane < DEGREES, applied + prior_row * residual, 0.0)
-    residual_1 = residual - step_0 * applied
-
-    fourier_1 = fold(residual_1, p_high, p_low)
-    got_1 = swap(
-        everywhere(
-            jnp.concatenate(
-                [
-                    fourier_1,
-                    extras(
-                        jnp.sum(residual_1 * residual_1),
-                        jnp.sum(prior_row * residual * residual_1),
-                        jnp.sum(prior_row * residual_1 * residual_1),
-                    ),
-                ],
-                0,
-            )
-        )
-    )
-    sums = jnp.sum(got_1[:, TILES : TILES + 8, 0], 0)
-    norm_1, prior_01, prior_11 = sums[1], sums[2], sums[3]
-    ratio = norm_1 / norm_0
-    energy_1 = pts_total(grid_second(me, ratio.reshape(1), got_1, kept, (c1, c1l, s1, s1l)))
-    values_1 = point_values(me, points, got_1, TILES)
-
-    own_rows = values_0.size // LANES
-    last = swap(
-        everywhere(
-            jnp.concatenate(
-                [values_0.reshape(own_rows, LANES), values_1.reshape(own_rows, LANES), energy_1], 0
-            )
-        )
-    )
-    energy_1 = jnp.sum(last[:, 2 * own_rows, 0])
-    curvature = energy_1 * (INV * INV) + prior_11 + 2.0 * ratio * prior_01 + ratio * ratio * prior_00
-    step_1 = norm_1 / curvature
-    on_0 = step_0 + step_1 * ratio
-    vector = on_0 * residual + step_1 * residual_1
-    fitted = on_0 * last[:, :own_rows] + step_1 * last[:, own_rows : 2 * own_rows]
+    )
+    payload = jnp.concatenate(
+        [x.reshape(-1, LANES) for x in [values_00, values_01] + values_1] + [energy_1], 0
+    )
+    last = swap(jnp.broadcast_to(payload[None], (GROUPS,) + payload.shape))
+    residual_out, vector = final(
+        last, step, got_1, residual, residual_1, observations.reshape(GROUPS, -1, LANES)
+    )
     coefficients = vector.reshape(2, SLOTS, DEG_PAD)[:, :, :DEGREES].transpose(2, 0, 1)
-    return coefficients, observations - fitted.reshape(-1) * INV
+    return coefficients, residual_out.reshape(-1)
 
 
 def solution(mesh):

time: 275 us -> 223 us (0.81)
  local copies, waits for them, and re-layouts: 38.7 us -> 18.4 us
  Pallas kernels: 104 us -> 93 us
  other arithmetic: 11.9 us -> 4.11 us
  between operations: 7.25 us -> 1.15 us
  blocking collectives: 16.1 us -> 12.5 us
    unnamed x60 -> x85, local copies, waits for them, and re-layouts: 25.4 us -> 17.5 us
    pallas_call x1, Pallas kernels: 45.3 us -> 38 us  [moments(): pl.pallas_call(moments_kernel, out_shape=[jax.ShapeDtypeStruct((2 * SLOTS...]
    pallas_call x1, Pallas kernels: 17.1 us -> 10.5 us  [legendre_table(): pl.pallas_call(table_kernel, out_shape=[shape, shape], in_specs=vmem(3) +...]
    another operation x1 -> x0, local copies, waits for them, and re-layouts: 6.45 us -> none  [shards(): jnp.stack([high, low, obs_weight, obs_weight * observations, jnp.cos(far)...]
    all_to_all x1, blocking collectives: 16.1 us -> 12.5 us  [swap(): return lax.all_to_all(x, 'coef', 0, 0)]
    pallas_call x6 -> x12, Pallas kernels: 36.9 us -> 40.5 us  [the longest x5 22 us: point_values(): pl.pallas_call(lambda *refs: values_kernel(start, *refs), out_shape=jax.S...]
    reduce_sum x6 -> x0, other arithmetic: 2.8 us -> none  [the longest x1 0.67 us: shards(): jnp.sum(prior_row * residual_1 * residual_1)]
  transfers between devices with their start and end apart: 15 -> 15, of which waited for: 13 -> 12; matrix products, arithmetic and copies ran while one was open for 0% -> 0% of each run, Pallas kernels for 9% -> 7%
where the time goes in v2:
time: 223 us; the launch traced here: 222 us
  Pallas kernels  93 us (42%)
  waiting for transfers between devices  56 us (25%)
  starting transfers between devices  37.3 us (17%)
  local copies, waits for them, and re-layouts  18.4 us (8%)
  blocking collectives  12.5 us (6%)
  other arithmetic  4.11 us (2%)
    pallas_call x1, Pallas kernels, moments(): pl.pallas_call(moments_kernel, out_shape=[jax.ShapeDtypeStruct((2 * SLOTS...  38 us
    all_to_all x3, waiting for transfers between devices, swap(): return lax.all_to_all(x, 'coef', 0, 0)  30.3 us
    ppermute x12, waiting for transfers between devices, pts_total(): other = lax.ppermute(x, 'pts', [(i, i ^ d) for i in range(16)])  25.7 us
    pallas_call x5, Pallas kernels, point_values(): pl.pallas_call(lambda *refs: values_kernel(start, *refs), out_shape=jax.S...  22 us
    ppermute x12, starting transfers between devices, pts_total(): other = lax.ppermute(x, 'pts', [(i, i ^ d) for i in range(16)])  21.8 us
    unnamed x85, local copies, waits for them, and re-layouts  17.5 us
    all_to_all x3, starting transfers between devices, swap(): return lax.all_to_all(x, 'coef', 0, 0)  15.5 us
    all_to_all x1, blocking collectives, swap(): return lax.all_to_all(x, 'coef', 0, 0)  12.5 us
  transfers between devices with their start and end apart: 15, of which 12 were waited for; matrix products, arithmetic and copies ran while one was open for 0% of the time, Pallas kernels for 7%

profile of v2, /device:TPU:0, one launch (start us, length us, event | category | flops | bytes accessed | tf_op | source)
XLA Modules:
  0.0 222.4 jit_solution(13719663932252731966)
XLA Ops:
  4.8 10.5 %shard_map.168 = (bf16[40,304,256]{2,1,0:T(8,128)(2,1)S(1)}, bf16[40,304,256]{2,1,0:T(8,128)(2,1)S(1)}) custom-call(f32[40,128]{1,0:T(8,128)S(1)} %broadcast_in_dim.54.orders, f32[1,256]{1,0:T(1,128)S(1)} %bitcast.42, f32[40,256]{1,0:T(8,128)S(1)} %add_exponential_fusion.sectoral, f32[304]{0:T(512)S(1)} %copy-done.26), custom_call_target="tpu_custom_call" | custom-call | flops 62259200 | bytes 12451840 | tf_op jit(solution)/shard_map/pallas_call | solution.py:193
  15.3 38.0 %shard_map.167 = (f32[80,256]{1,0:T(8,128)S(1)}, f32[256,128]{1,0:T(8,128)S(1)}, f32[256,128]{1,0:T(8,128)S(1)}) custom-call(f32[1,81920]{1,0:T(1,128)S(1)} %bitcast.32, f32[1,81920]{1,0:T(1,128)S(1)} %bitcast.26, f32[1,81920]{1,0:T(1,128)S(1)} %bitcast.25, f32[1,81920]{1,0:T(1,128)S(1)} %bitcast.40, f32[1,81920]{1,0:T(1,128)S(1)} %bitcast.39, ...), custom_call_target="tpu_custom_call" | custom-call | flops 20132659200 | bytes 2621440 | tf_op jit(solution)/shard_map/pallas_call | solution.py:135
  53.3 3.9 %shard_map.169 = f32[80,304]{1,0:T(8,128)S(1)} custom-call(f32[80,256]{1,0:T(8,128)S(1)} %get-tuple-element.38.field, bf16[40,304,256]{2,1,0:T(8,128)(2,1)S(1)} %get-tuple-element.39.p_high, bf16[40,304,256]{2,1,0:T(8,128)(2,1)S(1)} %get-tuple-element.40.p_low), custom_call_target="tpu_custom_call" | custom-call | flops 199229440 | bytes 12451840 | tf_op jit(solution)/shard_map/pallas_call | solution.py:334
  60.2 3.8 %collective-permute-done.1 = f32[80,304]{1,0:T(8,128)S(1)} collective-permute-done((f32[80,304]{1,0:T(8,128)S(1)}, f32[80,304]{1,0:T(8,128)S(1)}, u32[]{:S(2)}, u32[]{:S(2)}) %collective-permute-start.1) | collective-permute-done | bytes 97312 | tf_op jit(solution)/shard_map/ppermute | solution.py:568
  64.1 3.2 %collective-permute-start.2 = (f32[80,304]{1,0:T(8,128)S(1)}, f32[80,304]{1,0:T(8,128)S(1)}, u32[]{:S(2)}, u32[]{:S(2)}) collective-permute-start(f32[80,304]{1,0:T(8,128)S(1)} %add.97), channel_id=1, source_target_pairs={{0,32},{8,40},{16,48},{24,56},{32,0},{40,8},{48,16},{56,24},{64,96... | collective-permute-start | bytes 291848 | tf_op jit(solution)/shard_map/ppermute | solution.py:568
  67.2 3.3 %collective-permute-done.2 = f32[80,304]{1,0:T(8,128)S(1)} collective-permute-done((f32[80,304]{1,0:T(8,128)S(1)}, f32[80,304]{1,0:T(8,128)S(1)}, u32[]{:S(2)}, u32[]{:S(2)}) %collective-permute-start.2) | collective-permute-done | bytes 97312 | tf_op jit(solution)/shard_map/ppermute | solution.py:568
  70.5 3.4 %collective-permute-start.3 = (f32[80,304]{1,0:T(8,128)S(1)}, f32[80,304]{1,0:T(8,128)S(1)}, u32[]{:S(2)}, u32[]{:S(2)}) collective-permute-start(f32[80,304]{1,0:T(8,128)S(1)} %add.98), channel_id=1, source_target_pairs={{0,64},{8,72},{16,80},{24,88},{32,96},{40,104},{48,112},{56,120},{... | collective-permute-start | bytes 291848 | tf_op jit(solution)/shard_map/ppermute | solution.py:568
  77.0 3.9 %shard_map.170 = f32[8,328,128]{2,1,0:T(8,128)} custom-call(f32[80,304]{1,0:T(8,128)S(1)} %add.99.vector, bf16[40,304,256]{2,1,0:T(8,128)(2,1)S(1)} %get-tuple-element.39.p_high, bf16[40,304,256]{2,1,0:T(8,128)(2,1)S(1)} %get-tuple-element.40.p_low, f32[1,304]{1,0:T(1,128)S(1)} %broadcast_in_dim.56.prior, f32[1,128]{1,0:T(1,128)S(1)} %maximum_bitcast_fusion.order_row, ...), custom_call_target="tpu_custom_call" | custom-call | flops 199229440 | bytes 12451840 | tf_op jit(solution)/shard_map/pallas_call | solution.py:265
  80.9 6.5 %all-to-all-start = ((f32[8,328,128]{2,1,0:T(8,128)}), f32[8,328,128]{2,1,0:T(8,128)S(1)}, u32[]{:S(2)}, u32[]{:S(2)}) async-start(f32[8,328,128]{2,1,0:T(8,128)} %shard_map.170), calls=%async_computation | async-start | bytes 2686976 | tf_op jit(solution)/shard_map/all_to_all | solution.py:578
  87.5 16.1 %all-to-all-done.got.refs_0_ = f32[8,328,128]{2,1,0:T(8,128)S(1)} async-done(((f32[8,328,128]{2,1,0:T(8,128)}), f32[8,328,128]{2,1,0:T(8,128)S(1)}, u32[]{:S(2)}, u32[]{:S(2)}) %all-to-all-start) | async-done | bytes 1343520 | tf_op jit(solution)/shard_map/all_to_all | solution.py:578
  113.1 3.4 %all-to-all-start.1 = ((f32[8,40,128]{2,1,0:T(8,128)}), f32[8,40,128]{2,1,0:T(8,128)S(1)}, u32[]{:S(2)}, u32[]{:S(2)}) async-start(f32[8,40,128]{2,1,0:T(8,128)} %copy-done.23), calls=%async_computation.1 | async-start | bytes 327680 | tf_op jit(solution)/shard_map/all_to_all | solution.py:578
  117.5 5.5 %shard_map.173 = f32[10,512]{1,0:T(8,128)S(1)} custom-call(s32[1]{0:T(128)} %bitcast.me.refs_0_, f32[1,81920]{1,0:T(1,128)S(1)} %bitcast.33, f32[1,81920]{1,0:T(1,128)S(1)} %bitcast.27, f32[1,81920]{1,0:T(1,128)S(1)} %bitcast.20, bf16[640,256]{1,0:T(8,128)(2,1)S(1)} %get-tuple-element.46.refs_4_, bf16[640,256]{1,0:T(8,128)(2,1)S(1)} %get-tuple-element.47.refs_5_), custom_call_target="tpu_custom_call" | custom-call | flops 3355443200 | bytes 1000000 | tf_op jit(solution)/shard_map/pallas_call | solution.py:497
  130.0 4.0 %shard_map.174 = f32[80,304]{1,0:T(8,128)S(1)} custom-call(f32[8,40,128]{2,1,0:T(8,128)S(1)} %all-to-all-done.1.seen, bf16[40,304,256]{2,1,0:T(8,128)(2,1)S(1)} %copy-done.1, bf16[40,304,256]{2,1,0:T(8,128)(2,1)S(1)} %copy-done.3), custom_call_target="tpu_custom_call" | custom-call | flops 199229440 | bytes 12451840 | tf_op jit(solution)/shard_map/pallas_call | solution.py:334
  137.0 3.9 %collective-permute-done.5 = f32[80,304]{1,0:T(8,128)S(1)} collective-permute-done((f32[80,304]{1,0:T(8,128)S(1)}, f32[80,304]{1,0:T(8,128)S(1)}, u32[]{:S(2)}, u32[]{:S(2)}) %collective-permute-start.5) | collective-permute-done | bytes 97312 | tf_op jit(solution)/shard_map/ppermute | solution.py:568
  140.9 3.1 %collective-permute-start.6 = (f32[80,304]{1,0:T(8,128)S(1)}, f32[80,304]{1,0:T(8,128)S(1)}, u32[]{:S(2)}, u32[]{:S(2)}) collective-permute-start(f32[80,304]{1,0:T(8,128)S(1)} %add.101), channel_id=1, source_target_pairs={{0,32},{8,40},{16,48},{24,56},{32,0},{40,8},{48,16},{56,24},{64,96... | collective-permute-start | bytes 291848 | tf_op jit(solution)/shard_map/ppermute | solution.py:568
  144.0 5.5 %shard_map.175 = f32[10,512]{1,0:T(8,128)S(1)} custom-call(s32[1]{0:T(128)S(6)} %add.102.refs_0_, f32[1,81920]{1,0:T(1,128)S(1)} %bitcast.34, f32[1,81920]{1,0:T(1,128)S(1)} %bitcast.28, f32[1,81920]{1,0:T(1,128)S(1)} %bitcast.21, bf16[640,256]{1,0:T(8,128)(2,1)S(1)} %copy-done.28, bf16[640,256]{1,0:T(8,128)(2,1)S(1)} %copy-done.30), custom_call_target="tpu_custom_call" | custom-call | flops 3355443200 | bytes 1000000 | tf_op jit(solution)/shard_map/pallas_call | solution.py:497
  152.5 3.5 %collective-permute-done.7 = f32[80,304]{1,0:T(8,128)S(1)} collective-permute-done((f32[80,304]{1,0:T(8,128)S(1)}, f32[80,304]{1,0:T(8,128)S(1)}, u32[]{:S(2)}, u32[]{:S(2)}) %collective-permute-start.7) | collective-permute-done | bytes 97312 | tf_op jit(solution)/shard_map/ppermute | solution.py:568
  156.1 4.1 %shard_map.176 = (f32[8,264,128]{2,1,0:T(8,128)}, f32[80,304]{1,0:T(8,128)S(1)}, f32[8,128]{1,0:T(8,128)S(1)}) custom-call(f32[80,304]{1,0:T(8,128)S(1)} %add.99.vector, f32[80,304]{1,0:T(8,128)S(1)} %add.104.applied, f32[8,328,128]{2,1,0:T(8,128)S(1)} %all-to-all-done.got.refs_0_, bf16[40,304,256]{2,1,0:T(8,128)(2,1)S(1)} %bitcast.17, ...), custom_call_target="tpu_custom_call" | custom-call | flops 199229440 | bytes 12451840 | tf_op jit(solution)/shard_map/pallas_call | solution.py:297
  160.1 5.6 %all-to-all-start.2 = ((f32[8,264,128]{2,1,0:T(8,128)}), f32[8,264,128]{2,1,0:T(8,128)S(1)}, u32[]{:S(2)}, u32[]{:S(2)}) async-start(f32[8,264,128]{2,1,0:T(8,128)} %get-tuple-element.55), calls=%async_computation.2 | async-start | bytes 2162688 | tf_op jit(solution)/shard_map/all_to_all | solution.py:578
  165.8 14.1 %all-to-all-done.2.got.refs_0_ = f32[8,264,128]{2,1,0:T(8,128)S(1)} async-done(((f32[8,264,128]{2,1,0:T(8,128)}), f32[8,264,128]{2,1,0:T(8,128)S(1)}, u32[]{:S(2)}, u32[]{:S(2)}) %all-to-all-start.2) | async-done | bytes 1081376 | tf_op jit(solution)/shard_map/all_to_all | solution.py:578
  185.0 3.3 %shard_map.179 = f32[6,512]{1,0:T(8,128)S(1)} custom-call(s32[1]{0:T(128)S(6)} %add.106.refs_0_, f32[1,81920]{1,0:T(1,128)S(1)} %bitcast.35, f32[1,81920]{1,0:T(1,128)S(1)} %bitcast.29, f32[1,81920]{1,0:T(1,128)S(1)} %bitcast.22, bf16[640,256]{1,0:T(8,128)(2,1)S(1)} %get-tuple-element.59.refs_4_, bf16[640,256]{1,0:T(8,128)(2,1)S(1)} %get-tuple-element.60.refs_5_), custom_call_target="tpu_custom_call" | custom-call | flops 2013265920 | bytes 1000000 | tf_op jit(solution)/shard_map/pallas_call | solution.py:497
  188.3 3.3 %shard_map.180 = f32[6,512]{1,0:T(8,128)S(1)} custom-call(s32[1]{0:T(128)S(6)} %add.108.refs_0_, f32[1,81920]{1,0:T(1,128)S(1)} %bitcast.36, f32[1,81920]{1,0:T(1,128)S(1)} %bitcast.30, f32[1,81920]{1,0:T(1,128)S(1)} %bitcast.23, bf16[640,256]{1,0:T(8,128)(2,1)S(1)} %get-tuple-element.59.refs_4_, bf16[640,256]{1,0:T(8,128)(2,1)S(1)} %get-tuple-element.60.refs_5_), custom_call_target="tpu_custom_call" | custom-call | flops 2013265920 | bytes 1000000 | tf_op jit(solution)/shard_map/pallas_call | solution.py:497
  198.8 4.4 %shard_map.181 = f32[8,512]{1,0:T(8,128)S(1)} custom-call(s32[1]{0:T(128)S(6)} %add.110.refs_0_, f32[1,81920]{1,0:T(1,128)S(1)} %bitcast.37, f32[1,81920]{1,0:T(1,128)S(1)} %bitcast.31, f32[1,81920]{1,0:T(1,128)S(1)} %bitcast.24, bf16[640,256]{1,0:T(8,128)(2,1)S(1)} %copy-done.32, bf16[640,256]{1,0:T(8,128)(2,1)S(1)} %copy-done.34), custom_call_target="tpu_custom_call" | custom-call | flops 2684354560 | bytes 1000000 | tf_op jit(solution)/shard_map/pallas_call | solution.py:497
  208.4 12.5 %all_to_all.20.last = f32[8,168,128]{2,1,0:T(8,128)S(1)} all-to-all(f32[8,168,128]{2,1,0:T(8,128)S(1)} %broadcast_in_dim.59), channel_id=1, replica_groups=mesh['pts'=16,'coef'=8] {'coef'}, dimensions={0} | all-to-all | bytes 1376256 | tf_op jit(solution)/shard_map/all_to_all | solution.py:578
  (140 shorter events, 52.5 us)
Async XLA Ops:
  4.4 48.9 %copy-start.15 = (f32[81920]{0:T(1024)}, f32[81920]{0:T(1024)S(1)}, u32[]{:S(2)}) copy-start(f32[81920]{0:T(1024)S(1)} %get-tuple-element.76) | copy-start | bytes 983044
  4.4 48.9 %copy-start.19 = (f32[81920]{0:T(1024)}, f32[81920]{0:T(1024)S(1)}, u32[]{:S(2)}) copy-start(f32[81920]{0:T(1024)S(1)} %get-tuple-element.77) | copy-start | bytes 983044
  15.3 61.7 %copy-start = (bf16[40,304,256]{2,1,0:T(8,128)(2,1)}, bf16[40,304,256]{2,1,0:T(8,128)(2,1)S(1)}, u32[]{:S(2)}) copy-start(bf16[40,304,256]{2,1,0:T(8,128)(2,1)S(1)} %get-tuple-element.39.p_high) | copy-start | bytes 18677764
  15.3 61.7 %copy-start.2 = (bf16[40,304,256]{2,1,0:T(8,128)(2,1)}, bf16[40,304,256]{2,1,0:T(8,128)(2,1)S(1)}, u32[]{:S(2)}) copy-start(bf16[40,304,256]{2,1,0:T(8,128)(2,1)S(1)} %get-tuple-element.40.p_low) | copy-start | bytes 18677764
  57.2 1.4 collective-permute-start
  58.6 5.5 %collective-permute-start.1 = (f32[80,304]{1,0:T(8,128)S(1)}, f32[80,304]{1,0:T(8,128)S(1)}, u32[]{:S(2)}, u32[]{:S(2)}) collective-permute-start(f32[80,304]{1,0:T(8,128)S(1)} %add.96), channel_id=1, source_target_pairs={{0,16},{8,24},{16,0},{24,8},{32,48},{40,56},{48,32},{56,40},{64,80... | collective-permute-start | bytes 291848 | tf_op jit(solution)/shard_map/ppermute | solution.py:568
  64.1 6.5 %collective-permute-start.2 = (f32[80,304]{1,0:T(8,128)S(1)}, f32[80,304]{1,0:T(8,128)S(1)}, u32[]{:S(2)}, u32[]{:S(2)}) collective-permute-start(f32[80,304]{1,0:T(8,128)S(1)} %add.97), channel_id=1, source_target_pairs={{0,32},{8,40},{16,48},{24,56},{32,0},{40,8},{48,16},{56,24},{64,96... | collective-permute-start | bytes 291848 | tf_op jit(solution)/shard_map/ppermute | solution.py:568
  70.5 6.5 %collective-permute-start.3 = (f32[80,304]{1,0:T(8,128)S(1)}, f32[80,304]{1,0:T(8,128)S(1)}, u32[]{:S(2)}, u32[]{:S(2)}) collective-permute-start(f32[80,304]{1,0:T(8,128)S(1)} %add.98), channel_id=1, source_target_pairs={{0,64},{8,72},{16,80},{24,88},{32,96},{40,104},{48,112},{56,120},{... | collective-permute-start | bytes 291848 | tf_op jit(solution)/shard_map/ppermute | solution.py:568
  80.9 22.7 %copy-start.5 = (bf16[320,640]{1,0:T(8,128)(2,1)S(1)}, bf16[320,640]{1,0:T(8,128)(2,1)}, u32[]{:S(2)}) copy-start(bf16[320,640]{1,0:T(8,128)(2,1)} %constant.115.clone.c1) | copy-start | bytes 1228804
  80.9 22.7 %copy-start.6 = (bf16[320,640]{1,0:T(8,128)(2,1)S(1)}, bf16[320,640]{1,0:T(8,128)(2,1)}, u32[]{:S(2)}) copy-start(bf16[320,640]{1,0:T(8,128)(2,1)} %constant.116.clone.c1l) | copy-start | bytes 1228804
  80.9 22.7 %copy-start.7 = (bf16[320,640]{1,0:T(8,128)(2,1)S(1)}, bf16[320,640]{1,0:T(8,128)(2,1)}, u32[]{:S(2)}) copy-start(bf16[320,640]{1,0:T(8,128)(2,1)} %constant.119.clone.s1) | copy-start | bytes 1228804
  80.9 22.7 %all-to-all-start = ((f32[8,328,128]{2,1,0:T(8,128)}), f32[8,328,128]{2,1,0:T(8,128)S(1)}, u32[]{:S(2)}, u32[]{:S(2)}) async-start(f32[8,328,128]{2,1,0:T(8,128)} %shard_map.170), calls=%async_computation | async-start | bytes 2686976 | tf_op jit(solution)/shard_map/all_to_all | solution.py:578
  113.1 11.4 %all-to-all-start.1 = ((f32[8,40,128]{2,1,0:T(8,128)}), f32[8,40,128]{2,1,0:T(8,128)S(1)}, u32[]{:S(2)}, u32[]{:S(2)}) async-start(f32[8,40,128]{2,1,0:T(8,128)} %copy-done.23), calls=%async_computation.1 | async-start | bytes 327680 | tf_op jit(solution)/shard_map/all_to_all | solution.py:578
  134.0 1.4 collective-permute-start.4
  135.4 5.5 %collective-permute-start.5 = (f32[80,304]{1,0:T(8,128)S(1)}, f32[80,304]{1,0:T(8,128)S(1)}, u32[]{:S(2)}, u32[]{:S(2)}) collective-permute-start(f32[80,304]{1,0:T(8,128)S(1)} %add.100), channel_id=1, source_target_pairs={{0,16},{8,24},{16,0},{24,8},{32,48},{40,56},{48,32},{56,40},{64,80... | collective-permute-start | bytes 291848 | tf_op jit(solution)/shard_map/ppermute | solution.py:568
  140.9 15.2 %slice-start = ((s8[6225920]{0:T(1024)(128)(4,1)}), s8[4194304]{0:T(1024)(128)(4,1)S(1)}, s32[]{:S(2)}) async-start(s8[6225920]{0:T(1024)(128)(4,1)} %bitcast.16), calls=%async_computation.4 | async-start | bytes 8388608
  140.9 15.2 %slice-start.1 = ((s8[6225920]{0:T(1024)(128)(4,1)}), s8[2031616]{0:T(1024)(128)(4,1)S(1)}, s32[]{:S(2)}) async-start(s8[6225920]{0:T(1024)(128)(4,1)} %bitcast.16), calls=%async_computation.5 | async-start | bytes 4063232
  140.9 8.6 %collective-permute-start.6 = (f32[80,304]{1,0:T(8,128)S(1)}, f32[80,304]{1,0:T(8,128)S(1)}, u32[]{:S(2)}, u32[]{:S(2)}) collective-permute-start(f32[80,304]{1,0:T(8,128)S(1)} %add.101), channel_id=1, source_target_pairs={{0,32},{8,40},{16,48},{24,56},{32,0},{40,8},{48,16},{56,24},{64,96... | collective-permute-start | bytes 291848 | tf_op jit(solution)/shard_map/ppermute | solution.py:568
  149.5 6.5 %collective-permute-start.7 = (f32[80,304]{1,0:T(8,128)S(1)}, f32[80,304]{1,0:T(8,128)S(1)}, u32[]{:S(2)}, u32[]{:S(2)}) collective-permute-start(f32[80,304]{1,0:T(8,128)S(1)} %add.103), channel_id=1, source_target_pairs={{0,64},{8,72},{16,80},{24,88},{32,96},{40,104},{48,112},{56,120},{... | collective-permute-start | bytes 291848 | tf_op jit(solution)/shard_map/ppermute | solution.py:568
  160.1 19.8 %all-to-all-start.2 = ((f32[8,264,128]{2,1,0:T(8,128)}), f32[8,264,128]{2,1,0:T(8,128)S(1)}, u32[]{:S(2)}, u32[]{:S(2)}) async-start(f32[8,264,128]{2,1,0:T(8,128)} %get-tuple-element.55), calls=%async_computation.2 | async-start | bytes 2162688 | tf_op jit(solution)/shard_map/all_to_all | solution.py:578
  182.9 1.4 collective-permute-start.8
  184.3 3.9 %collective-permute-start.9 = (f32[8,128]{1,0:T(8,128)S(1)}, f32[8,128]{1,0:T(8,128)S(1)}, u32[]{:S(2)}, u32[]{:S(2)}) collective-permute-start(f32[8,128]{1,0:T(8,128)S(1)} %add.105), channel_id=1, source_target_pairs={{0,16},{8,24},{16,0},{24,8},{32,48},{40,56},{48,32},{56,40},{64,80... | collective-permute-start | bytes 12296 | tf_op jit(solution)/shard_map/ppermute | solution.py:568
  191.6 5.2 %collective-permute-start.10 = (f32[8,128]{1,0:T(8,128)S(1)}, f32[8,128]{1,0:T(8,128)S(1)}, u32[]{:S(2)}, u32[]{:S(2)}) collective-permute-start(f32[8,128]{1,0:T(8,128)S(1)} %add.107), channel_id=1, source_target_pairs={{0,32},{8,40},{16,48},{24,56},{32,0},{40,8},{48,16},{56,24},{64,96... | collective-permute-start | bytes 12296 | tf_op jit(solution)/shard_map/ppermute | solution.py:568
  203.2 5.2 %collective-permute-start.11 = (f32[8,128]{1,0:T(8,128)S(1)}, f32[8,128]{1,0:T(8,128)S(1)}, u32[]{:S(2)}, u32[]{:S(2)}) collective-permute-start(f32[8,128]{1,0:T(8,128)S(1)} %add.109), channel_id=1, source_target_pairs={{0,64},{8,72},{16,80},{24,88},{32,96},{40,104},{48,112},{56,120},{... | collective-permute-start | bytes 12296 | tf_op jit(solution)/shard_map/ppermute | solution.py:568
  (31 other events, 119.8 us)

commit v3 on v2

--- a/solution.py
+++ b/solution.py
@@ -91,7 +91,7 @@
 
 
 WIDTH = 1024
-UNROLL = 2
+UNROLL = 4
 
 
 def moments_kernel(high_r, low_r, weight_r, value_r, c_far_r, s_far_r, tile_r, orders, field, w_first, w_second, total):
@@ -201,26 +201,33 @@
     )(orders, cosine, sectoral, scale)
 
 
-def by_slot(vector, p_high, p_low, width, dims, put):
+def slot_group(vector, at, high_of, low_of, width, dims):
     row = lax.broadcasted_iota(jnp.int32, (16, width), 0)
-
+    rows = jnp.concatenate([vector[pl.ds(at, 8), :], vector[pl.ds(at + SLOTS, 8), :]], 0)
+    high, low = split(rows)
+    both = jnp.concatenate([high, low], 0)
+    out = jnp.zeros((16, width), F32)
+    for i in range(8):
+        first = dot(both, high_of(at + i), dims)
+        total = first[0:16] + first[16:32] + dot(high, low_of(at + i), dims)
+        out = jnp.where((row == i) | (row == i + 8), total, out)
+    return out
+
+
+def by_slot(vector, p_high, p_low, width, dims, put, ready=None):
     def group(g, carry):
         at = pl.multiple_of(g * 8, 8)
-        rows = jnp.concatenate([vector[pl.ds(at, 8), :], vector[pl.ds(at + SLOTS, 8), :]], 0)
-        high, low = split(rows)
-        both = jnp.concatenate([high, low], 0)
-        out = jnp.zeros((16, width), F32)
-        for i in range(8):
-            first = dot(both, p_high[at + i], dims)
-            total = first[0:16] + first[16:32] + dot(high, p_low[at + i], dims)
-            out = jnp.where((row == i) | (row == i + 8), total, out)
-        put(at, out)
+        if ready is not None:
+            ready(g)
+        put(at, slot_group(vector, at, lambda i: p_high[i], lambda i: p_low[i], width, dims))
         return carry
 
     lax.fori_loop(0, SLOTS // 8, group, 0)
 
 
-EXTRA_FIRST = TILES + 2 * OWN_TILES
+F_ROWS = 2 * SLOTS
+EXTRA_FIRST = F_ROWS + OWN_TILES
+EXTRA_SECOND = F_ROWS
 
 
 def all_sum(x):
@@ -229,7 +236,8 @@
 
 def extra_rows(order_row, sums):
     rows = [order_row] + [jnp.broadcast_to(x, (1, LANES)) for x in sums]
-    return jnp.concatenate(rows + [jnp.zeros((8 - len(rows), LANES), F32)], 0)
+    rows = jnp.concatenate(rows + [jnp.zeros((8 - len(rows), LANES), F32)], 0)
+    return jnp.concatenate([rows, rows], 1)
 
 
 def source_sum(got, row):
@@ -244,42 +252,52 @@
         rows[pl.ds(at, 8), :] = value[0:8]
         rows[pl.ds(at + SLOTS, 8), :] = value[8:16]
 
-    rows[2 * SLOTS :, :] = jnp.zeros((LANES - 2 * SLOTS, TILES), F32)
     by_slot(vector, p_high, p_low, TILES, NN, put)
-    return rows[...].T
-
-
-def fold_first_kernel(vector, p_high, p_low, prior, order_row, w_first, w_second, sent, rows):
+    return rows[...]
+
+
+def join(core, mine, other):
+    even = core[0] == 0
+    mine, other = mine[...], other[...]
+    return jnp.concatenate([jnp.where(even, mine, other), jnp.where(even, other, mine)], 0)
+
+
+def fold_first_kernel(core, mine, other, p_high, p_low, prior, order_row, w_first, w_second, sent, vector, rows):
+    v = join(core, mine, other)
+    vector[...] = v
     folded = fold_into(vector, p_high, p_low, rows)
-    v = vector[...]
     extra = extra_rows(order_row[...], [all_sum(v * v), all_sum(prior[...] * v * v)])
     t = OWN_TILES
     for g in range(GROUPS):
-        sent[g, 0:TILES, :] = folded
-        sent[g, TILES : TILES + t, :] = w_first[g * t : (g + 1) * t, :]
-        sent[g, TILES + t : TILES + 2 * t, :] = w_second[g * t : (g + 1) * t, :]
+        sent[g, 0:F_ROWS, :] = folded
+        sent[g, F_ROWS:EXTRA_FIRST, 0:LANES] = w_first[g * t : (g + 1) * t, :]
+        sent[g, F_ROWS:EXTRA_FIRST, LANES:TILES] = w_second[g * t : (g + 1) * t, :]
         sent[g, EXTRA_FIRST : EXTRA_FIRST + 8, :] = extra
 
 
-def fold_first(vector, p_high, p_low, prior, order_row, w_first, w_second):
+def fold_first(core, halves, p_high, p_low, prior, order_row, w_first, w_second):
     return pl.pallas_call(
         fold_first_kernel,
-        out_shape=jax.ShapeDtypeStruct((GROUPS, EXTRA_FIRST + 8, LANES), F32),
-        in_specs=vmem(7),
-        out_specs=pl.BlockSpec(memory_space=pltpu.VMEM),
-        scratch_shapes=[pltpu.VMEM((LANES, TILES), F32)],
+        out_shape=[
+            jax.ShapeDtypeStruct((GROUPS, EXTRA_FIRST + 8, TILES), F32),
+            jax.ShapeDtypeStruct((2 * SLOTS, DEG_PAD), F32),
+        ],
+        in_specs=[SMEM] + vmem(8),
+        out_specs=vmem(2),
+        scratch_shapes=[pltpu.VMEM((2 * SLOTS, TILES), F32)],
         compiler_params=params(8),
         cost_estimate=cost(64 * SLOTS * DEG_PAD * TILES, 4 * SLOTS * DEG_PAD * TILES),
-    )(vector, p_high, p_low, prior, order_row, w_first, w_second)
-
-
-def fold_second_kernel(vector, applied, got, p_high, p_low, prior, order_row, sent, next_vector, step, rows):
+    )(core, *halves, p_high, p_low, prior, order_row, w_first, w_second)
+
+
+def fold_second_kernel(core, mine, other, vector, got, p_high, p_low, prior, order_row, sent, next_vector, step, rows):
     v = vector[...]
+    applied = join(core, mine, other)
     lane = lax.broadcasted_iota(jnp.int32, v.shape, 1)
     norm = source_sum(got, EXTRA_FIRST + 1)
     weighed = source_sum(got, EXTRA_FIRST + 2)
     alpha = norm / (applied[0:1, DEGREES : DEGREES + 1] * (INV * INV) + weighed)
-    r = v - alpha * jnp.where(lane < DEGREES, applied[...] + prior[...] * v, 0.0)
+    r = v - alpha * jnp.where(lane < DEGREES, applied + prior[...] * v, 0.0)
     next_vector[...] = r
     step[...] = jnp.concatenate(
         [jnp.broadcast_to(x, (1, LANES)) for x in (alpha, norm, weighed)] + [jnp.zeros((5, LANES), F32)], 0
@@ -289,57 +307,63 @@
         order_row[...], [all_sum(r * r), all_sum(prior[...] * v * r), all_sum(prior[...] * r * r)]
     )
     for g in range(GROUPS):
-        sent[g, 0:TILES, :] = folded
-        sent[g, TILES : TILES + 8, :] = extra
-
-
-def fold_second(vector, applied, got, p_high, p_low, prior, order_row):
+        sent[g, 0:F_ROWS, :] = folded
+        sent[g, EXTRA_SECOND : EXTRA_SECOND + 8, :] = extra
+
+
+def fold_second(core, halves, vector, got, p_high, p_low, prior, order_row):
     return pl.pallas_call(
         fold_second_kernel,
         out_shape=[
-            jax.ShapeDtypeStruct((GROUPS, TILES + 8, LANES), F32),
+            jax.ShapeDtypeStruct((GROUPS, EXTRA_SECOND + 8, TILES), F32),
             jax.ShapeDtypeStruct((2 * SLOTS, DEG_PAD), F32),
             jax.ShapeDtypeStruct((8, LANES), F32),
         ],
-        in_specs=vmem(7),
+        in_specs=[SMEM] + vmem(8),
         out_specs=vmem(3),
-        scratch_shapes=[pltpu.VMEM((LANES, TILES), F32)],
+        scratch_shapes=[pltpu.VMEM((2 * SLOTS, TILES), F32)],
         compiler_params=params(8),
         cost_estimate=cost(64 * SLOTS * DEG_PAD * TILES, 4 * SLOTS * DEG_PAD * TILES),
-    )(vector, applied, got, p_high, p_low, prior, order_row)
-
-
-def unfold_first_kernel(field, p_high, p_low, out):
+    )(core, *halves, vector, got, p_high, p_low, prior, order_row)
+
+
+def put_halves(core, keep, give, at, first, second):
+    even = core[0] == 0
+    keep[pl.ds(at, 8), :] = jnp.where(even, first, second)
+    give[pl.ds(at, 8), :] = jnp.where(even, second, first)
+
+
+def unfold_first_kernel(core, field, p_high, p_low, keep, give):
     def put(at, value):
-        out[pl.ds(at, 8), :] = value[0:8] * INV
-        out[pl.ds(at + SLOTS, 8), :] = value[8:16] * INV
+        put_halves(core, keep, give, at, value[0:8] * INV, value[8:16] * INV)
 
     by_slot(field, p_high, p_low, DEG_PAD, NT, put)
 
 
-def unfold_second_kernel(seen, p_high, p_low, out, rows):
+def unfold_second_kernel(core, seen, p_high, p_low, keep, give, rows):
     t = OWN_TILES
     rows[...] = jnp.concatenate([seen[g, 0:t, :] for g in range(GROUPS)], 0).T
     energy = source_sum(seen, t)
     lane = lax.broadcasted_iota(jnp.int32, (8, DEG_PAD), 1)
 
     def put(at, value):
-        out[pl.ds(at, 8), :] = jnp.where(lane == DEGREES, energy, value[0:8] * (INV * INV))
-        out[pl.ds(at + SLOTS, 8), :] = value[8:16] * (INV * INV)
+        first = jnp.where(lane == DEGREES, energy, value[0:8] * (INV * INV))
+        put_halves(core, keep, give, at, first, value[8:16] * (INV * INV))
 
     by_slot(rows, p_high, p_low, DEG_PAD, NT, put)
 
 
-def unfold(field, p_high, p_low, second):
+def unfold(core, field, p_high, p_low, second):
+    half = jax.ShapeDtypeStruct((SLOTS, DEG_PAD), F32)
     return pl.pallas_call(
         unfold_second_kernel if second else unfold_first_kernel,
-        out_shape=jax.ShapeDtypeStruct((2 * SLOTS, DEG_PAD), F32),
-        in_specs=vmem(3),
-        out_specs=pl.BlockSpec(memory_space=pltpu.VMEM),
+        out_shape=[half, half],
+        in_specs=[SMEM] + vmem(3),
+        out_specs=vmem(2),
         scratch_shapes=[pltpu.VMEM((LANES, TILES), F32)] if second else [],
         compiler_params=params(8),
         cost_estimate=cost(64 * SLOTS * DEG_PAD * TILES, 4 * SLOTS * DEG_PAD * TILES),
-    )(field, p_high, p_low)
+    )(core, field, p_high, p_low)
 
 
 def slot_hits(order_row):
@@ -363,25 +387,46 @@
     return total[:n] + total[n:]
 
 
-def grid_first_kernel(me, got, c1, c1l, c2, c2l, s1, s1l, s2, s2l, back, kept):
-    mine = pl.multiple_of(me[0] * OWN_TILES, OWN_TILES)
+def own_tiles(me, z_high, z_low):
+    shape = (OWN_TILES, TILES)
+    wanted = lax.broadcasted_iota(jnp.int32, shape, 0) + me[0] * OWN_TILES
+    pick = jnp.where(lax.broadcasted_iota(jnp.int32, shape, 1) == wanted, 1.0, 0.0).astype(BF)
+    return [
+        dot(pick, z_high[pl.ds(c * ORDERS, ORDERS), :], NT) + dot(pick, z_low[pl.ds(c * ORDERS, ORDERS), :], NT)
+        for c in range(2)
+    ]
+
+
+def wave_parts(wave):
+    return [wave.at[pl.ds(i * ORDERS, ORDERS), :] for i in range(4)]
+
+
+def grid_first_kernel(me, got, z_high, z_low, wave, back, kept):
+    c1, c1l, s1, s1l = wave_parts(wave)
     t = OWN_TILES
-    hits = [slot_hits(got[g, EXTRA_FIRST : EXTRA_FIRST + 1, :]) for g in range(GROUPS)]
+    hits = [slot_hits(got[g, EXTRA_FIRST : EXTRA_FIRST + 1, 0:LANES]) for g in range(GROUPS)]
     nat = to_natural(
         [
-            [got[g, pl.ds(mine, t), :], got[g, TILES : TILES + t, :], got[g, TILES + t : TILES + 2 * t, :]]
+            [got[g, F_ROWS:EXTRA_FIRST, 0:LANES], got[g, F_ROWS:EXTRA_FIRST, LANES:TILES]]
             for g in range(GROUPS)
         ],
         hits,
     )
+    own_c, own_s = own_tiles(me, z_high, z_low)
     k = lax.broadcasted_iota(jnp.int32, (1, ORDERS), 1)
     k_first = jnp.where(k == 0, 1.0 / GRID, 2.0 / GRID)
     k_second = jnp.where(k + ORDERS <= 2 * (DEGREES - 1), 2.0 / GRID, 0.0)
-    even = mm3(jnp.concatenate([nat[0:t], nat[2 * t : 3 * t] * k_first], 0), c1[...], c1l[...], NN)
-    odd = mm3(jnp.concatenate([nat[t : 2 * t], nat[3 * t : 4 * t] * k_first], 0), s1[...], s1l[...], NN)
-    w_even = even[t:] + mm3(nat[4 * t : 5 * t] * k_second, c2[...], c2l[...], NN)
-    w_odd = odd[t:] + mm3(nat[5 * t : 6 * t] * k_second, s2[...], s2l[...], NN)
-    even, odd = even[:t], odd[:t]
+    near_c, near_s = nat[0:t] * k_first, nat[t : 2 * t] * k_first
+    far_c, far_s = nat[2 * t : 3 * t] * k_second, nat[3 * t :] * k_second
+    by_c = mm3(jnp.concatenate([own_c, near_c, far_c, far_s], 0), c1[...], c1l[...], NN)
+    by_s = mm3(jnp.concatenate([own_s, near_s, far_c, far_s], 0), s1[...], s1l[...], NN)
+    q = lax.broadcasted_iota(jnp.int32, (1, HALF), 1) % 4
+    root = math.sqrt(0.5)
+    turn_c = jnp.where((q == 0) | (q == 3), root, -root)
+    turn_s = jnp.where(q < 2, root, -root)
+    even, odd = by_c[:t], by_s[:t]
+    w_even = by_c[t : 2 * t] + turn_c * by_c[2 * t : 3 * t] - turn_s * by_s[2 * t : 3 * t]
+    w_odd = by_s[t : 2 * t] + turn_c * by_s[3 * t :] + turn_s * by_c[3 * t :]
     h_even = 2.0 * (w_even * even + w_odd * odd)
     h_odd = 2.0 * (w_even * odd + w_odd * even)
     energy = all_sum(h_even * even + h_odd * odd)
@@ -403,57 +448,58 @@
         back[g, t : t + 8, :] = jnp.broadcast_to(energy, (8, LANES))
 
 
-def grid_first(me, got, waves):
+def grid_first(me, got, tables, waves):
     return pl.pallas_call(
         grid_first_kernel,
         out_shape=[
             jax.ShapeDtypeStruct((GROUPS, OWN_TILES + 8, LANES), F32),
             jax.ShapeDtypeStruct((4, OWN_TILES, HALF), F32),
         ],
-        in_specs=[SMEM] + vmem(9),
+        in_specs=[SMEM] + vmem(4),
         out_specs=vmem(2),
         compiler_params=params(8),
         cost_estimate=cost(10**9, 5 * 10**6),
-    )(me, got, *waves)
-
-
-def grid_second_kernel(me, step, got, kept, c1, c1l, s1, s1l, out):
-    mine = pl.multiple_of(me[0] * OWN_TILES, OWN_TILES)
-    t = OWN_TILES
-    hits = [slot_hits(got[g, TILES : TILES + 1, :]) for g in range(GROUPS)]
-    nat = to_natural([[got[g, pl.ds(mine, t), :]] for g in range(GROUPS)], hits)
-    ratio = source_sum(got, TILES + 1) / step[1:2, 0:1]
-    even = mm3(nat[0:t], c1[...], c1l[...], NN) + ratio * kept[0]
-    odd = mm3(nat[t:], s1[...], s1l[...], NN) + ratio * kept[1]
+    )(me, got, *tables, waves)
+
+
+def grid_second_kernel(me, step, got, z_high, z_low, kept, wave, out):
+    c1, c1l, s1, s1l = wave_parts(wave)
+    own_c, own_s = own_tiles(me, z_high, z_low)
+    ratio = source_sum(got, EXTRA_SECOND + 1) / step[1:2, 0:1]
+    even = mm3(own_c, c1[...], c1l[...], NN) + ratio * kept[0]
+    odd = mm3(own_s, s1[...], s1l[...], NN) + ratio * kept[1]
     w_even, w_odd = kept[2], kept[3]
     terms = 2.0 * w_even * (even * even + odd * odd) + 4.0 * w_odd * (even * odd)
     energy = all_sum(terms)
     out[...] = jnp.broadcast_to(energy, (8, LANES))
 
 
-def grid_second(me, step, got, kept, waves):
+def grid_second(me, step, got, tables, kept, waves):
     return pl.pallas_call(
         grid_second_kernel,
         out_shape=jax.ShapeDtypeStruct((8, LANES), F32),
-        in_specs=[SMEM] + vmem(7),
+        in_specs=[SMEM] + vmem(6),
         out_specs=pl.BlockSpec(memory_space=pltpu.VMEM),
         compiler_params=params(8),
         cost_estimate=cost(10**9, 5 * 10**6),
-    )(me, step, got, kept, *waves)
+    )(me, step, got, *tables, kept, waves)
 
 
 S_WIDTH = 512
 
 
 def lookup_kernel(extra_row, got, z_high, z_low):
-    hits = jnp.concatenate(
-        [slot_hits(got[g, extra_row : extra_row + 1, :]) for g in range(GROUPS)], 1
-    )
-    halves = [two_halves(got[g, 0:TILES, :]) for g in range(GROUPS)]
+    lane = lax.broadcasted_iota(jnp.int32, (1, LANES), 1)
+    blank = jnp.zeros((LANES - F_ROWS, TILES), F32)
+    high, low = split(
+        jnp.concatenate([x for g in range(GROUPS) for x in (got[g, 0:F_ROWS, :], blank)], 0)
+    )
+    order_rows = [got[g, extra_row : extra_row + 1, 0:LANES] for g in range(GROUPS)]
     for c in range(2):
-        high, low = split(jnp.concatenate([h[c] for h in halves], 1))
-        z_high[pl.ds(c * ORDERS, ORDERS), :] = dot(hits, high, NT).astype(BF)
-        z_low[pl.ds(c * ORDERS, ORDERS), :] = dot(hits, low, NT).astype(BF)
+        ours = (lane >= c * SLOTS) & (lane < (c + 1) * SLOTS)
+        hits = jnp.concatenate([slot_hits(jnp.where(ours, row, -1.0)) for row in order_rows], 1)
+        z_high[pl.ds(c * ORDERS, ORDERS), :] = dot(hits, high, NN).astype(BF)
+        z_low[pl.ds(c * ORDERS, ORDERS), :] = dot(hits, low, NN).astype(BF)
 
 
 def lookup(got, extra_row):
@@ -468,8 +514,8 @@
     )(got)
 
 
-def values_kernel(start, me, high_r, low_r, tile_r, z_high, z_low, out):
-    first = me[0] * (high_r.shape[1] // GROUPS) + start * S_WIDTH
+def values_kernel(start, me, gate, high_r, low_r, tile_r, z_high, z_low, out):
+    first = (me[0] + gate[0]) * (high_r.shape[1] // GROUPS) + start * S_WIDTH
     near_order = lax.broadcasted_iota(jnp.int32, (8, S_WIDTH), 0).astype(F32)
 
     def step(i, carry):
@@ -486,30 +532,32 @@
             add = c * picked[8 * b : 8 * b + 8, :] + s * picked[ORDERS + 8 * b : ORDERS + 8 * b + 8, :]
             total = add if total is None else total + add
             c, s = c * c8 - s * s8, s * c8 + c * s8
-        out[pl.ds(i, 1), :] = jnp.sum(total, axis=0, keepdims=True)
+        row = jnp.sum(total, axis=0, keepdims=True)
+        for j in range(S_WIDTH // LANES):
+            out[pl.ds(i * (S_WIDTH // LANES) + j, 1), :] = row[:, j * LANES : (j + 1) * LANES]
         return carry
 
-    lax.fori_loop(0, out.shape[0], step, 0)
-
-
-def point_values(me, points, tables, start, rows):
+    lax.fori_loop(0, out.shape[0] * LANES // S_WIDTH, step, 0)
+
+
+def point_values(me, points, tables, start, rows, gate):
     high, low, tile = points
     return pl.pallas_call(
         lambda *refs: values_kernel(start, *refs),
-        out_shape=jax.ShapeDtypeStruct((rows, S_WIDTH), F32),
-        in_specs=[SMEM] + vmem(5),
+        out_shape=jax.ShapeDtypeStruct((rows * S_WIDTH // LANES, LANES), F32),
+        in_specs=[SMEM, SMEM] + vmem(5),
         out_specs=pl.BlockSpec(memory_space=pltpu.VMEM),
         compiler_params=params(10),
         cost_estimate=cost(8 * ORDERS * TILES * rows * S_WIDTH, 10**6),
-    )(me, high, low, tile, *tables)
+    )(me, gate, high, low, tile, *tables)
 
 
 def final_kernel(last, step, got, vector, next_vector, observed, fitted, coefficients):
     rows = fitted.shape[1]
     alpha, norm, prior_00 = step[0:1, 0:1], step[1:2, 0:1], step[2:3, 0:1]
-    norm_1 = source_sum(got, TILES + 1)
-    prior_01 = source_sum(got, TILES + 2)
-    prior_11 = source_sum(got, TILES + 3)
+    norm_1 = source_sum(got, EXTRA_SECOND + 1)
+    prior_01 = source_sum(got, EXTRA_SECOND + 2)
+    prior_11 = source_sum(got, EXTRA_SECOND + 3)
     energy = source_sum(last, 2 * rows)
     ratio = norm_1 / norm
     curvature = energy * (INV * INV) + prior_11 + 2.0 * ratio * prior_01 + ratio * ratio * prior_00
@@ -536,15 +584,14 @@
 
 
 def waves():
-    k = np.arange(2 * ORDERS)[:, None]
+    k = np.arange(ORDERS)[:, None]
     q = np.arange(HALF)[None, :] * 2 + 1
     phase = 2 * np.pi * ((k * q) % (2 * GRID)) / (2 * GRID)
     out = []
     for f in (np.cos(phase), np.sin(phase)):
         high = f.astype(jnp.bfloat16)
-        low = (f - high.astype(np.float64)).astype(jnp.bfloat16)
-        out += [high[:ORDERS], low[:ORDERS], high[ORDERS:], low[ORDERS:]]
-    return out
+        out += [high, (f - high.astype(np.float64)).astype(jnp.bfloat16)]
+    return np.concatenate(out, 0)
 
 
 def sectoral_values(orders, sines):
@@ -558,20 +605,35 @@
     return jnp.exp(log_lead + orders * jnp.log(sines))
 
 
-def pts_total(x, beside=()):
+def exchange(x, d):
+    return lax.ppermute(x, "pts", [(i, i ^ d) for i in range(16)])
+
+
+def gated(x, move, task):
+    if task is None:
+        return move(x), None
+    x, gate = lax.optimization_barrier((x, jnp.zeros((1,), jnp.int32)))
+    return lax.optimization_barrier((move(x), task(gate)))
+
+
+def halves_total(keep, give, tasks=(None, None)):
+    x = keep + exchange(give, 1)
+    (x, across, near, both), first = gated(
+        x, lambda v: (v, exchange(v, 4), exchange(v, 2), exchange(v, 6)), tasks[0]
+    )
+    x = (x + across) + (near + both)
+    (x, far), second = gated(x, lambda v: (v, exchange(v, 8)), tasks[1])
+    x = x + far
+    return (x, exchange(x, 1)), [first, second]
+
+
+def pts_total(x, tasks):
     made = []
-    for k, d in enumerate((1, 2, 4, 8)):
-        task = beside[k] if k < len(beside) else None
-        gate = jnp.zeros((1,), jnp.int32)
-        if task is not None:
-            x, gate = lax.optimization_barrier((x, gate))
-        other = lax.ppermute(x, "pts", [(i, i ^ d) for i in range(16)])
-        if task is not None:
-            out = task(gate)
-            other, out = lax.optimization_barrier((other, out))
-            made.append(out)
+    for d, task in zip((1, 2, 4, 8), tasks):
+        (x, other), out = gated(x, lambda v: (v, exchange(v, d)), task)
         x = x + other
-    return x, made
+        made.append(out)
+    return x, [m for m in made if m is not None]
 
 
 def swap(x):
@@ -580,14 +642,19 @@
 
 def shards(colatitude, longitude, tile_of_point, order_of_slot, observations, obs_weight, prior):
     me = lax.axis_index("coef").astype(jnp.int32).reshape(1)
-    local_tile = (tile_of_point - lax.axis_index("pts") * TILES).astype(F32)
+    place = lax.axis_index("pts").astype(jnp.int32)
+    core = (place & 1).reshape(1)
+    me, core, place, order_of_slot, longitude, tile_of_point = lax.optimization_barrier(
+        (me, core, place * TILES, order_of_slot, longitude, tile_of_point)
+    )
+    local_tile = (tile_of_point - place).astype(F32)
     order = order_of_slot.astype(F32)
     orders = jnp.broadcast_to(order[:, None], (SLOTS, LANES))
     cosine = jnp.cos(colatitude)[None, :]
     sectoral = sectoral_values(order[:, None], jnp.sin(colatitude)[None, :])
     degree = np.arange(DEG_PAD, dtype=np.float64)
     scale = jnp.asarray((1.0 / (4 * degree * degree - 1)).astype(np.float32))
-    c1, c1l, c2, c2l, s1, s1l, s2, s2l = [jnp.asarray(x) for x in waves()]
+    wave = jnp.asarray(waves())
 
     turn = 2.0 * math.pi
     turn_high = 6.28125
@@ -607,35 +674,41 @@
     own_rows = high.shape[0] // (GROUPS * S_WIDTH)
     half = own_rows // 2
 
-    residual, _ = pts_total(unfold(field, p_high, p_low, False))
-    got = swap(fold_first(residual, p_high, p_low, prior_row, order_row, w_first, w_second))
-
-    back, kept = grid_first(me, got, (c1, c1l, c2, c2l, s1, s1l, s2, s2l))
+    halves, _ = halves_total(*unfold(core, field, p_high, p_low, False))
+    sent, residual = fold_first(core, halves, p_high, p_low, prior_row, order_row, w_first, w_second)
+    sent, me, core = lax.optimization_barrier((sent, me, core))
+    got, me, core = lax.optimization_barrier((swap(sent), me, core))
+
     tables_0 = lookup(got, EXTRA_FIRST)
-    back, me_0 = lax.optimization_barrier((back, me))
-    seen = swap(back)
-    values_00 = point_values(me_0, near, tables_0, 0, half)
-    seen, values_00 = lax.optimization_barrier((seen, values_00))
-    applied, (values_01,) = pts_total(
-        unfold(seen, p_high, p_low, True),
-        [None, None, lambda gate: point_values(me + gate, near, tables_0, half, own_rows - half)],
-    )
-    sent_1, residual_1, step = fold_second(residual, applied, got, p_high, p_low, prior_row, order_row)
-    got_1 = swap(sent_1)
-    part = grid_second(me, step, got_1, kept, (c1, c1l, s1, s1l))
-    tables_1 = lookup(got_1, TILES)
-    third = own_rows // 3
+    back, kept = grid_first(me, got, tables_0, wave)
+    held = (me, core, tables_0, kept, near)
+    back, held = lax.optimization_barrier((back, held))
+    seen, (me, core, tables_0, kept, near) = lax.optimization_barrier((swap(back), held))
+    halves, values_0 = halves_total(
+        *unfold(core, seen, p_high, p_low, True),
+        [
+            lambda gate: point_values(me, near, tables_0, 0, half, gate),
+            lambda gate: point_values(me, near, tables_0, half, own_rows - half, gate),
+        ],
+    )
+    sent_1, residual_1, step = fold_second(core, halves, residual, got, p_high, p_low, prior_row, order_row)
+    held = (me, values_0, kept, near, residual, residual_1, step)
+    sent_1, held = lax.optimization_barrier((sent_1, held))
+    got_1, held = lax.optimization_barrier((swap(sent_1), held))
+    me, values_0, kept, near, residual, residual_1, step = held
+    tables_1 = lookup(got_1, EXTRA_SECOND)
+    part = grid_second(me, step, got_1, tables_1, kept, wave)
     energy_1, values_1 = pts_total(
         part,
         [
             None,
-            lambda gate: point_values(me + gate, near, tables_1, 0, third),
-            lambda gate: point_values(me + gate, near, tables_1, third, third),
-            lambda gate: point_values(me + gate, near, tables_1, 2 * third, own_rows - 2 * third),
+            lambda gate: point_values(me, near, tables_1, 0, half, gate),
+            lambda gate: point_values(me, near, tables_1, half, own_rows - half, gate),
+            None,
         ],
     )
     payload = jnp.concatenate(
-        [x.reshape(-1, LANES) for x in [values_00, values_01] + values_1] + [energy_1], 0
+        values_0 + values_1 + [energy_1], 0
     )
     last = swap(jnp.broadcast_to(payload[None], (GROUPS,) + payload.shape))
     residual_out, vector = final(

time: 223 us -> 194 us (0.87)
  blocking collectives: 12.5 us -> 58.4 us
  waiting for transfers between devices: 56 us -> 19.1 us
  starting transfers between devices: 37.3 us -> 20.4 us
  local copies, waits for them, and re-layouts: 18.4 us -> 3.19 us
  Pallas kernels: 93 us -> 85.8 us
    all_to_all x1 -> x4, blocking collectives: 12.5 us -> 58.4 us  [swap(): return lax.all_to_all(x, 'coef', 0, 0)]
    all_to_all x3 -> x0, waiting for transfers between devices: 30.3 us -> none  [swap(): return lax.all_to_all(x, 'coef', 0, 0)]
    unnamed x85 -> x14, local copies, waits for them, and re-layouts: 17.5 us -> 1.68 us
    all_to_all x3 -> x0, starting transfers between devices: 15.5 us -> none  [swap(): return lax.all_to_all(x, 'coef', 0, 0)]
    ppermute x12 -> x16, waiting for transfers between devices: 25.7 us -> 19.1 us  [exchange(): return lax.ppermute(x, 'pts', [(i, i ^ d) for i in range(16)])]
    pallas_call x1, Pallas kernels: 38 us -> 34.2 us  [moments(): pl.pallas_call(moments_kernel, out_shape=[jax.ShapeDtypeStruct((2 * SLOTS...]
    ppermute x12 -> x16, starting transfers between devices: 21.8 us -> 20.4 us  [exchange(): return lax.ppermute(x, 'pts', [(i, i ^ d) for i in range(16)])]
    pallas_call x5 -> x4, Pallas kernels: 22 us -> 21.8 us  [point_values(): pl.pallas_call(lambda *refs: values_kernel(start, *refs), out_shape=jax.S...]
  transfers between devices with their start and end apart: 15 -> 16, of which waited for: 12 -> 11; matrix products, arithmetic and copies ran while one was open for 0% -> 0% of each run, Pallas kernels for 7% -> 8%
where the time goes in v3:
time: 194 us
  Pallas kernels  85.8 us (44%)
  blocking collectives  58.4 us (30%)
  starting transfers between devices  20.4 us (11%)
  waiting for transfers between devices  19.1 us (10%)
  other arithmetic  6.01 us (3%)
  local copies, waits for them, and re-layouts  3.19 us (2%)
    all_to_all x4, blocking collectives, swap(): return lax.all_to_all(x, 'coef', 0, 0)  58.4 us
    pallas_call x1, Pallas kernels, moments(): pl.pallas_call(moments_kernel, out_shape=[jax.ShapeDtypeStruct((2 * SLOTS...  34.2 us
    pallas_call x4, Pallas kernels, point_values(): pl.pallas_call(lambda *refs: values_kernel(start, *refs), out_shape=jax.S...  21.8 us
    ppermute x16, starting transfers between devices, exchange(): return lax.ppermute(x, 'pts', [(i, i ^ d) for i in range(16)])  20.4 us
    ppermute x16, waiting for transfers between devices, exchange(): return lax.ppermute(x, 'pts', [(i, i ^ d) for i in range(16)])  19.1 us
    pallas_call x1, Pallas kernels, legendre_table(): pl.pallas_call(table_kernel, out_shape=[shape, shape], in_specs=vmem(3) +...  10.5 us
    pallas_call x2, Pallas kernels, unfold(): pl.pallas_call(unfold_second_kernel if second else unfold_first_kernel, o...  7.87 us
  transfers between devices with their start and end apart: 16, of which 11 were waited for; matrix products, arithmetic and copies ran while one was open for 0% of the time, Pallas kernels for 8%

profile of v3, /device:TPU:0, one launch (start us, length us, event | category | flops | bytes accessed | tf_op | source)
XLA Modules:
  0.0 193.9 jit_solution(18428277905253351133)
XLA Ops:
  2.8 2.2 %fusion.4 = (f32[81920]{0:T(1024)S(1)}, f32[81920]{0:T(1024)S(1)}, f32[81920]{0:T(1024)S(1)}, f32[81920]{0:T(1024)S(1)}) fusion(f32[81920]{0:T(1024)} %param.10), kind=kLoop, calls=%fused_computation.11 | loop fusion | flops 1146880 | bytes 1638400 | tf_op jit(solution)/shard_map/sin | solution.py:667
  8.0 10.5 %shard_map.105 = (bf16[40,304,256]{2,1,0:T(8,128)(2,1)S(1)}, bf16[40,304,256]{2,1,0:T(8,128)(2,1)S(1)}) custom-call(f32[40,128]{1,0:T(8,128)S(1)} %broadcast_in_dim.54.orders, f32[1,256]{1,0:T(1,128)S(1)} %bitcast.38, f32[40,256]{1,0:T(8,128)S(1)} %add_exponential_fusion.sectoral, f32[304]{0:T(512)S(1)} %copy-done.3), custom_call_target="tpu_custom_call" | custom-call | flops 62259200 | bytes 12451840 | tf_op jit(solution)/shard_map/pallas_call | solution.py:193
  19.5 34.2 %shard_map.104 = (f32[80,256]{1,0:T(8,128)S(1)}, f32[256,128]{1,0:T(8,128)S(1)}, f32[256,128]{1,0:T(8,128)S(1)}) custom-call(f32[1,81920]{1,0:T(1,128)S(1)} %bitcast.29, f32[1,81920]{1,0:T(1,128)S(1)} %bitcast.24, f32[1,81920]{1,0:T(1,128)S(1)} %bitcast.23, f32[1,81920]{1,0:T(1,128)S(1)} %bitcast.36, f32[1,81920]{1,0:T(1,128)S(1)} %bitcast.35, ...), custom_call_target="tpu_custom_call" | custom-call | flops 20132659200 | bytes 2621440 | tf_op jit(solution)/shard_map/pallas_call | solution.py:135
  53.7 3.9 %shard_map.106 = (f32[40,304]{1,0:T(8,128)S(1)}, f32[40,304]{1,0:T(8,128)S(1)}) custom-call(s32[1]{0:T(128)} %bitcast.1.core, f32[80,256]{1,0:T(8,128)S(1)} %get-tuple-element.103.field, bf16[40,304,256]{2,1,0:T(8,128)(2,1)S(1)} %get-tuple-element.104.p_high, bf16[40,304,256]{2,1,0:T(8,128)(2,1)S(1)} %get-tuple-element.105.p_low), custom_call_target="tpu_custom_call" | custom-call | flops 199229440 | bytes 12451840 | tf_op jit(solution)/shard_map/pallas_call | solution.py:358
  58.8 2.9 %collective-permute-start.3 = (f32[40,304]{1,0:T(8,128)S(1)}, f32[40,304]{1,0:T(8,128)S(1)}, u32[]{:S(2)}, u32[]{:S(2)}) collective-permute-start(f32[40,304]{1,0:T(8,128)S(1)} %add.90), channel_id=1, source_target_pairs={{0,48},{8,56},{16,32},{24,40},{32,16},{40,24},{48,0},{56,8},{64,11... | collective-permute-start | bytes 145928 | tf_op jit(solution)/shard_map/ppermute | solution.py:609
  67.7 3.3 %collective-permute-start.4 = (f32[40,304]{1,0:T(8,128)S(1)}, f32[40,304]{1,0:T(8,128)S(1)}, u32[]{:S(2)}, u32[]{:S(2)}) collective-permute-start(f32[40,304]{1,0:T(8,128)S(1)} %add_add_fusion.1), channel_id=1, source_target_pairs={{0,64},{8,72},{16,80},{24,88},{32,96},{40,104},{48,112},{56,120},{... | collective-permute-start | bytes 145928 | tf_op jit(solution)/shard_map/ppermute | solution.py:609
  71.0 2.5 %collective-permute-done.4 = f32[40,304]{1,0:T(8,128)S(1)} collective-permute-done((f32[40,304]{1,0:T(8,128)S(1)}, f32[40,304]{1,0:T(8,128)S(1)}, u32[]{:S(2)}, u32[]{:S(2)}) %collective-permute-start.4) | collective-permute-done | bytes 48672 | tf_op jit(solution)/shard_map/ppermute | solution.py:609
  74.9 2.8 %shard_map.107 = (f32[8,120,256]{2,1,0:T(8,128)S(1)}, f32[80,304]{1,0:T(8,128)S(1)}) custom-call(s32[1]{0:T(128)} %bitcast.1.core, f32[40,304]{1,0:T(8,128)S(1)} %add.94.mine, f32[40,304]{1,0:T(8,128)S(1)} %collective-permute-done.5.other, bf16[40,304,256]{2,1,0:T(8,128)(2,1)S(1)} %get-tuple-element.104.p_high, ...), custom_call_target="tpu_custom_call" | custom-call | flops 199229440 | bytes 12451840 | tf_op jit(solution)/shard_map/pallas_call | solution.py:279
  77.6 21.5 %all_to_all.20.refs_0_.got = f32[8,120,256]{2,1,0:T(8,128)S(1)} all-to-all(f32[8,120,256]{2,1,0:T(8,128)S(1)} %get-tuple-element.112), channel_id=1, replica_groups=mesh['pts'=16,'coef'=8] {'coef'}, dimensions={0} | all-to-all | bytes 1966080 | tf_op jit(solution)/shard_map/all_to_all | solution.py:640
  100.0 2.4 %shard_map.109 = (f32[8,40,128]{2,1,0:T(8,128)S(1)}, f32[4,32,640]{2,1,0:T(8,128)S(1)}) custom-call(s32[1]{0:T(128)} %bitcast.me.refs_0_, f32[8,120,256]{2,1,0:T(8,128)S(1)} %all_to_all.20.refs_0_.got, bf16[640,256]{1,0:T(8,128)(2,1)S(1)} %get-tuple-element.141.z_high.refs_5_, bf16[640,256]{1,0:T(8,128)(2,1)S(1)} %get-tuple-element.142.z_low.refs_6_, ...), custom_call_target="tpu_custom_call" | custom-call | flops 1000000000 | bytes 5000000 | tf_op jit(solution)/shard_map/pallas_call | solution.py:452
  102.4 9.3 %all_to_all.21.seen = f32[8,40,128]{2,1,0:T(8,128)S(1)} all-to-all(f32[8,40,128]{2,1,0:T(8,128)S(1)} %get-tuple-element.122), channel_id=1, replica_groups=mesh['pts'=16,'coef'=8] {'coef'}, dimensions={0} | all-to-all | bytes 327680 | tf_op jit(solution)/shard_map/all_to_all | solution.py:640
  111.7 4.0 %shard_map.110 = (f32[40,304]{1,0:T(8,128)S(1)}, f32[40,304]{1,0:T(8,128)S(1)}) custom-call(s32[1]{0:T(128)} %bitcast.1.core, f32[8,40,128]{2,1,0:T(8,128)S(1)} %all_to_all.21.seen, bf16[40,304,256]{2,1,0:T(8,128)(2,1)S(1)} %get-tuple-element.104.p_high, bf16[40,304,256]{2,1,0:T(8,128)(2,1)S(1)} %get-tuple-element.105.p_low), custom_call_target="tpu_custom_call" | custom-call | flops 199229440 | bytes 12451840 | tf_op jit(solution)/shard_map/pallas_call | solution.py:358
  119.0 2.8 %collective-permute-start.7 = (f32[40,304]{1,0:T(8,128)S(1)}, f32[40,304]{1,0:T(8,128)S(1)}, u32[]{:S(2)}, u32[]{:S(2)}) collective-permute-start(f32[40,304]{1,0:T(8,128)S(1)} %add.95), channel_id=1, source_target_pairs={{0,32},{8,40},{16,48},{24,56},{32,0},{40,8},{48,16},{56,24},{64,96... | collective-permute-start | bytes 145928 | tf_op jit(solution)/shard_map/ppermute | solution.py:609
  121.8 5.5 %shard_map.111 = f32[40,128]{1,0:T(8,128)S(1)} custom-call(s32[1]{0:T(128)} %bitcast.me.refs_0_, s32[1]{0:T(128)} %constant.101.clone.1.refs_1_, f32[1,81920]{1,0:T(1,128)S(1)} %bitcast.30, f32[1,81920]{1,0:T(1,128)S(1)} %bitcast.25, f32[1,81920]{1,0:T(1,128)S(1)} %bitcast.19, bf16[640,256]{1,0:T(8,128)(2,1)S(1)} %get-tuple-element.141.z_high.refs_5_, ...), custom_call_target="tpu_custom_call" | custom-call | flops 3355443200 | bytes 1000000 | tf_op jit(solution)/shard_map/pallas_call | solution.py:545
  127.3 3.0 %collective-permute-start.10 = (f32[40,304]{1,0:T(8,128)S(1)}, f32[40,304]{1,0:T(8,128)S(1)}, u32[]{:S(2)}, u32[]{:S(2)}) collective-permute-start(f32[40,304]{1,0:T(8,128)S(1)} %add_add_fusion), channel_id=1, source_target_pairs={{0,64},{8,72},{16,80},{24,88},{32,96},{40,104},{48,112},{56,120},{... | collective-permute-start | bytes 145928 | tf_op jit(solution)/shard_map/ppermute | solution.py:609
  130.3 5.4 %shard_map.112 = f32[40,128]{1,0:T(8,128)S(1)} custom-call(s32[1]{0:T(128)} %bitcast.me.refs_0_, s32[1]{0:T(128)} %constant.101.clone.1.refs_1_, f32[1,81920]{1,0:T(1,128)S(1)} %bitcast.31, f32[1,81920]{1,0:T(1,128)S(1)} %bitcast.26, f32[1,81920]{1,0:T(1,128)S(1)} %bitcast.20, bf16[640,256]{1,0:T(8,128)(2,1)S(1)} %get-tuple-element.141.z_high.refs_5_, ...), custom_call_target="tpu_custom_call" | custom-call | flops 3355443200 | bytes 1000000 | tf_op jit(solution)/shard_map/pallas_call | solution.py:545
  137.1 3.0 %shard_map.113 = (f32[8,88,256]{2,1,0:T(8,128)S(1)}, f32[80,304]{1,0:T(8,128)S(1)}, f32[8,128]{1,0:T(8,128)S(1)}) custom-call(s32[1]{0:T(128)} %bitcast.1.core, f32[40,304]{1,0:T(8,128)S(1)} %add.99.mine, f32[40,304]{1,0:T(8,128)S(1)} %collective-permute-done.11.other, f32[80,304]{1,0:T(8,128)S(1)} %get-tuple-element.190.vector, ...), custom_call_target="tpu_custom_call" | custom-call | flops 199229440 | bytes 12451840 | tf_op jit(solution)/shard_map/pallas_call | solution.py:315
  140.1 15.2 %all_to_all.22.refs_0_.got = f32[8,88,256]{2,1,0:T(8,128)S(1)} all-to-all(f32[8,88,256]{2,1,0:T(8,128)S(1)} %get-tuple-element.158), channel_id=1, replica_groups=mesh['pts'=16,'coef'=8] {'coef'}, dimensions={0} | all-to-all | bytes 1441792 | tf_op jit(solution)/shard_map/all_to_all | solution.py:640
  158.7 5.5 %shard_map.116 = f32[40,128]{1,0:T(8,128)S(1)} custom-call(s32[1]{0:T(128)} %bitcast.me.refs_0_, s32[1]{0:T(128)} %constant.101.clone.1.refs_1_, f32[1,81920]{1,0:T(1,128)S(1)} %bitcast.32, f32[1,81920]{1,0:T(1,128)S(1)} %bitcast.27, f32[1,81920]{1,0:T(1,128)S(1)} %bitcast.21, bf16[640,256]{1,0:T(8,128)(2,1)S(1)} %get-tuple-element.174.z_high.refs_5_, ...), custom_call_target="tpu_custom_call" | custom-call | flops 3355443200 | bytes 1000000 | tf_op jit(solution)/shard_map/pallas_call | solution.py:545
  164.2 5.5 %shard_map.117 = f32[40,128]{1,0:T(8,128)S(1)} custom-call(s32[1]{0:T(128)} %bitcast.me.refs_0_, s32[1]{0:T(128)} %constant.101.clone.1.refs_1_, f32[1,81920]{1,0:T(1,128)S(1)} %bitcast.33, f32[1,81920]{1,0:T(1,128)S(1)} %bitcast.28, f32[1,81920]{1,0:T(1,128)S(1)} %bitcast.22, bf16[640,256]{1,0:T(8,128)(2,1)S(1)} %get-tuple-element.174.z_high.refs_5_, ...), custom_call_target="tpu_custom_call" | custom-call | flops 3355443200 | bytes 1000000 | tf_op jit(solution)/shard_map/pallas_call | solution.py:545
  169.7 2.8 %collective-permute-start.14 = (f32[8,128]{1,0:T(8,128)S(1)}, f32[8,128]{1,0:T(8,128)S(1)}, u32[]{:S(2)}, u32[]{:S(2)}) collective-permute-start(f32[8,128]{1,0:T(8,128)S(1)} %add.101), channel_id=1, source_target_pairs={{0,32},{8,40},{16,48},{24,56},{32,0},{40,8},{48,16},{56,24},{64,96... | collective-permute-start | bytes 12296 | tf_op jit(solution)/shard_map/ppermute | solution.py:609
  172.5 2.4 %collective-permute-done.14 = f32[8,128]{1,0:T(8,128)S(1)} collective-permute-done((f32[8,128]{1,0:T(8,128)S(1)}, f32[8,128]{1,0:T(8,128)S(1)}, u32[]{:S(2)}, u32[]{:S(2)}) %collective-permute-start.14) | collective-permute-done | bytes 4128 | tf_op jit(solution)/shard_map/ppermute | solution.py:609
  175.9 4.1 %collective-permute-done.15 = f32[8,128]{1,0:T(8,128)S(1)} collective-permute-done((f32[8,128]{1,0:T(8,128)S(1)}, f32[8,128]{1,0:T(8,128)S(1)}, u32[]{:S(2)}, u32[]{:S(2)}) %collective-permute-start.15) | collective-permute-done | bytes 4128 | tf_op jit(solution)/shard_map/ppermute | solution.py:609
  180.0 12.3 %all_to_all.23.last = f32[8,168,128]{2,1,0:T(8,128)S(1)} all-to-all(f32[8,168,128]{2,1,0:T(8,128)S(1)} %broadcast_in_dim.59), channel_id=1, replica_groups=mesh['pts'=16,'coef'=8] {'coef'}, dimensions={0} | all-to-all | bytes 1376256 | tf_op jit(solution)/shard_map/all_to_all | solution.py:640
  (65 shorter events, 26.0 us)
Async XLA Ops:
  7.3 0.7 copy-start.3
  18.5 1.0 copy-start.1
  53.7 20.0 %copy-start.4 = (f32[301]{0:T(512)S(1)}, f32[301]{0:T(512)}, u32[]{:S(2)}) copy-start(f32[301]{0:T(512)} %param.15) | copy-start | bytes 3616
  57.6 1.3 collective-permute-start
  58.8 5.5 %collective-permute-start.3 = (f32[40,304]{1,0:T(8,128)S(1)}, f32[40,304]{1,0:T(8,128)S(1)}, u32[]{:S(2)}, u32[]{:S(2)}) collective-permute-start(f32[40,304]{1,0:T(8,128)S(1)} %add.90), channel_id=1, source_target_pairs={{0,48},{8,56},{16,32},{24,40},{32,16},{40,24},{48,0},{56,8},{64,11... | collective-permute-start | bytes 145928 | tf_op jit(solution)/shard_map/ppermute | solution.py:609
  61.8 4.4 %collective-permute-start.2 = (f32[40,304]{1,0:T(8,128)S(1)}, f32[40,304]{1,0:T(8,128)S(1)}, u32[]{:S(2)}, u32[]{:S(2)}) collective-permute-start(f32[40,304]{1,0:T(8,128)S(1)} %add.90), channel_id=1, source_target_pairs={{0,16},{8,24},{16,0},{24,8},{32,48},{40,56},{48,32},{56,40},{64,80... | collective-permute-start | bytes 145928 | tf_op jit(solution)/shard_map/ppermute | solution.py:609
  62.0 5.7 %collective-permute-start.1 = (f32[40,304]{1,0:T(8,128)S(1)}, f32[40,304]{1,0:T(8,128)S(1)}, u32[]{:S(2)}, u32[]{:S(2)}) collective-permute-start(f32[40,304]{1,0:T(8,128)S(1)} %add.90), channel_id=1, source_target_pairs={{0,32},{8,40},{16,48},{24,56},{32,0},{40,8},{48,16},{56,24},{64,96... | collective-permute-start | bytes 145928 | tf_op jit(solution)/shard_map/ppermute | solution.py:609
  67.7 5.8 %collective-permute-start.4 = (f32[40,304]{1,0:T(8,128)S(1)}, f32[40,304]{1,0:T(8,128)S(1)}, u32[]{:S(2)}, u32[]{:S(2)}) collective-permute-start(f32[40,304]{1,0:T(8,128)S(1)} %add_add_fusion.1), channel_id=1, source_target_pairs={{0,64},{8,72},{16,80},{24,88},{32,96},{40,104},{48,112},{56,120},{... | collective-permute-start | bytes 145928 | tf_op jit(solution)/shard_map/ppermute | solution.py:609
  73.5 1.3 collective-permute-start.5
  74.9 25.1 %copy-start.2 = (bf16[1280,640]{1,0:T(8,128)(2,1)S(1)}, bf16[1280,640]{1,0:T(8,128)(2,1)}, u32[]{:S(2)}) copy-start(bf16[1280,640]{1,0:T(8,128)(2,1)} %constant.103.clone.wave) | copy-start | bytes 4915204
  115.7 1.3 collective-permute-start.6
  117.0 10.2 %collective-permute-start.9 = (f32[40,304]{1,0:T(8,128)S(1)}, f32[40,304]{1,0:T(8,128)S(1)}, u32[]{:S(2)}, u32[]{:S(2)}) collective-permute-start(f32[40,304]{1,0:T(8,128)S(1)} %add.95), channel_id=1, source_target_pairs={{0,48},{8,56},{16,32},{24,40},{32,16},{40,24},{48,0},{56,8},{64,11... | collective-permute-start | bytes 145928 | tf_op jit(solution)/shard_map/ppermute | solution.py:609
  118.9 8.3 %collective-permute-start.8 = (f32[40,304]{1,0:T(8,128)S(1)}, f32[40,304]{1,0:T(8,128)S(1)}, u32[]{:S(2)}, u32[]{:S(2)}) collective-permute-start(f32[40,304]{1,0:T(8,128)S(1)} %add.95), channel_id=1, source_target_pairs={{0,16},{8,24},{16,0},{24,8},{32,48},{40,56},{48,32},{56,40},{64,80... | collective-permute-start | bytes 145928 | tf_op jit(solution)/shard_map/ppermute | solution.py:609
  119.0 8.3 %collective-permute-start.7 = (f32[40,304]{1,0:T(8,128)S(1)}, f32[40,304]{1,0:T(8,128)S(1)}, u32[]{:S(2)}, u32[]{:S(2)}) collective-permute-start(f32[40,304]{1,0:T(8,128)S(1)} %add.95), channel_id=1, source_target_pairs={{0,32},{8,40},{16,48},{24,56},{32,0},{40,8},{48,16},{56,24},{64,96... | collective-permute-start | bytes 145928 | tf_op jit(solution)/shard_map/ppermute | solution.py:609
  127.3 8.4 %collective-permute-start.10 = (f32[40,304]{1,0:T(8,128)S(1)}, f32[40,304]{1,0:T(8,128)S(1)}, u32[]{:S(2)}, u32[]{:S(2)}) collective-permute-start(f32[40,304]{1,0:T(8,128)S(1)} %add_add_fusion), channel_id=1, source_target_pairs={{0,64},{8,72},{16,80},{24,88},{32,96},{40,104},{48,112},{56,120},{... | collective-permute-start | bytes 145928 | tf_op jit(solution)/shard_map/ppermute | solution.py:609
  135.8 1.3 collective-permute-start.11
  156.9 1.2 collective-permute-start.12
  158.1 6.0 %collective-permute-start.13 = (f32[8,128]{1,0:T(8,128)S(1)}, f32[8,128]{1,0:T(8,128)S(1)}, u32[]{:S(2)}, u32[]{:S(2)}) collective-permute-start(f32[8,128]{1,0:T(8,128)S(1)} %add.100), channel_id=1, source_target_pairs={{0,16},{8,24},{16,0},{24,8},{32,48},{40,56},{48,32},{56,40},{64,80... | collective-permute-start | bytes 12296 | tf_op jit(solution)/shard_map/ppermute | solution.py:609
  164.2 28.2 %copy-start = (f32[81920]{0:T(1024)S(1)}, f32[81920]{0:T(1024)}, u32[]{:S(2)}) copy-start(f32[81920]{0:T(1024)} %param.13) | copy-start | bytes 983044
  169.7 5.2 %collective-permute-start.14 = (f32[8,128]{1,0:T(8,128)S(1)}, f32[8,128]{1,0:T(8,128)S(1)}, u32[]{:S(2)}, u32[]{:S(2)}) collective-permute-start(f32[8,128]{1,0:T(8,128)S(1)} %add.101), channel_id=1, source_target_pairs={{0,32},{8,40},{16,48},{24,56},{32,0},{40,8},{48,16},{56,24},{64,96... | collective-permute-start | bytes 12296 | tf_op jit(solution)/shard_map/ppermute | solution.py:609
  174.8 5.1 %collective-permute-start.15 = (f32[8,128]{1,0:T(8,128)S(1)}, f32[8,128]{1,0:T(8,128)S(1)}, u32[]{:S(2)}, u32[]{:S(2)}) collective-permute-start(f32[8,128]{1,0:T(8,128)S(1)} %add.102), channel_id=1, source_target_pairs={{0,64},{8,72},{16,80},{24,88},{32,96},{40,104},{48,112},{56,120},{... | collective-permute-start | bytes 12296 | tf_op jit(solution)/shard_map/ppermute | solution.py:609

commit v4 on v3

--- a/solution.py
+++ b/solution.py
@@ -90,7 +90,7 @@
     return jnp.where(ids == tile_row, 1.0, 0.0).astype(BF)
 
 
-WIDTH = 1024
+WIDTH = 2048
 UNROLL = 4
 
 
@@ -196,7 +196,7 @@
         in_specs=vmem(3) + [SMEM],
         out_specs=vmem(2),
         scratch_shapes=[pltpu.VMEM((SLOTS * DEG_PAD, LANES), F32)] * 2,
-        compiler_params=params(16),
+        compiler_params=params(30),
         cost_estimate=cost(20 * SLOTS * DEG_PAD * TILES, 4 * SLOTS * DEG_PAD * TILES),
     )(orders, cosine, sectoral, scale)
 
@@ -285,7 +285,7 @@
         in_specs=[SMEM] + vmem(8),
         out_specs=vmem(2),
         scratch_shapes=[pltpu.VMEM((2 * SLOTS, TILES), F32)],
-        compiler_params=params(8),
+        compiler_params=params(20),
         cost_estimate=cost(64 * SLOTS * DEG_PAD * TILES, 4 * SLOTS * DEG_PAD * TILES),
     )(core, *halves, p_high, p_low, prior, order_row, w_first, w_second)
 
@@ -322,7 +322,7 @@
         in_specs=[SMEM] + vmem(8),
         out_specs=vmem(3),
         scratch_shapes=[pltpu.VMEM((2 * SLOTS, TILES), F32)],
-        compiler_params=params(8),
+        compiler_params=params(20),
         cost_estimate=cost(64 * SLOTS * DEG_PAD * TILES, 4 * SLOTS * DEG_PAD * TILES),
     )(core, *halves, vector, got, p_high, p_low, prior, order_row)
 
@@ -361,7 +361,7 @@
         in_specs=[SMEM] + vmem(3),
         out_specs=vmem(2),
         scratch_shapes=[pltpu.VMEM((LANES, TILES), F32)] if second else [],
-        compiler_params=params(8),
+        compiler_params=params(20),
         cost_estimate=cost(64 * SLOTS * DEG_PAD * TILES, 4 * SLOTS * DEG_PAD * TILES),
     )(core, field, p_high, p_low)
 
@@ -471,13 +471,13 @@
     w_even, w_odd = kept[2], kept[3]
     terms = 2.0 * w_even * (even * even + odd * odd) + 4.0 * w_odd * (even * odd)
     energy = all_sum(terms)
-    out[...] = jnp.broadcast_to(energy, (8, LANES))
+    out[...] = jnp.broadcast_to(energy, out.shape)
 
 
 def grid_second(me, step, got, tables, kept, waves):
     return pl.pallas_call(
         grid_second_kernel,
-        out_shape=jax.ShapeDtypeStruct((8, LANES), F32),
+        out_shape=jax.ShapeDtypeStruct((SLOTS, TILES), F32),
         in_specs=[SMEM] + vmem(6),
         out_specs=pl.BlockSpec(memory_space=pltpu.VMEM),
         compiler_params=params(8),
@@ -537,7 +537,7 @@
             out[pl.ds(i * (S_WIDTH // LANES) + j, 1), :] = row[:, j * LANES : (j + 1) * LANES]
         return carry
 
-    lax.fori_loop(0, out.shape[0] * LANES // S_WIDTH, step, 0)
+    lax.fori_loop(0, out.shape[0] * LANES // S_WIDTH, step, 0, unroll=2)
 
 
 def point_values(me, points, tables, start, rows, gate):
@@ -616,24 +616,18 @@
     return lax.optimization_barrier((move(x), task(gate)))
 
 
-def halves_total(keep, give, tasks=(None, None)):
-    x = keep + exchange(give, 1)
+def chips_total(x, tasks):
     (x, across, near, both), first = gated(
         x, lambda v: (v, exchange(v, 4), exchange(v, 2), exchange(v, 6)), tasks[0]
     )
     x = (x + across) + (near + both)
     (x, far), second = gated(x, lambda v: (v, exchange(v, 8)), tasks[1])
-    x = x + far
-    return (x, exchange(x, 1)), [first, second]
-
-
-def pts_total(x, tasks):
-    made = []
-    for d, task in zip((1, 2, 4, 8), tasks):
-        (x, other), out = gated(x, lambda v: (v, exchange(v, d)), task)
-        x = x + other
-        made.append(out)
-    return x, [m for m in made if m is not None]
+    return x + far, [first, second]
+
+
+def halves_total(keep, give, tasks=(None, None)):
+    x, made = chips_total(keep + exchange(give, 1), tasks)
+    return (x, exchange(x, 1)), made
 
 
 def swap(x):
@@ -698,17 +692,15 @@
     me, values_0, kept, near, residual, residual_1, step = held
     tables_1 = lookup(got_1, EXTRA_SECOND)
     part = grid_second(me, step, got_1, tables_1, kept, wave)
-    energy_1, values_1 = pts_total(
-        part,
+    energy_1, values_1 = chips_total(
+        part + exchange(part, 1),
         [
-            None,
             lambda gate: point_values(me, near, tables_1, 0, half, gate),
             lambda gate: point_values(me, near, tables_1, half, own_rows - half, gate),
-            None,
         ],
     )
     payload = jnp.concatenate(
-        values_0 + values_1 + [energy_1], 0
+        values_0 + values_1 + [energy_1[0:8, 0:LANES]], 0
     )
     last = swap(jnp.broadcast_to(payload[None], (GROUPS,) + payload.shape))
     residual_out, vector = final(

time: 194 us -> 190 us (0.979)
  Pallas kernels: 85.8 us -> 81.1 us
    pallas_call x4, Pallas kernels: 21.8 us -> 18.8 us  [point_values(): pl.pallas_call(lambda *refs: values_kernel(start, *refs), out_shape=jax.S...]
    ppermute x16 -> x17, waiting for transfers between devices: 19.1 us -> 17.2 us  [exchange(): return lax.ppermute(x, 'pts', [(i, i ^ d) for i in range(16)])]
    ppermute x16 -> x17, starting transfers between devices: 20.4 us -> 21.9 us  [exchange(): return lax.ppermute(x, 'pts', [(i, i ^ d) for i in range(16)])]
  transfers between devices with their start and end apart: 16 -> 17, of which waited for: 11 -> 10; matrix products, arithmetic and copies ran while one was open for 0% -> 0% of each run, Pallas kernels for 8% -> 7%
where the time goes in v4:
time: 190 us; the launch traced here: 189 us
  Pallas kernels  81.1 us (43%)
  blocking collectives  59 us (31%)
  starting transfers between devices  21.9 us (12%)
  waiting for transfers between devices  17.2 us (9%)
  other arithmetic  6.02 us (3%)
  local copies, waits for them, and re-layouts  3.19 us (2%)
    all_to_all x4, blocking collectives, swap(): return lax.all_to_all(x, 'coef', 0, 0)  59 us
    pallas_call x1, Pallas kernels, moments(): pl.pallas_call(moments_kernel, out_shape=[jax.ShapeDtypeStruct((2 * SLOTS...  32.5 us
    ppermute x17, starting transfers between devices, exchange(): return lax.ppermute(x, 'pts', [(i, i ^ d) for i in range(16)])  21.9 us
    pallas_call x4, Pallas kernels, point_values(): pl.pallas_call(lambda *refs: values_kernel(start, *refs), out_shape=jax.S...  18.8 us
    ppermute x17, waiting for transfers between devices, exchange(): return lax.ppermute(x, 'pts', [(i, i ^ d) for i in range(16)])  17.2 us
    pallas_call x1, Pallas kernels, legendre_table(): pl.pallas_call(table_kernel, out_shape=[shape, shape], in_specs=vmem(3) +...  10.5 us
    pallas_call x2, Pallas kernels, unfold(): pl.pallas_call(unfold_second_kernel if second else unfold_first_kernel, o...  7.87 us
  transfers between devices with their start and end apart: 17, of which 10 were waited for; matrix products, arithmetic and copies ran while one was open for 0% of the time, Pallas kernels for 7%

profile of v4, /device:TPU:0, one launch (start us, length us, event | category | flops | bytes accessed | tf_op | source)
XLA Modules:
  0.0 189.3 jit_solution(2196769695033495614)
XLA Ops:
  2.8 2.2 %fusion.4 = (f32[81920]{0:T(1024)S(1)}, f32[81920]{0:T(1024)S(1)}, f32[81920]{0:T(1024)S(1)}, f32[81920]{0:T(1024)S(1)}) fusion(f32[81920]{0:T(1024)} %param.10), kind=kLoop, calls=%fused_computation.11 | loop fusion | flops 1146880 | bytes 1638400 | tf_op jit(solution)/shard_map/sin | solution.py:661
  8.0 10.5 %shard_map.105 = (bf16[40,304,256]{2,1,0:T(8,128)(2,1)S(1)}, bf16[40,304,256]{2,1,0:T(8,128)(2,1)S(1)}) custom-call(f32[40,128]{1,0:T(8,128)S(1)} %broadcast_in_dim.54.orders, f32[1,256]{1,0:T(1,128)S(1)} %bitcast.38, f32[40,256]{1,0:T(8,128)S(1)} %add_exponential_fusion.sectoral, f32[304]{0:T(512)S(1)} %copy-done.3), custom_call_target="tpu_custom_call" | custom-call | flops 62259200 | bytes 12451840 | tf_op jit(solution)/shard_map/pallas_call | solution.py:193
  19.5 32.5 %shard_map.104 = (f32[80,256]{1,0:T(8,128)S(1)}, f32[256,128]{1,0:T(8,128)S(1)}, f32[256,128]{1,0:T(8,128)S(1)}) custom-call(f32[1,81920]{1,0:T(1,128)S(1)} %bitcast.29, f32[1,81920]{1,0:T(1,128)S(1)} %bitcast.24, f32[1,81920]{1,0:T(1,128)S(1)} %bitcast.23, f32[1,81920]{1,0:T(1,128)S(1)} %bitcast.36, f32[1,81920]{1,0:T(1,128)S(1)} %bitcast.35, ...), custom_call_target="tpu_custom_call" | custom-call | flops 20132659200 | bytes 2621440 | tf_op jit(solution)/shard_map/pallas_call | solution.py:135
  52.0 3.9 %shard_map.106 = (f32[40,304]{1,0:T(8,128)S(1)}, f32[40,304]{1,0:T(8,128)S(1)}) custom-call(s32[1]{0:T(128)} %bitcast.1.core, f32[80,256]{1,0:T(8,128)S(1)} %get-tuple-element.105.field, bf16[40,304,256]{2,1,0:T(8,128)(2,1)S(1)} %get-tuple-element.106.p_high, bf16[40,304,256]{2,1,0:T(8,128)(2,1)S(1)} %get-tuple-element.107.p_low), custom_call_target="tpu_custom_call" | custom-call | flops 199229440 | bytes 12451840 | tf_op jit(solution)/shard_map/pallas_call | solution.py:358
  57.2 2.9 %collective-permute-start.3 = (f32[40,304]{1,0:T(8,128)S(1)}, f32[40,304]{1,0:T(8,128)S(1)}, u32[]{:S(2)}, u32[]{:S(2)}) collective-permute-start(f32[40,304]{1,0:T(8,128)S(1)} %add.93), channel_id=1, source_target_pairs={{0,48},{8,56},{16,32},{24,40},{32,16},{40,24},{48,0},{56,8},{64,11... | collective-permute-start | bytes 145928 | tf_op jit(solution)/shard_map/ppermute | solution.py:609
  66.0 3.3 %collective-permute-start.4 = (f32[40,304]{1,0:T(8,128)S(1)}, f32[40,304]{1,0:T(8,128)S(1)}, u32[]{:S(2)}, u32[]{:S(2)}) collective-permute-start(f32[40,304]{1,0:T(8,128)S(1)} %add_add_fusion.1), channel_id=1, source_target_pairs={{0,64},{8,72},{16,80},{24,88},{32,96},{40,104},{48,112},{56,120},{... | collective-permute-start | bytes 145928 | tf_op jit(solution)/shard_map/ppermute | solution.py:609
  69.3 2.5 %collective-permute-done.4 = f32[40,304]{1,0:T(8,128)S(1)} collective-permute-done((f32[40,304]{1,0:T(8,128)S(1)}, f32[40,304]{1,0:T(8,128)S(1)}, u32[]{:S(2)}, u32[]{:S(2)}) %collective-permute-start.4) | collective-permute-done | bytes 48672 | tf_op jit(solution)/shard_map/ppermute | solution.py:609
  73.2 2.8 %shard_map.107 = (f32[8,120,256]{2,1,0:T(8,128)S(1)}, f32[80,304]{1,0:T(8,128)S(1)}) custom-call(s32[1]{0:T(128)} %bitcast.1.core, f32[40,304]{1,0:T(8,128)S(1)} %add.97.mine, f32[40,304]{1,0:T(8,128)S(1)} %collective-permute-done.5.other, bf16[40,304,256]{2,1,0:T(8,128)(2,1)S(1)} %get-tuple-element.106.p_high, ...), custom_call_target="tpu_custom_call" | custom-call | flops 199229440 | bytes 12451840 | tf_op jit(solution)/shard_map/pallas_call | solution.py:279
  76.0 21.5 %all_to_all.20.refs_0_.got = f32[8,120,256]{2,1,0:T(8,128)S(1)} all-to-all(f32[8,120,256]{2,1,0:T(8,128)S(1)} %get-tuple-element.114), channel_id=1, replica_groups=mesh['pts'=16,'coef'=8] {'coef'}, dimensions={0} | all-to-all | bytes 1966080 | tf_op jit(solution)/shard_map/all_to_all | solution.py:634
  98.3 2.4 %shard_map.109 = (f32[8,40,128]{2,1,0:T(8,128)S(1)}, f32[4,32,640]{2,1,0:T(8,128)S(1)}) custom-call(s32[1]{0:T(128)} %bitcast.me.refs_0_, f32[8,120,256]{2,1,0:T(8,128)S(1)} %all_to_all.20.refs_0_.got, bf16[640,256]{1,0:T(8,128)(2,1)S(1)} %get-tuple-element.143.z_high.refs_5_, bf16[640,256]{1,0:T(8,128)(2,1)S(1)} %get-tuple-element.144.z_low.refs_6_, ...), custom_call_target="tpu_custom_call" | custom-call | flops 1000000000 | bytes 5000000 | tf_op jit(solution)/shard_map/pallas_call | solution.py:452
  100.7 9.3 %all_to_all.21.seen = f32[8,40,128]{2,1,0:T(8,128)S(1)} all-to-all(f32[8,40,128]{2,1,0:T(8,128)S(1)} %get-tuple-element.124), channel_id=1, replica_groups=mesh['pts'=16,'coef'=8] {'coef'}, dimensions={0} | all-to-all | bytes 327680 | tf_op jit(solution)/shard_map/all_to_all | solution.py:634
  110.1 4.0 %shard_map.110 = (f32[40,304]{1,0:T(8,128)S(1)}, f32[40,304]{1,0:T(8,128)S(1)}) custom-call(s32[1]{0:T(128)} %bitcast.1.core, f32[8,40,128]{2,1,0:T(8,128)S(1)} %all_to_all.21.seen, bf16[40,304,256]{2,1,0:T(8,128)(2,1)S(1)} %get-tuple-element.106.p_high, bf16[40,304,256]{2,1,0:T(8,128)(2,1)S(1)} %get-tuple-element.107.p_low), custom_call_target="tpu_custom_call" | custom-call | flops 199229440 | bytes 12451840 | tf_op jit(solution)/shard_map/pallas_call | solution.py:358
  115.3 1.9 %collective-permute-start.9 = (f32[40,304]{1,0:T(8,128)S(1)}, f32[40,304]{1,0:T(8,128)S(1)}, u32[]{:S(2)}, u32[]{:S(2)}) collective-permute-start(f32[40,304]{1,0:T(8,128)S(1)} %add.98), channel_id=1, source_target_pairs={{0,48},{8,56},{16,32},{24,40},{32,16},{40,24},{48,0},{56,8},{64,11... | collective-permute-start | bytes 145928 | tf_op jit(solution)/shard_map/ppermute | solution.py:609
  117.3 2.8 %collective-permute-start.7 = (f32[40,304]{1,0:T(8,128)S(1)}, f32[40,304]{1,0:T(8,128)S(1)}, u32[]{:S(2)}, u32[]{:S(2)}) collective-permute-start(f32[40,304]{1,0:T(8,128)S(1)} %add.98), channel_id=1, source_target_pairs={{0,32},{8,40},{16,48},{24,56},{32,0},{40,8},{48,16},{56,24},{64,96... | collective-permute-start | bytes 145928 | tf_op jit(solution)/shard_map/ppermute | solution.py:609
  120.1 4.7 %shard_map.111 = f32[40,128]{1,0:T(8,128)S(1)} custom-call(s32[1]{0:T(128)} %bitcast.me.refs_0_, s32[1]{0:T(128)} %constant.101.clone.1.refs_1_, f32[1,81920]{1,0:T(1,128)S(1)} %bitcast.30, f32[1,81920]{1,0:T(1,128)S(1)} %bitcast.25, f32[1,81920]{1,0:T(1,128)S(1)} %bitcast.19, bf16[640,256]{1,0:T(8,128)(2,1)S(1)} %get-tuple-element.143.z_high.refs_5_, ...), custom_call_target="tpu_custom_call" | custom-call | flops 3355443200 | bytes 1000000 | tf_op jit(solution)/shard_map/pallas_call | solution.py:545
  124.9 3.0 %collective-permute-start.10 = (f32[40,304]{1,0:T(8,128)S(1)}, f32[40,304]{1,0:T(8,128)S(1)}, u32[]{:S(2)}, u32[]{:S(2)}) collective-permute-start(f32[40,304]{1,0:T(8,128)S(1)} %add_add_fusion), channel_id=1, source_target_pairs={{0,64},{8,72},{16,80},{24,88},{32,96},{40,104},{48,112},{56,120},{... | collective-permute-start | bytes 145928 | tf_op jit(solution)/shard_map/ppermute | solution.py:609
  127.8 4.7 %shard_map.112 = f32[40,128]{1,0:T(8,128)S(1)} custom-call(s32[1]{0:T(128)} %bitcast.me.refs_0_, s32[1]{0:T(128)} %constant.101.clone.1.refs_1_, f32[1,81920]{1,0:T(1,128)S(1)} %bitcast.31, f32[1,81920]{1,0:T(1,128)S(1)} %bitcast.26, f32[1,81920]{1,0:T(1,128)S(1)} %bitcast.20, bf16[640,256]{1,0:T(8,128)(2,1)S(1)} %get-tuple-element.143.z_high.refs_5_, ...), custom_call_target="tpu_custom_call" | custom-call | flops 3355443200 | bytes 1000000 | tf_op jit(solution)/shard_map/pallas_call | solution.py:545
  133.9 3.0 %shard_map.113 = (f32[8,88,256]{2,1,0:T(8,128)S(1)}, f32[80,304]{1,0:T(8,128)S(1)}, f32[8,128]{1,0:T(8,128)S(1)}) custom-call(s32[1]{0:T(128)} %bitcast.1.core, f32[40,304]{1,0:T(8,128)S(1)} %add.102.mine, f32[40,304]{1,0:T(8,128)S(1)} %collective-permute-done.11.other, f32[80,304]{1,0:T(8,128)S(1)} %get-tuple-element.194.vector, ...), custom_call_target="tpu_custom_call" | custom-call | flops 199229440 | bytes 12451840 | tf_op jit(solution)/shard_map/pallas_call | solution.py:315
  136.9 15.2 %all_to_all.22.refs_0_.got = f32[8,88,256]{2,1,0:T(8,128)S(1)} all-to-all(f32[8,88,256]{2,1,0:T(8,128)S(1)} %get-tuple-element.160), channel_id=1, replica_groups=mesh['pts'=16,'coef'=8] {'coef'}, dimensions={0} | all-to-all | bytes 1441792 | tf_op jit(solution)/shard_map/all_to_all | solution.py:634
  156.8 2.9 %collective-permute-start.13 = (f32[40,256]{1,0:T(8,128)S(1)}, f32[40,256]{1,0:T(8,128)S(1)}, u32[]{:S(2)}, u32[]{:S(2)}) collective-permute-start(f32[40,256]{1,0:T(8,128)S(1)} %add.103), channel_id=1, source_target_pairs={{0,32},{8,40},{16,48},{24,56},{32,0},{40,8},{48,16},{56,24},{64,96... | collective-permute-start | bytes 122888 | tf_op jit(solution)/shard_map/ppermute | solution.py:609
  159.7 4.7 %shard_map.116 = f32[40,128]{1,0:T(8,128)S(1)} custom-call(s32[1]{0:T(128)} %bitcast.me.refs_0_, s32[1]{0:T(128)} %constant.101.clone.1.refs_1_, f32[1,81920]{1,0:T(1,128)S(1)} %bitcast.32, f32[1,81920]{1,0:T(1,128)S(1)} %bitcast.27, f32[1,81920]{1,0:T(1,128)S(1)} %bitcast.21, bf16[640,256]{1,0:T(8,128)(2,1)S(1)} %get-tuple-element.176.z_high.refs_5_, ...), custom_call_target="tpu_custom_call" | custom-call | flops 3355443200 | bytes 1000000 | tf_op jit(solution)/shard_map/pallas_call | solution.py:545
  164.5 4.7 %shard_map.117 = f32[40,128]{1,0:T(8,128)S(1)} custom-call(s32[1]{0:T(128)} %bitcast.me.refs_0_, s32[1]{0:T(128)} %constant.101.clone.1.refs_1_, f32[1,81920]{1,0:T(1,128)S(1)} %bitcast.33, f32[1,81920]{1,0:T(1,128)S(1)} %bitcast.28, f32[1,81920]{1,0:T(1,128)S(1)} %bitcast.22, bf16[640,256]{1,0:T(8,128)(2,1)S(1)} %get-tuple-element.176.z_high.refs_5_, ...), custom_call_target="tpu_custom_call" | custom-call | flops 3355443200 | bytes 1000000 | tf_op jit(solution)/shard_map/pallas_call | solution.py:545
  170.3 4.5 %collective-permute-done.16 = f32[40,256]{1,0:T(8,128)S(1)} collective-permute-done((f32[40,256]{1,0:T(8,128)S(1)}, f32[40,256]{1,0:T(8,128)S(1)}, u32[]{:S(2)}, u32[]{:S(2)}) %collective-permute-start.16) | collective-permute-done | bytes 40992 | tf_op jit(solution)/shard_map/ppermute | solution.py:609
  174.8 12.9 %all_to_all.23.last = f32[8,168,128]{2,1,0:T(8,128)S(1)} all-to-all(f32[8,168,128]{2,1,0:T(8,128)S(1)} %broadcast_in_dim.59), channel_id=1, replica_groups=mesh['pts'=16,'coef'=8] {'coef'}, dimensions={0} | all-to-all | bytes 1376256 | tf_op jit(solution)/shard_map/all_to_all | solution.py:634
  (66 shorter events, 25.5 us)
Async XLA Ops:
  7.3 0.7 copy-start.3
  18.5 1.0 copy-start.1
  52.0 20.1 %copy-start.4 = (f32[301]{0:T(512)S(1)}, f32[301]{0:T(512)}, u32[]{:S(2)}) copy-start(f32[301]{0:T(512)} %param.15) | copy-start | bytes 3616
  55.9 1.3 collective-permute-start
  57.2 5.5 %collective-permute-start.3 = (f32[40,304]{1,0:T(8,128)S(1)}, f32[40,304]{1,0:T(8,128)S(1)}, u32[]{:S(2)}, u32[]{:S(2)}) collective-permute-start(f32[40,304]{1,0:T(8,128)S(1)} %add.93), channel_id=1, source_target_pairs={{0,48},{8,56},{16,32},{24,40},{32,16},{40,24},{48,0},{56,8},{64,11... | collective-permute-start | bytes 145928 | tf_op jit(solution)/shard_map/ppermute | solution.py:609
  60.1 4.4 %collective-permute-start.2 = (f32[40,304]{1,0:T(8,128)S(1)}, f32[40,304]{1,0:T(8,128)S(1)}, u32[]{:S(2)}, u32[]{:S(2)}) collective-permute-start(f32[40,304]{1,0:T(8,128)S(1)} %add.93), channel_id=1, source_target_pairs={{0,16},{8,24},{16,0},{24,8},{32,48},{40,56},{48,32},{56,40},{64,80... | collective-permute-start | bytes 145928 | tf_op jit(solution)/shard_map/ppermute | solution.py:609
  60.3 5.7 %collective-permute-start.1 = (f32[40,304]{1,0:T(8,128)S(1)}, f32[40,304]{1,0:T(8,128)S(1)}, u32[]{:S(2)}, u32[]{:S(2)}) collective-permute-start(f32[40,304]{1,0:T(8,128)S(1)} %add.93), channel_id=1, source_target_pairs={{0,32},{8,40},{16,48},{24,56},{32,0},{40,8},{48,16},{56,24},{64,96... | collective-permute-start | bytes 145928 | tf_op jit(solution)/shard_map/ppermute | solution.py:609
  66.0 5.8 %collective-permute-start.4 = (f32[40,304]{1,0:T(8,128)S(1)}, f32[40,304]{1,0:T(8,128)S(1)}, u32[]{:S(2)}, u32[]{:S(2)}) collective-permute-start(f32[40,304]{1,0:T(8,128)S(1)} %add_add_fusion.1), channel_id=1, source_target_pairs={{0,64},{8,72},{16,80},{24,88},{32,96},{40,104},{48,112},{56,120},{... | collective-permute-start | bytes 145928 | tf_op jit(solution)/shard_map/ppermute | solution.py:609
  71.9 1.3 collective-permute-start.5
  73.2 25.1 %copy-start.2 = (bf16[1280,640]{1,0:T(8,128)(2,1)S(1)}, bf16[1280,640]{1,0:T(8,128)(2,1)}, u32[]{:S(2)}) copy-start(bf16[1280,640]{1,0:T(8,128)(2,1)} %constant.103.clone.wave) | copy-start | bytes 4915204
  114.1 1.3 collective-permute-start.6
  115.3 9.5 %collective-permute-start.9 = (f32[40,304]{1,0:T(8,128)S(1)}, f32[40,304]{1,0:T(8,128)S(1)}, u32[]{:S(2)}, u32[]{:S(2)}) collective-permute-start(f32[40,304]{1,0:T(8,128)S(1)} %add.98), channel_id=1, source_target_pairs={{0,48},{8,56},{16,32},{24,40},{32,16},{40,24},{48,0},{56,8},{64,11... | collective-permute-start | bytes 145928 | tf_op jit(solution)/shard_map/ppermute | solution.py:609
  117.2 7.6 %collective-permute-start.8 = (f32[40,304]{1,0:T(8,128)S(1)}, f32[40,304]{1,0:T(8,128)S(1)}, u32[]{:S(2)}, u32[]{:S(2)}) collective-permute-start(f32[40,304]{1,0:T(8,128)S(1)} %add.98), channel_id=1, source_target_pairs={{0,16},{8,24},{16,0},{24,8},{32,48},{40,56},{48,32},{56,40},{64,80... | collective-permute-start | bytes 145928 | tf_op jit(solution)/shard_map/ppermute | solution.py:609
  117.3 7.5 %collective-permute-start.7 = (f32[40,304]{1,0:T(8,128)S(1)}, f32[40,304]{1,0:T(8,128)S(1)}, u32[]{:S(2)}, u32[]{:S(2)}) collective-permute-start(f32[40,304]{1,0:T(8,128)S(1)} %add.98), channel_id=1, source_target_pairs={{0,32},{8,40},{16,48},{24,56},{32,0},{40,8},{48,16},{56,24},{64,96... | collective-permute-start | bytes 145928 | tf_op jit(solution)/shard_map/ppermute | solution.py:609
  124.9 7.7 %collective-permute-start.10 = (f32[40,304]{1,0:T(8,128)S(1)}, f32[40,304]{1,0:T(8,128)S(1)}, u32[]{:S(2)}, u32[]{:S(2)}) collective-permute-start(f32[40,304]{1,0:T(8,128)S(1)} %add_add_fusion), channel_id=1, source_target_pairs={{0,64},{8,72},{16,80},{24,88},{32,96},{40,104},{48,112},{56,120},{... | collective-permute-start | bytes 145928 | tf_op jit(solution)/shard_map/ppermute | solution.py:609
  132.5 1.3 collective-permute-start.11
  153.7 1.3 collective-permute-start.12
  155.0 9.4 %collective-permute-start.15 = (f32[40,256]{1,0:T(8,128)S(1)}, f32[40,256]{1,0:T(8,128)S(1)}, u32[]{:S(2)}, u32[]{:S(2)}) collective-permute-start(f32[40,256]{1,0:T(8,128)S(1)} %add.103), channel_id=1, source_target_pairs={{0,48},{8,56},{16,32},{24,40},{32,16},{40,24},{48,0},{56,8},{64,11... | collective-permute-start | bytes 122888 | tf_op jit(solution)/shard_map/ppermute | solution.py:609
  156.8 7.6 %collective-permute-start.14 = (f32[40,256]{1,0:T(8,128)S(1)}, f32[40,256]{1,0:T(8,128)S(1)}, u32[]{:S(2)}, u32[]{:S(2)}) collective-permute-start(f32[40,256]{1,0:T(8,128)S(1)} %add.103), channel_id=1, source_target_pairs={{0,16},{8,24},{16,0},{24,8},{32,48},{40,56},{48,32},{56,40},{64,80... | collective-permute-start | bytes 122888 | tf_op jit(solution)/shard_map/ppermute | solution.py:609
  156.8 7.6 %collective-permute-start.13 = (f32[40,256]{1,0:T(8,128)S(1)}, f32[40,256]{1,0:T(8,128)S(1)}, u32[]{:S(2)}, u32[]{:S(2)}) collective-permute-start(f32[40,256]{1,0:T(8,128)S(1)} %add.103), channel_id=1, source_target_pairs={{0,32},{8,40},{16,48},{24,56},{32,0},{40,8},{48,16},{56,24},{64,96... | collective-permute-start | bytes 122888 | tf_op jit(solution)/shard_map/ppermute | solution.py:609
  164.5 23.3 %copy-start = (f32[81920]{0:T(1024)S(1)}, f32[81920]{0:T(1024)}, u32[]{:S(2)}) copy-start(f32[81920]{0:T(1024)} %param.13) | copy-start | bytes 983044
  169.2 5.6 %collective-permute-start.16 = (f32[40,256]{1,0:T(8,128)S(1)}, f32[40,256]{1,0:T(8,128)S(1)}, u32[]{:S(2)}, u32[]{:S(2)}) collective-permute-start(f32[40,256]{1,0:T(8,128)S(1)} %add_add_fusion.2), channel_id=1, source_target_pairs={{0,64},{8,72},{16,80},{24,88},{32,96},{40,104},{48,112},{56,120},{... | collective-permute-start | bytes 122888 | tf_op jit(solution)/shard_map/ppermute | solution.py:609

commit v5 on v4

--- a/solution.py
+++ b/solution.py
@@ -174,7 +174,7 @@
 
     empty = jnp.zeros((SLOTS, TILES), F32)
     unset = start * 0.0
-    lax.fori_loop(0, DEG_PAD, step, (unset, unset, order_sq * 0.0), unroll=4)
+    lax.fori_loop(0, DEG_PAD, step, (unset, unset, order_sq * 0.0), unroll=8)
     for n in range(DEGREES, DEG_PAD):
         put(n, empty)
 
@@ -185,7 +185,7 @@
         p_low[slot] = low
         return carry
 
-    lax.fori_loop(0, SLOTS, pack, 0)
+    lax.fori_loop(0, SLOTS, pack, 0, unroll=4)
 
 
 def legendre_table(orders, cosine, sectoral, scale):
@@ -222,7 +222,7 @@
         put(at, slot_group(vector, at, lambda i: p_high[i], lambda i: p_low[i], width, dims))
         return carry
 
-    lax.fori_loop(0, SLOTS // 8, group, 0)
+    lax.fori_loop(0, SLOTS // 8, group, 0, unroll=True)
 
 
 F_ROWS = 2 * SLOTS
@@ -537,7 +537,7 @@
             out[pl.ds(i * (S_WIDTH // LANES) + j, 1), :] = row[:, j * LANES : (j + 1) * LANES]
         return carry
 
-    lax.fori_loop(0, out.shape[0] * LANES // S_WIDTH, step, 0, unroll=2)
+    lax.fori_loop(0, out.shape[0] * LANES // S_WIDTH, step, 0, unroll=10)
 
 
 def point_values(me, points, tables, start, rows, gate):

time: 190 us -> 184 us (0.968)
  Pallas kernels: 81.1 us -> 75.3 us
    pallas_call x4, Pallas kernels: 18.8 us -> 15.4 us  [point_values(): pl.pallas_call(lambda *refs: values_kernel(start, *refs), out_shape=jax.S...]
  transfers between devices with their start and end apart: 17 -> 17, of which waited for: 10 -> 10; matrix products, arithmetic and copies ran while one was open for 0% -> 0% of each run, Pallas kernels for 7% -> 6%
where the time goes in v5:
time: 184 us
  Pallas kernels  75.3 us (41%)
  blocking collectives  58.9 us (32%)
  starting transfers between devices  22.9 us (12%)
  waiting for transfers between devices  16.4 us (9%)
  other arithmetic  6.02 us (3%)
  local copies, waits for them, and re-layouts  3.19 us (2%)
    all_to_all x4, blocking collectives, swap(): return lax.all_to_all(x, 'coef', 0, 0)  58.9 us
    pallas_call x1, Pallas kernels, moments(): pl.pallas_call(moments_kernel, out_shape=[jax.ShapeDtypeStruct((2 * SLOTS...  32.5 us
    ppermute x17, starting transfers between devices, exchange(): return lax.ppermute(x, 'pts', [(i, i ^ d) for i in range(16)])  22.9 us
    ppermute x17, waiting for transfers between devices, exchange(): return lax.ppermute(x, 'pts', [(i, i ^ d) for i in range(16)])  16.4 us
    pallas_call x4, Pallas kernels, point_values(): pl.pallas_call(lambda *refs: values_kernel(start, *refs), out_shape=jax.S...  15.4 us
    pallas_call x1, Pallas kernels, legendre_table(): pl.pallas_call(table_kernel, out_shape=[shape, shape], in_specs=vmem(3) +...  10.2 us
    pallas_call x2, Pallas kernels, unfold(): pl.pallas_call(unfold_second_kernel if second else unfold_first_kernel, o...  6.77 us
  transfers between devices with their start and end apart: 17, of which 10 were waited for; matrix products, arithmetic and copies ran while one was open for 0% of the time, Pallas kernels for 6%

profile of v5, /device:TPU:0, one launch (start us, length us, event | category | flops | bytes accessed | tf_op | source)
XLA Modules:
  0.0 183.6 jit_solution(3353186087625441637)
XLA Ops:
  2.8 2.2 %fusion.4 = (f32[81920]{0:T(1024)S(1)}, f32[81920]{0:T(1024)S(1)}, f32[81920]{0:T(1024)S(1)}, f32[81920]{0:T(1024)S(1)}) fusion(f32[81920]{0:T(1024)} %param.10), kind=kLoop, calls=%fused_computation.11 | loop fusion | flops 1146880 | bytes 1638400 | tf_op jit(solution)/shard_map/sin | solution.py:661
  8.0 10.2 %shard_map.105 = (bf16[40,304,256]{2,1,0:T(8,128)(2,1)S(1)}, bf16[40,304,256]{2,1,0:T(8,128)(2,1)S(1)}) custom-call(f32[40,128]{1,0:T(8,128)S(1)} %broadcast_in_dim.54.orders, f32[1,256]{1,0:T(1,128)S(1)} %bitcast.38, f32[40,256]{1,0:T(8,128)S(1)} %add_exponential_fusion.sectoral, f32[304]{0:T(512)S(1)} %copy-done.3), custom_call_target="tpu_custom_call" | custom-call | flops 62259200 | bytes 12451840 | tf_op jit(solution)/shard_map/pallas_call | solution.py:193
  19.2 32.5 %shard_map.104 = (f32[80,256]{1,0:T(8,128)S(1)}, f32[256,128]{1,0:T(8,128)S(1)}, f32[256,128]{1,0:T(8,128)S(1)}) custom-call(f32[1,81920]{1,0:T(1,128)S(1)} %bitcast.29, f32[1,81920]{1,0:T(1,128)S(1)} %bitcast.24, f32[1,81920]{1,0:T(1,128)S(1)} %bitcast.23, f32[1,81920]{1,0:T(1,128)S(1)} %bitcast.36, f32[1,81920]{1,0:T(1,128)S(1)} %bitcast.35, ...), custom_call_target="tpu_custom_call" | custom-call | flops 20132659200 | bytes 2621440 | tf_op jit(solution)/shard_map/pallas_call | solution.py:135
  51.7 3.4 %shard_map.106 = (f32[40,304]{1,0:T(8,128)S(1)}, f32[40,304]{1,0:T(8,128)S(1)}) custom-call(s32[1]{0:T(128)} %bitcast.1.core, f32[80,256]{1,0:T(8,128)S(1)} %get-tuple-element.105.field, bf16[40,304,256]{2,1,0:T(8,128)(2,1)S(1)} %get-tuple-element.106.p_high, bf16[40,304,256]{2,1,0:T(8,128)(2,1)S(1)} %get-tuple-element.107.p_low), custom_call_target="tpu_custom_call" | custom-call | flops 199229440 | bytes 12451840 | tf_op jit(solution)/shard_map/pallas_call | solution.py:358
  56.4 2.9 %collective-permute-start.3 = (f32[40,304]{1,0:T(8,128)S(1)}, f32[40,304]{1,0:T(8,128)S(1)}, u32[]{:S(2)}, u32[]{:S(2)}) collective-permute-start(f32[40,304]{1,0:T(8,128)S(1)} %add.93), channel_id=1, source_target_pairs={{0,48},{8,56},{16,32},{24,40},{32,16},{40,24},{48,0},{56,8},{64,11... | collective-permute-start | bytes 145928 | tf_op jit(solution)/shard_map/ppermute | solution.py:609
  65.3 3.3 %collective-permute-start.4 = (f32[40,304]{1,0:T(8,128)S(1)}, f32[40,304]{1,0:T(8,128)S(1)}, u32[]{:S(2)}, u32[]{:S(2)}) collective-permute-start(f32[40,304]{1,0:T(8,128)S(1)} %add_add_fusion.1), channel_id=1, source_target_pairs={{0,64},{8,72},{16,80},{24,88},{32,96},{40,104},{48,112},{56,120},{... | collective-permute-start | bytes 145928 | tf_op jit(solution)/shard_map/ppermute | solution.py:609
  68.5 2.5 %collective-permute-done.4 = f32[40,304]{1,0:T(8,128)S(1)} collective-permute-done((f32[40,304]{1,0:T(8,128)S(1)}, f32[40,304]{1,0:T(8,128)S(1)}, u32[]{:S(2)}, u32[]{:S(2)}) %collective-permute-start.4) | collective-permute-done | bytes 48672 | tf_op jit(solution)/shard_map/ppermute | solution.py:609
  72.4 2.2 %shard_map.107 = (f32[8,120,256]{2,1,0:T(8,128)S(1)}, f32[80,304]{1,0:T(8,128)S(1)}) custom-call(s32[1]{0:T(128)} %bitcast.1.core, f32[40,304]{1,0:T(8,128)S(1)} %add.97.mine, f32[40,304]{1,0:T(8,128)S(1)} %collective-permute-done.5.other, bf16[40,304,256]{2,1,0:T(8,128)(2,1)S(1)} %get-tuple-element.106.p_high, ...), custom_call_target="tpu_custom_call" | custom-call | flops 199229440 | bytes 12451840 | tf_op jit(solution)/shard_map/pallas_call | solution.py:279
  74.6 21.5 %all_to_all.20.refs_0_.got = f32[8,120,256]{2,1,0:T(8,128)S(1)} all-to-all(f32[8,120,256]{2,1,0:T(8,128)S(1)} %get-tuple-element.114), channel_id=1, replica_groups=mesh['pts'=16,'coef'=8] {'coef'}, dimensions={0} | all-to-all | bytes 1966080 | tf_op jit(solution)/shard_map/all_to_all | solution.py:634
  97.0 2.4 %shard_map.109 = (f32[8,40,128]{2,1,0:T(8,128)S(1)}, f32[4,32,640]{2,1,0:T(8,128)S(1)}) custom-call(s32[1]{0:T(128)} %bitcast.me.refs_0_, f32[8,120,256]{2,1,0:T(8,128)S(1)} %all_to_all.20.refs_0_.got, bf16[640,256]{1,0:T(8,128)(2,1)S(1)} %get-tuple-element.143.z_high.refs_5_, bf16[640,256]{1,0:T(8,128)(2,1)S(1)} %get-tuple-element.144.z_low.refs_6_, ...), custom_call_target="tpu_custom_call" | custom-call | flops 1000000000 | bytes 5000000 | tf_op jit(solution)/shard_map/pallas_call | solution.py:452
  99.4 9.3 %all_to_all.21.seen = f32[8,40,128]{2,1,0:T(8,128)S(1)} all-to-all(f32[8,40,128]{2,1,0:T(8,128)S(1)} %get-tuple-element.124), channel_id=1, replica_groups=mesh['pts'=16,'coef'=8] {'coef'}, dimensions={0} | all-to-all | bytes 327680 | tf_op jit(solution)/shard_map/all_to_all | solution.py:634
  108.7 3.4 %shard_map.110 = (f32[40,304]{1,0:T(8,128)S(1)}, f32[40,304]{1,0:T(8,128)S(1)}) custom-call(s32[1]{0:T(128)} %bitcast.1.core, f32[8,40,128]{2,1,0:T(8,128)S(1)} %all_to_all.21.seen, bf16[40,304,256]{2,1,0:T(8,128)(2,1)S(1)} %get-tuple-element.106.p_high, bf16[40,304,256]{2,1,0:T(8,128)(2,1)S(1)} %get-tuple-element.107.p_low), custom_call_target="tpu_custom_call" | custom-call | flops 199229440 | bytes 12451840 | tf_op jit(solution)/shard_map/pallas_call | solution.py:358
  115.4 2.8 %collective-permute-start.7 = (f32[40,304]{1,0:T(8,128)S(1)}, f32[40,304]{1,0:T(8,128)S(1)}, u32[]{:S(2)}, u32[]{:S(2)}) collective-permute-start(f32[40,304]{1,0:T(8,128)S(1)} %add.98), channel_id=1, source_target_pairs={{0,32},{8,40},{16,48},{24,56},{32,0},{40,8},{48,16},{56,24},{64,96... | collective-permute-start | bytes 145928 | tf_op jit(solution)/shard_map/ppermute | solution.py:609
  118.2 3.8 %shard_map.111 = f32[40,128]{1,0:T(8,128)S(1)} custom-call(s32[1]{0:T(128)} %bitcast.me.refs_0_, s32[1]{0:T(128)} %constant.101.clone.1.refs_1_, f32[1,81920]{1,0:T(1,128)S(1)} %bitcast.30, f32[1,81920]{1,0:T(1,128)S(1)} %bitcast.25, f32[1,81920]{1,0:T(1,128)S(1)} %bitcast.19, bf16[640,256]{1,0:T(8,128)(2,1)S(1)} %get-tuple-element.143.z_high.refs_5_, ...), custom_call_target="tpu_custom_call" | custom-call | flops 3355443200 | bytes 1000000 | tf_op jit(solution)/shard_map/pallas_call | solution.py:545
  122.1 3.2 %collective-permute-start.10 = (f32[40,304]{1,0:T(8,128)S(1)}, f32[40,304]{1,0:T(8,128)S(1)}, u32[]{:S(2)}, u32[]{:S(2)}) collective-permute-start(f32[40,304]{1,0:T(8,128)S(1)} %add_add_fusion), channel_id=1, source_target_pairs={{0,64},{8,72},{16,80},{24,88},{32,96},{40,104},{48,112},{56,120},{... | collective-permute-start | bytes 145928 | tf_op jit(solution)/shard_map/ppermute | solution.py:609
  125.3 3.8 %shard_map.112 = f32[40,128]{1,0:T(8,128)S(1)} custom-call(s32[1]{0:T(128)} %bitcast.me.refs_0_, s32[1]{0:T(128)} %constant.101.clone.1.refs_1_, f32[1,81920]{1,0:T(1,128)S(1)} %bitcast.31, f32[1,81920]{1,0:T(1,128)S(1)} %bitcast.26, f32[1,81920]{1,0:T(1,128)S(1)} %bitcast.20, bf16[640,256]{1,0:T(8,128)(2,1)S(1)} %get-tuple-element.143.z_high.refs_5_, ...), custom_call_target="tpu_custom_call" | custom-call | flops 3355443200 | bytes 1000000 | tf_op jit(solution)/shard_map/pallas_call | solution.py:545
  130.5 2.4 %shard_map.113 = (f32[8,88,256]{2,1,0:T(8,128)S(1)}, f32[80,304]{1,0:T(8,128)S(1)}, f32[8,128]{1,0:T(8,128)S(1)}) custom-call(s32[1]{0:T(128)} %bitcast.1.core, f32[40,304]{1,0:T(8,128)S(1)} %add.102.mine, f32[40,304]{1,0:T(8,128)S(1)} %collective-permute-done.11.other, f32[80,304]{1,0:T(8,128)S(1)} %get-tuple-element.194.vector, ...), custom_call_target="tpu_custom_call" | custom-call | flops 199229440 | bytes 12451840 | tf_op jit(solution)/shard_map/pallas_call | solution.py:315
  132.9 15.2 %all_to_all.22.refs_0_.got = f32[8,88,256]{2,1,0:T(8,128)S(1)} all-to-all(f32[8,88,256]{2,1,0:T(8,128)S(1)} %get-tuple-element.160), channel_id=1, replica_groups=mesh['pts'=16,'coef'=8] {'coef'}, dimensions={0} | all-to-all | bytes 1441792 | tf_op jit(solution)/shard_map/all_to_all | solution.py:634
  152.9 2.9 %collective-permute-start.13 = (f32[40,256]{1,0:T(8,128)S(1)}, f32[40,256]{1,0:T(8,128)S(1)}, u32[]{:S(2)}, u32[]{:S(2)}) collective-permute-start(f32[40,256]{1,0:T(8,128)S(1)} %add.103), channel_id=1, source_target_pairs={{0,32},{8,40},{16,48},{24,56},{32,0},{40,8},{48,16},{56,24},{64,96... | collective-permute-start | bytes 122888 | tf_op jit(solution)/shard_map/ppermute | solution.py:609
  155.7 3.9 %shard_map.116 = f32[40,128]{1,0:T(8,128)S(1)} custom-call(s32[1]{0:T(128)} %bitcast.me.refs_0_, s32[1]{0:T(128)} %constant.101.clone.1.refs_1_, f32[1,81920]{1,0:T(1,128)S(1)} %bitcast.32, f32[1,81920]{1,0:T(1,128)S(1)} %bitcast.27, f32[1,81920]{1,0:T(1,128)S(1)} %bitcast.21, bf16[640,256]{1,0:T(8,128)(2,1)S(1)} %get-tuple-element.176.z_high.refs_5_, ...), custom_call_target="tpu_custom_call" | custom-call | flops 3355443200 | bytes 1000000 | tf_op jit(solution)/shard_map/pallas_call | solution.py:545
  159.7 3.9 %shard_map.117 = f32[40,128]{1,0:T(8,128)S(1)} custom-call(s32[1]{0:T(128)} %bitcast.me.refs_0_, s32[1]{0:T(128)} %constant.101.clone.1.refs_1_, f32[1,81920]{1,0:T(1,128)S(1)} %bitcast.33, f32[1,81920]{1,0:T(1,128)S(1)} %bitcast.28, f32[1,81920]{1,0:T(1,128)S(1)} %bitcast.22, bf16[640,256]{1,0:T(8,128)(2,1)S(1)} %get-tuple-element.176.z_high.refs_5_, ...), custom_call_target="tpu_custom_call" | custom-call | flops 3355443200 | bytes 1000000 | tf_op jit(solution)/shard_map/pallas_call | solution.py:545
  163.6 1.9 %collective-permute-start.16 = (f32[40,256]{1,0:T(8,128)S(1)}, f32[40,256]{1,0:T(8,128)S(1)}, u32[]{:S(2)}, u32[]{:S(2)}) collective-permute-start(f32[40,256]{1,0:T(8,128)S(1)} %add_add_fusion.2), channel_id=1, source_target_pairs={{0,64},{8,72},{16,80},{24,88},{32,96},{40,104},{48,112},{56,120},{... | collective-permute-start | bytes 122888 | tf_op jit(solution)/shard_map/ppermute | solution.py:609
  165.5 3.6 %collective-permute-done.16 = f32[40,256]{1,0:T(8,128)S(1)} collective-permute-done((f32[40,256]{1,0:T(8,128)S(1)}, f32[40,256]{1,0:T(8,128)S(1)}, u32[]{:S(2)}, u32[]{:S(2)}) %collective-permute-start.16) | collective-permute-done | bytes 40992 | tf_op jit(solution)/shard_map/ppermute | solution.py:609
  169.2 12.9 %all_to_all.23.last = f32[8,168,128]{2,1,0:T(8,128)S(1)} all-to-all(f32[8,168,128]{2,1,0:T(8,128)S(1)} %broadcast_in_dim.59), channel_id=1, replica_groups=mesh['pts'=16,'coef'=8] {'coef'}, dimensions={0} | all-to-all | bytes 1376256 | tf_op jit(solution)/shard_map/all_to_all | solution.py:634
  (66 shorter events, 26.4 us)
Async XLA Ops:
  7.3 0.7 copy-start.3
  18.2 1.0 copy-start.1
  51.7 19.6 %copy-start.4 = (f32[301]{0:T(512)S(1)}, f32[301]{0:T(512)}, u32[]{:S(2)}) copy-start(f32[301]{0:T(512)} %param.15) | copy-start | bytes 3616
  55.1 1.3 collective-permute-start
  56.4 5.5 %collective-permute-start.3 = (f32[40,304]{1,0:T(8,128)S(1)}, f32[40,304]{1,0:T(8,128)S(1)}, u32[]{:S(2)}, u32[]{:S(2)}) collective-permute-start(f32[40,304]{1,0:T(8,128)S(1)} %add.93), channel_id=1, source_target_pairs={{0,48},{8,56},{16,32},{24,40},{32,16},{40,24},{48,0},{56,8},{64,11... | collective-permute-start | bytes 145928 | tf_op jit(solution)/shard_map/ppermute | solution.py:609
  59.3 4.4 %collective-permute-start.2 = (f32[40,304]{1,0:T(8,128)S(1)}, f32[40,304]{1,0:T(8,128)S(1)}, u32[]{:S(2)}, u32[]{:S(2)}) collective-permute-start(f32[40,304]{1,0:T(8,128)S(1)} %add.93), channel_id=1, source_target_pairs={{0,16},{8,24},{16,0},{24,8},{32,48},{40,56},{48,32},{56,40},{64,80... | collective-permute-start | bytes 145928 | tf_op jit(solution)/shard_map/ppermute | solution.py:609
  59.5 5.7 %collective-permute-start.1 = (f32[40,304]{1,0:T(8,128)S(1)}, f32[40,304]{1,0:T(8,128)S(1)}, u32[]{:S(2)}, u32[]{:S(2)}) collective-permute-start(f32[40,304]{1,0:T(8,128)S(1)} %add.93), channel_id=1, source_target_pairs={{0,32},{8,40},{16,48},{24,56},{32,0},{40,8},{48,16},{56,24},{64,96... | collective-permute-start | bytes 145928 | tf_op jit(solution)/shard_map/ppermute | solution.py:609
  65.3 5.8 %collective-permute-start.4 = (f32[40,304]{1,0:T(8,128)S(1)}, f32[40,304]{1,0:T(8,128)S(1)}, u32[]{:S(2)}, u32[]{:S(2)}) collective-permute-start(f32[40,304]{1,0:T(8,128)S(1)} %add_add_fusion.1), channel_id=1, source_target_pairs={{0,64},{8,72},{16,80},{24,88},{32,96},{40,104},{48,112},{56,120},{... | collective-permute-start | bytes 145928 | tf_op jit(solution)/shard_map/ppermute | solution.py:609
  71.1 1.3 collective-permute-start.5
  72.4 24.6 %copy-start.2 = (bf16[1280,640]{1,0:T(8,128)(2,1)S(1)}, bf16[1280,640]{1,0:T(8,128)(2,1)}, u32[]{:S(2)}) copy-start(bf16[1280,640]{1,0:T(8,128)(2,1)} %constant.103.clone.wave) | copy-start | bytes 4915204
  112.1 1.3 collective-permute-start.6
  113.4 8.6 %collective-permute-start.9 = (f32[40,304]{1,0:T(8,128)S(1)}, f32[40,304]{1,0:T(8,128)S(1)}, u32[]{:S(2)}, u32[]{:S(2)}) collective-permute-start(f32[40,304]{1,0:T(8,128)S(1)} %add.98), channel_id=1, source_target_pairs={{0,48},{8,56},{16,32},{24,40},{32,16},{40,24},{48,0},{56,8},{64,11... | collective-permute-start | bytes 145928 | tf_op jit(solution)/shard_map/ppermute | solution.py:609
  115.3 6.7 %collective-permute-start.8 = (f32[40,304]{1,0:T(8,128)S(1)}, f32[40,304]{1,0:T(8,128)S(1)}, u32[]{:S(2)}, u32[]{:S(2)}) collective-permute-start(f32[40,304]{1,0:T(8,128)S(1)} %add.98), channel_id=1, source_target_pairs={{0,16},{8,24},{16,0},{24,8},{32,48},{40,56},{48,32},{56,40},{64,80... | collective-permute-start | bytes 145928 | tf_op jit(solution)/shard_map/ppermute | solution.py:609
  115.4 6.7 %collective-permute-start.7 = (f32[40,304]{1,0:T(8,128)S(1)}, f32[40,304]{1,0:T(8,128)S(1)}, u32[]{:S(2)}, u32[]{:S(2)}) collective-permute-start(f32[40,304]{1,0:T(8,128)S(1)} %add.98), channel_id=1, source_target_pairs={{0,32},{8,40},{16,48},{24,56},{32,0},{40,8},{48,16},{56,24},{64,96... | collective-permute-start | bytes 145928 | tf_op jit(solution)/shard_map/ppermute | solution.py:609
  122.1 7.1 %collective-permute-start.10 = (f32[40,304]{1,0:T(8,128)S(1)}, f32[40,304]{1,0:T(8,128)S(1)}, u32[]{:S(2)}, u32[]{:S(2)}) collective-permute-start(f32[40,304]{1,0:T(8,128)S(1)} %add_add_fusion), channel_id=1, source_target_pairs={{0,64},{8,72},{16,80},{24,88},{32,96},{40,104},{48,112},{56,120},{... | collective-permute-start | bytes 145928 | tf_op jit(solution)/shard_map/ppermute | solution.py:609
  129.1 1.3 collective-permute-start.11
  149.7 1.3 collective-permute-start.12
  151.0 8.6 %collective-permute-start.15 = (f32[40,256]{1,0:T(8,128)S(1)}, f32[40,256]{1,0:T(8,128)S(1)}, u32[]{:S(2)}, u32[]{:S(2)}) collective-permute-start(f32[40,256]{1,0:T(8,128)S(1)} %add.103), channel_id=1, source_target_pairs={{0,48},{8,56},{16,32},{24,40},{32,16},{40,24},{48,0},{56,8},{64,11... | collective-permute-start | bytes 122888 | tf_op jit(solution)/shard_map/ppermute | solution.py:609
  152.9 6.8 %collective-permute-start.14 = (f32[40,256]{1,0:T(8,128)S(1)}, f32[40,256]{1,0:T(8,128)S(1)}, u32[]{:S(2)}, u32[]{:S(2)}) collective-permute-start(f32[40,256]{1,0:T(8,128)S(1)} %add.103), channel_id=1, source_target_pairs={{0,16},{8,24},{16,0},{24,8},{32,48},{40,56},{48,32},{56,40},{64,80... | collective-permute-start | bytes 122888 | tf_op jit(solution)/shard_map/ppermute | solution.py:609
  152.9 6.8 %collective-permute-start.13 = (f32[40,256]{1,0:T(8,128)S(1)}, f32[40,256]{1,0:T(8,128)S(1)}, u32[]{:S(2)}, u32[]{:S(2)}) collective-permute-start(f32[40,256]{1,0:T(8,128)S(1)} %add.103), channel_id=1, source_target_pairs={{0,32},{8,40},{16,48},{24,56},{32,0},{40,8},{48,16},{56,24},{64,96... | collective-permute-start | bytes 122888 | tf_op jit(solution)/shard_map/ppermute | solution.py:609
  159.7 22.5 %copy-start = (f32[81920]{0:T(1024)S(1)}, f32[81920]{0:T(1024)}, u32[]{:S(2)}) copy-start(f32[81920]{0:T(1024)} %param.13) | copy-start | bytes 983044
  163.6 5.6 %collective-permute-start.16 = (f32[40,256]{1,0:T(8,128)S(1)}, f32[40,256]{1,0:T(8,128)S(1)}, u32[]{:S(2)}, u32[]{:S(2)}) collective-permute-start(f32[40,256]{1,0:T(8,128)S(1)} %add_add_fusion.2), channel_id=1, source_target_pairs={{0,64},{8,72},{16,80},{24,88},{32,96},{40,104},{48,112},{56,120},{... | collective-permute-start | bytes 122888 | tf_op jit(solution)/shard_map/ppermute | solution.py:609

commit v6 on v5

--- a/solution.py
+++ b/solution.py
@@ -616,11 +616,13 @@
     return lax.optimization_barrier((move(x), task(gate)))
 
 
+def chips_near(x, task):
+    (x, across, near, both), made = gated(x, lambda v: (v, exchange(v, 4), exchange(v, 2), exchange(v, 6)), task)
+    return (x + across) + (near + both), (made, None)
+
+
 def chips_total(x, tasks):
-    (x, across, near, both), first = gated(
-        x, lambda v: (v, exchange(v, 4), exchange(v, 2), exchange(v, 6)), tasks[0]
-    )
-    x = (x + across) + (near + both)
+    x, (first, _) = chips_near(x, tasks[0])
     (x, far), second = gated(x, lambda v: (v, exchange(v, 8)), tasks[1])
     return x + far, [first, second]
 
@@ -692,13 +694,15 @@
     me, values_0, kept, near, residual, residual_1, step = held
     tables_1 = lookup(got_1, EXTRA_SECOND)
     part = grid_second(me, step, got_1, tables_1, kept, wave)
-    energy_1, values_1 = chips_total(
-        part + exchange(part, 1),
-        [
-            lambda gate: point_values(me, near, tables_1, 0, half, gate),
-            lambda gate: point_values(me, near, tables_1, half, own_rows - half, gate),
-        ],
-    )
+    part = part + exchange(part, 1)
+    (part, far), first = gated(
+        part, lambda v: (v, exchange(v, 8)), lambda gate: point_values(me, near, tables_1, 0, half, gate)
+    )
+    energy_1, (second, _) = chips_near(
+        part + far,
+        lambda gate: point_values(me, near, tables_1, half, own_rows - half, gate),
+    )
+    values_1 = [first, second]
     payload = jnp.concatenate(
         values_0 + values_1 + [energy_1[0:8, 0:LANES]], 0
     )

time: 184 us -> 181 us (0.984)
  waiting for transfers between devices: 16.4 us -> 12.7 us
    ppermute x17, waiting for transfers between devices: 16.4 us -> 12.7 us  [exchange(): return lax.ppermute(x, 'pts', [(i, i ^ d) for i in range(16)])]
  transfers between devices with their start and end apart: 17 -> 17, of which waited for: 10 -> 9; matrix products, arithmetic and copies ran while one was open for 0% -> 0% of each run, Pallas kernels for 6% -> 9%
where the time goes in v6:
time: 181 us
  Pallas kernels  75.3 us (42%)
  blocking collectives  59.8 us (33%)
  starting transfers between devices  22.9 us (13%)
  waiting for transfers between devices  12.7 us (7%)
  other arithmetic  6.02 us (3%)
  local copies, waits for them, and re-layouts  3.19 us (2%)
    all_to_all x4, blocking collectives, swap(): return lax.all_to_all(x, 'coef', 0, 0)  59.8 us
    pallas_call x1, Pallas kernels, moments(): pl.pallas_call(moments_kernel, out_shape=[jax.ShapeDtypeStruct((2 * SLOTS...  32.5 us
    ppermute x17, starting transfers between devices, exchange(): return lax.ppermute(x, 'pts', [(i, i ^ d) for i in range(16)])  22.9 us
    pallas_call x4, Pallas kernels, point_values(): pl.pallas_call(lambda *refs: values_kernel(start, *refs), out_shape=jax.S...  15.4 us
    ppermute x17, waiting for transfers between devices, exchange(): return lax.ppermute(x, 'pts', [(i, i ^ d) for i in range(16)])  12.7 us
    pallas_call x1, Pallas kernels, legendre_table(): pl.pallas_call(table_kernel, out_shape=[shape, shape], in_specs=vmem(3) +...  10.2 us
    pallas_call x2, Pallas kernels, unfold(): pl.pallas_call(unfold_second_kernel if second else unfold_first_kernel, o...  6.77 us
  transfers between devices with their start and end apart: 17, of which 9 were waited for; matrix products, arithmetic and copies ran while one was open for 0% of the time, Pallas kernels for 9%

profile of v6, /device:TPU:0, one launch (start us, length us, event | category | flops | bytes accessed | tf_op | source)
XLA Modules:
  0.0 180.9 jit_solution(12667184005710273638)
XLA Ops:
  2.8 2.2 %fusion.4 = (f32[81920]{0:T(1024)S(1)}, f32[81920]{0:T(1024)S(1)}, f32[81920]{0:T(1024)S(1)}, f32[81920]{0:T(1024)S(1)}) fusion(f32[81920]{0:T(1024)} %param.10), kind=kLoop, calls=%fused_computation.11 | loop fusion | flops 1146880 | bytes 1638400 | tf_op jit(solution)/shard_map/sin | solution.py:663
  8.0 10.2 %shard_map.105 = (bf16[40,304,256]{2,1,0:T(8,128)(2,1)S(1)}, bf16[40,304,256]{2,1,0:T(8,128)(2,1)S(1)}) custom-call(f32[40,128]{1,0:T(8,128)S(1)} %broadcast_in_dim.54.orders, f32[1,256]{1,0:T(1,128)S(1)} %bitcast.38, f32[40,256]{1,0:T(8,128)S(1)} %add_exponential_fusion.sectoral, f32[304]{0:T(512)S(1)} %copy-done.3), custom_call_target="tpu_custom_call" | custom-call | flops 62259200 | bytes 12451840 | tf_op jit(solution)/shard_map/pallas_call | solution.py:193
  19.2 32.5 %shard_map.104 = (f32[80,256]{1,0:T(8,128)S(1)}, f32[256,128]{1,0:T(8,128)S(1)}, f32[256,128]{1,0:T(8,128)S(1)}) custom-call(f32[1,81920]{1,0:T(1,128)S(1)} %bitcast.29, f32[1,81920]{1,0:T(1,128)S(1)} %bitcast.24, f32[1,81920]{1,0:T(1,128)S(1)} %bitcast.23, f32[1,81920]{1,0:T(1,128)S(1)} %bitcast.36, f32[1,81920]{1,0:T(1,128)S(1)} %bitcast.35, ...), custom_call_target="tpu_custom_call" | custom-call | flops 20132659200 | bytes 2621440 | tf_op jit(solution)/shard_map/pallas_call | solution.py:135
  51.7 3.4 %shard_map.106 = (f32[40,304]{1,0:T(8,128)S(1)}, f32[40,304]{1,0:T(8,128)S(1)}) custom-call(s32[1]{0:T(128)} %bitcast.1.core, f32[80,256]{1,0:T(8,128)S(1)} %get-tuple-element.105.field, bf16[40,304,256]{2,1,0:T(8,128)(2,1)S(1)} %get-tuple-element.106.p_high, bf16[40,304,256]{2,1,0:T(8,128)(2,1)S(1)} %get-tuple-element.107.p_low), custom_call_target="tpu_custom_call" | custom-call | flops 199229440 | bytes 12451840 | tf_op jit(solution)/shard_map/pallas_call | solution.py:358
  56.4 2.9 %collective-permute-start.3 = (f32[40,304]{1,0:T(8,128)S(1)}, f32[40,304]{1,0:T(8,128)S(1)}, u32[]{:S(2)}, u32[]{:S(2)}) collective-permute-start(f32[40,304]{1,0:T(8,128)S(1)} %add.93), channel_id=1, source_target_pairs={{0,48},{8,56},{16,32},{24,40},{32,16},{40,24},{48,0},{56,8},{64,11... | collective-permute-start | bytes 145928 | tf_op jit(solution)/shard_map/ppermute | solution.py:609
  65.3 3.3 %collective-permute-start.4 = (f32[40,304]{1,0:T(8,128)S(1)}, f32[40,304]{1,0:T(8,128)S(1)}, u32[]{:S(2)}, u32[]{:S(2)}) collective-permute-start(f32[40,304]{1,0:T(8,128)S(1)} %add_add_fusion.1), channel_id=1, source_target_pairs={{0,64},{8,72},{16,80},{24,88},{32,96},{40,104},{48,112},{56,120},{... | collective-permute-start | bytes 145928 | tf_op jit(solution)/shard_map/ppermute | solution.py:609
  68.5 2.5 %collective-permute-done.4 = f32[40,304]{1,0:T(8,128)S(1)} collective-permute-done((f32[40,304]{1,0:T(8,128)S(1)}, f32[40,304]{1,0:T(8,128)S(1)}, u32[]{:S(2)}, u32[]{:S(2)}) %collective-permute-start.4) | collective-permute-done | bytes 48672 | tf_op jit(solution)/shard_map/ppermute | solution.py:609
  72.4 2.2 %shard_map.107 = (f32[8,120,256]{2,1,0:T(8,128)S(1)}, f32[80,304]{1,0:T(8,128)S(1)}) custom-call(s32[1]{0:T(128)} %bitcast.1.core, f32[40,304]{1,0:T(8,128)S(1)} %add.97.mine, f32[40,304]{1,0:T(8,128)S(1)} %collective-permute-done.5.other, bf16[40,304,256]{2,1,0:T(8,128)(2,1)S(1)} %get-tuple-element.106.p_high, ...), custom_call_target="tpu_custom_call" | custom-call | flops 199229440 | bytes 12451840 | tf_op jit(solution)/shard_map/pallas_call | solution.py:279
  74.6 21.5 %all_to_all.20.refs_0_.got = f32[8,120,256]{2,1,0:T(8,128)S(1)} all-to-all(f32[8,120,256]{2,1,0:T(8,128)S(1)} %get-tuple-element.114), channel_id=1, replica_groups=mesh['pts'=16,'coef'=8] {'coef'}, dimensions={0} | all-to-all | bytes 1966080 | tf_op jit(solution)/shard_map/all_to_all | solution.py:636
  97.0 2.4 %shard_map.109 = (f32[8,40,128]{2,1,0:T(8,128)S(1)}, f32[4,32,640]{2,1,0:T(8,128)S(1)}) custom-call(s32[1]{0:T(128)} %bitcast.me.refs_0_, f32[8,120,256]{2,1,0:T(8,128)S(1)} %all_to_all.20.refs_0_.got, bf16[640,256]{1,0:T(8,128)(2,1)S(1)} %get-tuple-element.143.z_high.refs_5_, bf16[640,256]{1,0:T(8,128)(2,1)S(1)} %get-tuple-element.144.z_low.refs_6_, ...), custom_call_target="tpu_custom_call" | custom-call | flops 1000000000 | bytes 5000000 | tf_op jit(solution)/shard_map/pallas_call | solution.py:452
  99.4 9.3 %all_to_all.21.seen = f32[8,40,128]{2,1,0:T(8,128)S(1)} all-to-all(f32[8,40,128]{2,1,0:T(8,128)S(1)} %get-tuple-element.124), channel_id=1, replica_groups=mesh['pts'=16,'coef'=8] {'coef'}, dimensions={0} | all-to-all | bytes 327680 | tf_op jit(solution)/shard_map/all_to_all | solution.py:636
  108.7 3.4 %shard_map.110 = (f32[40,304]{1,0:T(8,128)S(1)}, f32[40,304]{1,0:T(8,128)S(1)}) custom-call(s32[1]{0:T(128)} %bitcast.1.core, f32[8,40,128]{2,1,0:T(8,128)S(1)} %all_to_all.21.seen, bf16[40,304,256]{2,1,0:T(8,128)(2,1)S(1)} %get-tuple-element.106.p_high, bf16[40,304,256]{2,1,0:T(8,128)(2,1)S(1)} %get-tuple-element.107.p_low), custom_call_target="tpu_custom_call" | custom-call | flops 199229440 | bytes 12451840 | tf_op jit(solution)/shard_map/pallas_call | solution.py:358
  113.4 1.9 %collective-permute-start.9 = (f32[40,304]{1,0:T(8,128)S(1)}, f32[40,304]{1,0:T(8,128)S(1)}, u32[]{:S(2)}, u32[]{:S(2)}) collective-permute-start(f32[40,304]{1,0:T(8,128)S(1)} %add.98), channel_id=1, source_target_pairs={{0,48},{8,56},{16,32},{24,40},{32,16},{40,24},{48,0},{56,8},{64,11... | collective-permute-start | bytes 145928 | tf_op jit(solution)/shard_map/ppermute | solution.py:609
  115.4 2.8 %collective-permute-start.7 = (f32[40,304]{1,0:T(8,128)S(1)}, f32[40,304]{1,0:T(8,128)S(1)}, u32[]{:S(2)}, u32[]{:S(2)}) collective-permute-start(f32[40,304]{1,0:T(8,128)S(1)} %add.98), channel_id=1, source_target_pairs={{0,32},{8,40},{16,48},{24,56},{32,0},{40,8},{48,16},{56,24},{64,96... | collective-permute-start | bytes 145928 | tf_op jit(solution)/shard_map/ppermute | solution.py:609
  118.2 3.8 %shard_map.111 = f32[40,128]{1,0:T(8,128)S(1)} custom-call(s32[1]{0:T(128)} %bitcast.me.refs_0_, s32[1]{0:T(128)} %constant.101.clone.1.refs_1_, f32[1,81920]{1,0:T(1,128)S(1)} %bitcast.30, f32[1,81920]{1,0:T(1,128)S(1)} %bitcast.25, f32[1,81920]{1,0:T(1,128)S(1)} %bitcast.19, bf16[640,256]{1,0:T(8,128)(2,1)S(1)} %get-tuple-element.143.z_high.refs_5_, ...), custom_call_target="tpu_custom_call" | custom-call | flops 3355443200 | bytes 1000000 | tf_op jit(solution)/shard_map/pallas_call | solution.py:545
  122.1 3.2 %collective-permute-start.10 = (f32[40,304]{1,0:T(8,128)S(1)}, f32[40,304]{1,0:T(8,128)S(1)}, u32[]{:S(2)}, u32[]{:S(2)}) collective-permute-start(f32[40,304]{1,0:T(8,128)S(1)} %add_add_fusion), channel_id=1, source_target_pairs={{0,64},{8,72},{16,80},{24,88},{32,96},{40,104},{48,112},{56,120},{... | collective-permute-start | bytes 145928 | tf_op jit(solution)/shard_map/ppermute | solution.py:609
  125.3 3.8 %shard_map.112 = f32[40,128]{1,0:T(8,128)S(1)} custom-call(s32[1]{0:T(128)} %bitcast.me.refs_0_, s32[1]{0:T(128)} %constant.101.clone.1.refs_1_, f32[1,81920]{1,0:T(1,128)S(1)} %bitcast.31, f32[1,81920]{1,0:T(1,128)S(1)} %bitcast.26, f32[1,81920]{1,0:T(1,128)S(1)} %bitcast.20, bf16[640,256]{1,0:T(8,128)(2,1)S(1)} %get-tuple-element.143.z_high.refs_5_, ...), custom_call_target="tpu_custom_call" | custom-call | flops 3355443200 | bytes 1000000 | tf_op jit(solution)/shard_map/pallas_call | solution.py:545
  130.5 2.4 %shard_map.113 = (f32[8,88,256]{2,1,0:T(8,128)S(1)}, f32[80,304]{1,0:T(8,128)S(1)}, f32[8,128]{1,0:T(8,128)S(1)}) custom-call(s32[1]{0:T(128)} %bitcast.1.core, f32[40,304]{1,0:T(8,128)S(1)} %add.102.mine, f32[40,304]{1,0:T(8,128)S(1)} %collective-permute-done.11.other, f32[80,304]{1,0:T(8,128)S(1)} %get-tuple-element.194.vector, ...), custom_call_target="tpu_custom_call" | custom-call | flops 199229440 | bytes 12451840 | tf_op jit(solution)/shard_map/pallas_call | solution.py:315
  132.9 15.2 %all_to_all.22.refs_0_.got = f32[8,88,256]{2,1,0:T(8,128)S(1)} all-to-all(f32[8,88,256]{2,1,0:T(8,128)S(1)} %get-tuple-element.160), channel_id=1, replica_groups=mesh['pts'=16,'coef'=8] {'coef'}, dimensions={0} | all-to-all | bytes 1441792 | tf_op jit(solution)/shard_map/all_to_all | solution.py:636
  152.9 3.9 %shard_map.116 = f32[40,128]{1,0:T(8,128)S(1)} custom-call(s32[1]{0:T(128)} %bitcast.me.refs_0_, s32[1]{0:T(128)} %constant.101.clone.1.refs_1_, f32[1,81920]{1,0:T(1,128)S(1)} %bitcast.32, f32[1,81920]{1,0:T(1,128)S(1)} %bitcast.27, f32[1,81920]{1,0:T(1,128)S(1)} %bitcast.21, bf16[640,256]{1,0:T(8,128)(2,1)S(1)} %get-tuple-element.176.z_high.refs_5_, ...), custom_call_target="tpu_custom_call" | custom-call | flops 3355443200 | bytes 1000000 | tf_op jit(solution)/shard_map/pallas_call | solution.py:545
  156.8 1.9 %collective-permute-start.16 = (f32[40,256]{1,0:T(8,128)S(1)}, f32[40,256]{1,0:T(8,128)S(1)}, u32[]{:S(2)}, u32[]{:S(2)}) collective-permute-start(f32[40,256]{1,0:T(8,128)S(1)} %add.104), channel_id=1, source_target_pairs={{0,48},{8,56},{16,32},{24,40},{32,16},{40,24},{48,0},{56,8},{64,11... | collective-permute-start | bytes 122888 | tf_op jit(solution)/shard_map/ppermute | solution.py:609
  158.7 2.9 %collective-permute-start.14 = (f32[40,256]{1,0:T(8,128)S(1)}, f32[40,256]{1,0:T(8,128)S(1)}, u32[]{:S(2)}, u32[]{:S(2)}) collective-permute-start(f32[40,256]{1,0:T(8,128)S(1)} %add.104), channel_id=1, source_target_pairs={{0,32},{8,40},{16,48},{24,56},{32,0},{40,8},{48,16},{56,24},{64,96... | collective-permute-start | bytes 122888 | tf_op jit(solution)/shard_map/ppermute | solution.py:609
  161.6 3.9 %shard_map.117 = f32[40,128]{1,0:T(8,128)S(1)} custom-call(s32[1]{0:T(128)} %bitcast.me.refs_0_, s32[1]{0:T(128)} %constant.101.clone.1.refs_1_, f32[1,81920]{1,0:T(1,128)S(1)} %bitcast.33, f32[1,81920]{1,0:T(1,128)S(1)} %bitcast.28, f32[1,81920]{1,0:T(1,128)S(1)} %bitcast.22, bf16[640,256]{1,0:T(8,128)(2,1)S(1)} %get-tuple-element.176.z_high.refs_5_, ...), custom_call_target="tpu_custom_call" | custom-call | flops 3355443200 | bytes 1000000 | tf_op jit(solution)/shard_map/pallas_call | solution.py:545
  165.6 13.8 %all_to_all.23.last = f32[8,168,128]{2,1,0:T(8,128)S(1)} all-to-all(f32[8,168,128]{2,1,0:T(8,128)S(1)} %broadcast_in_dim.59), channel_id=1, replica_groups=mesh['pts'=16,'coef'=8] {'coef'}, dimensions={0} | all-to-all | bytes 1376256 | tf_op jit(solution)/shard_map/all_to_all | solution.py:636
  (66 shorter events, 24.5 us)
Async XLA Ops:
  7.3 0.7 copy-start.3
  18.2 1.0 copy-start.1
  51.7 19.6 %copy-start.4 = (f32[301]{0:T(512)S(1)}, f32[301]{0:T(512)}, u32[]{:S(2)}) copy-start(f32[301]{0:T(512)} %param.15) | copy-start | bytes 3616
  55.1 1.3 collective-permute-start
  56.4 5.5 %collective-permute-start.3 = (f32[40,304]{1,0:T(8,128)S(1)}, f32[40,304]{1,0:T(8,128)S(1)}, u32[]{:S(2)}, u32[]{:S(2)}) collective-permute-start(f32[40,304]{1,0:T(8,128)S(1)} %add.93), channel_id=1, source_target_pairs={{0,48},{8,56},{16,32},{24,40},{32,16},{40,24},{48,0},{56,8},{64,11... | collective-permute-start | bytes 145928 | tf_op jit(solution)/shard_map/ppermute | solution.py:609
  59.3 4.4 %collective-permute-start.2 = (f32[40,304]{1,0:T(8,128)S(1)}, f32[40,304]{1,0:T(8,128)S(1)}, u32[]{:S(2)}, u32[]{:S(2)}) collective-permute-start(f32[40,304]{1,0:T(8,128)S(1)} %add.93), channel_id=1, source_target_pairs={{0,16},{8,24},{16,0},{24,8},{32,48},{40,56},{48,32},{56,40},{64,80... | collective-permute-start | bytes 145928 | tf_op jit(solution)/shard_map/ppermute | solution.py:609
  59.5 5.7 %collective-permute-start.1 = (f32[40,304]{1,0:T(8,128)S(1)}, f32[40,304]{1,0:T(8,128)S(1)}, u32[]{:S(2)}, u32[]{:S(2)}) collective-permute-start(f32[40,304]{1,0:T(8,128)S(1)} %add.93), channel_id=1, source_target_pairs={{0,32},{8,40},{16,48},{24,56},{32,0},{40,8},{48,16},{56,24},{64,96... | collective-permute-start | bytes 145928 | tf_op jit(solution)/shard_map/ppermute | solution.py:609
  65.3 5.8 %collective-permute-start.4 = (f32[40,304]{1,0:T(8,128)S(1)}, f32[40,304]{1,0:T(8,128)S(1)}, u32[]{:S(2)}, u32[]{:S(2)}) collective-permute-start(f32[40,304]{1,0:T(8,128)S(1)} %add_add_fusion.1), channel_id=1, source_target_pairs={{0,64},{8,72},{16,80},{24,88},{32,96},{40,104},{48,112},{56,120},{... | collective-permute-start | bytes 145928 | tf_op jit(solution)/shard_map/ppermute | solution.py:609
  71.1 1.3 collective-permute-start.5
  72.4 24.6 %copy-start.2 = (bf16[1280,640]{1,0:T(8,128)(2,1)S(1)}, bf16[1280,640]{1,0:T(8,128)(2,1)}, u32[]{:S(2)}) copy-start(bf16[1280,640]{1,0:T(8,128)(2,1)} %constant.103.clone.wave) | copy-start | bytes 4915204
  112.1 1.3 collective-permute-start.6
  113.4 8.6 %collective-permute-start.9 = (f32[40,304]{1,0:T(8,128)S(1)}, f32[40,304]{1,0:T(8,128)S(1)}, u32[]{:S(2)}, u32[]{:S(2)}) collective-permute-start(f32[40,304]{1,0:T(8,128)S(1)} %add.98), channel_id=1, source_target_pairs={{0,48},{8,56},{16,32},{24,40},{32,16},{40,24},{48,0},{56,8},{64,11... | collective-permute-start | bytes 145928 | tf_op jit(solution)/shard_map/ppermute | solution.py:609
  115.3 6.7 %collective-permute-start.8 = (f32[40,304]{1,0:T(8,128)S(1)}, f32[40,304]{1,0:T(8,128)S(1)}, u32[]{:S(2)}, u32[]{:S(2)}) collective-permute-start(f32[40,304]{1,0:T(8,128)S(1)} %add.98), channel_id=1, source_target_pairs={{0,16},{8,24},{16,0},{24,8},{32,48},{40,56},{48,32},{56,40},{64,80... | collective-permute-start | bytes 145928 | tf_op jit(solution)/shard_map/ppermute | solution.py:609
  115.4 6.7 %collective-permute-start.7 = (f32[40,304]{1,0:T(8,128)S(1)}, f32[40,304]{1,0:T(8,128)S(1)}, u32[]{:S(2)}, u32[]{:S(2)}) collective-permute-start(f32[40,304]{1,0:T(8,128)S(1)} %add.98), channel_id=1, source_target_pairs={{0,32},{8,40},{16,48},{24,56},{32,0},{40,8},{48,16},{56,24},{64,96... | collective-permute-start | bytes 145928 | tf_op jit(solution)/shard_map/ppermute | solution.py:609
  122.1 7.1 %collective-permute-start.10 = (f32[40,304]{1,0:T(8,128)S(1)}, f32[40,304]{1,0:T(8,128)S(1)}, u32[]{:S(2)}, u32[]{:S(2)}) collective-permute-start(f32[40,304]{1,0:T(8,128)S(1)} %add_add_fusion), channel_id=1, source_target_pairs={{0,64},{8,72},{16,80},{24,88},{32,96},{40,104},{48,112},{56,120},{... | collective-permute-start | bytes 145928 | tf_op jit(solution)/shard_map/ppermute | solution.py:609
  129.1 1.3 collective-permute-start.11
  149.7 1.3 collective-permute-start.12
  151.0 5.7 %collective-permute-start.13 = (f32[40,256]{1,0:T(8,128)S(1)}, f32[40,256]{1,0:T(8,128)S(1)}, u32[]{:S(2)}, u32[]{:S(2)}) collective-permute-start(f32[40,256]{1,0:T(8,128)S(1)} %add.103), channel_id=1, source_target_pairs={{0,64},{8,72},{16,80},{24,88},{32,96},{40,104},{48,112},{56,120},{... | collective-permute-start | bytes 122888 | tf_op jit(solution)/shard_map/ppermute | solution.py:609
  156.8 22.6 %copy-start = (f32[81920]{0:T(1024)S(1)}, f32[81920]{0:T(1024)}, u32[]{:S(2)}) copy-start(f32[81920]{0:T(1024)} %param.13) | copy-start | bytes 983044
  156.8 8.7 %collective-permute-start.16 = (f32[40,256]{1,0:T(8,128)S(1)}, f32[40,256]{1,0:T(8,128)S(1)}, u32[]{:S(2)}, u32[]{:S(2)}) collective-permute-start(f32[40,256]{1,0:T(8,128)S(1)} %add.104), channel_id=1, source_target_pairs={{0,48},{8,56},{16,32},{24,40},{32,16},{40,24},{48,0},{56,8},{64,11... | collective-permute-start | bytes 122888 | tf_op jit(solution)/shard_map/ppermute | solution.py:609
  158.7 6.8 %collective-permute-start.15 = (f32[40,256]{1,0:T(8,128)S(1)}, f32[40,256]{1,0:T(8,128)S(1)}, u32[]{:S(2)}, u32[]{:S(2)}) collective-permute-start(f32[40,256]{1,0:T(8,128)S(1)} %add.104), channel_id=1, source_target_pairs={{0,16},{8,24},{16,0},{24,8},{32,48},{40,56},{48,32},{56,40},{64,80... | collective-permute-start | bytes 122888 | tf_op jit(solution)/shard_map/ppermute | solution.py:609
  158.7 6.8 %collective-permute-start.14 = (f32[40,256]{1,0:T(8,128)S(1)}, f32[40,256]{1,0:T(8,128)S(1)}, u32[]{:S(2)}, u32[]{:S(2)}) collective-permute-start(f32[40,256]{1,0:T(8,128)S(1)} %add.104), channel_id=1, source_target_pairs={{0,32},{8,40},{16,48},{24,56},{32,0},{40,8},{48,16},{56,24},{64,96... | collective-permute-start | bytes 122888 | tf_op jit(solution)/shard_map/ppermute | solution.py:609
